TPU v7x, 32 devices: a whole 2x2x4 slice. The times are simulated.
32 devices in a mesh: dp: 4 (over y, core), fsdp: 8 (over z, x).
Axes of the slice: x: 2, y: 2, z: 4, core: 2. Of those that a mesh axis runs over, the one named last changes fastest.
Arguments:
- frames: bfloat16 [32, 160, 512], P(('dp', 'fsdp')), may hold values from -6 to 6
- lengths: int32 [32], P(('dp', 'fsdp')), may hold values from 10 to 160, as said below
- cotangent: bfloat16 [32, 160, 512], P(('dp', 'fsdp')), may hold values from -6 to 6
- params: float32 [8210944], P(('dp', 'fsdp')), as said below
- first_moment: float32 [8210944], P(('dp', 'fsdp'))
- second_moment: float32 [8210944], P(('dp', 'fsdp')), as said below
Outputs:
- out: bfloat16 [32, 160, 512], P(('dp', 'fsdp'))
- frames_grad: bfloat16 [32, 160, 512], P(('dp', 'fsdp'))
- new_params: float32 [8210944], P(('dp', 'fsdp'))
- new_first: float32 [8210944], P(('dp', 'fsdp'))
- new_second: float32 [8210944], P(('dp', 'fsdp'))
- weight_norms: float32 [12], replicated
- update_norms: float32 [12], replicated
- trust_ratios: float32 [12], replicated
- gain_grads: float32 [4096], replicated
Inputs may be any that keep to these rules, and one draw needn't show every extreme that they name: `lengths`: in every draw some utterance has exactly 160 valid frames. `params`: the gains are positive. `second_moment`: every entry is positive.
All inputs are finite; a program needn't handle non-finite values.
Results may differ from a plain program's by a relative error of at most 0.02.
Values may be sent and summed in bfloat16 or wider, within the bound.
No kernel may reach another device: no remote copies, remote signals or barrier semaphores. Data moves between devices by JAX's collectives and lax.ppermute only.
A program may use at most 256 MiB of HBM per device.

v0:
```python
import math
from types import SimpleNamespace

import jax
import jax.numpy as jnp
from jax import lax
from jax.experimental import pallas as pl
from jax.experimental.pallas import tpu as pltpu
from jax.sharding import PartitionSpec as P

STEP = 8
BETA_FIRST = 0.5
BETA_SECOND = 0.5
LEARN_RATE = 0.5
WEIGHT_DECAY = 0.01
ADAM_EPS = 1e-06
AXES = ("dp", "fsdp")


def segment_shapes():
    gate_width = CG // 2
    return [
        (D, FF),
        (FF, D),
        (D, 3 * D),
        (D, D),
        (D, CG),
        (gate_width, D),
        (2 * D, D),
        (D, FF),
        (FF, D),
        (5 * D + gate_width,),
        (KER, gate_width + 2 * D),
        (RELW, H),
    ]


D = 512
H = 8
HS = 64
FF = 2048
CG = 3072
KER = 31
RELW = 128
NORM_EPS = 1e-05
MASK_FILL = -1000000000.0
ROW = 512
HALF = ROW // 2
SLOTS = 160
KEYS = 256
PAD = 16
PADDED = SLOTS + 2 * PAD
GATE = CG // 2
BLOCK = {
    "ffa_in": (0, 4),
    "ffa_out": (4, 4),
    "qkv": (8, 3),
    "att_out": (11, 1),
    "cg_in": (12, 6),
    "cg_out": (18, 3),
    "merge": (21, 2),
    "ffb_in": (23, 4),
    "ffb_out": (27, 4),
    "small": (31, 1),
}
TAPS_AT = 8
REL_AT = 8 + 5 * KER
SMALL = 176
F32, BF16 = jnp.float32, jnp.bfloat16


def dot(left, right):
    return lax.dot_general(left, right, (((1,), (0,)), ((), ())), preferred_element_type=F32)


def dot_t(left, right):
    return lax.dot_general(left, right, (((1,), (1,)), ((), ())), preferred_element_type=F32)


def t_dot(left, right):
    return lax.dot_general(left, right, (((0,), (0,)), ((), ())), preferred_element_type=F32)


def low(values):
    return values.astype(BF16)


def each(count, body):
    for at in range(count):
        body(at)


def each_loop(count, body, together=1):
    def step(at, carry):
        for inner in range(together):
            body(at * together + inner)
        return carry

    lax.fori_loop(0, count // together, step, 0)


def part(at, size):
    if isinstance(at, int):
        return slice(at * size, at * size + size)
    return pl.ds(pl.multiple_of(at * size, size), size)


def rows_of(name):
    first, count = BLOCK[name]
    return slice(ROW * first, ROW * (first + count))


def lane_mean(values, width):
    return jnp.sum(values, axis=-1, keepdims=True) * (1.0 / width)


def normed(values):
    centered = values - lane_mean(values, values.shape[-1])
    scale = lax.rsqrt(lane_mean(centered * centered, values.shape[-1]) + NORM_EPS)
    return centered * scale, scale


def valid_rows(length):
    return (lax.broadcasted_iota(jnp.int32, (SLOTS, 1), 0) < length).astype(F32)


def fold_rows(values):
    return jnp.sum(values, axis=0, keepdims=True)


def norm_rows(source, gain, target):
    for k in range(2):
        hat, _ = normed(source[part(k, 80), :].astype(F32))
        target[part(k, 80), :] = low(hat * gain)


def norm_rows_back(values, gain, grad, add):
    total = jnp.zeros((1, values.shape[1]), F32)
    for k in range(2):
        rows = part(k, 80)
        hat, scale = normed(values[rows, :].astype(F32))
        mine = grad[rows, :]
        total = total + fold_rows(mine * hat)
        inner = mine * gain
        width = values.shape[1]
        moved = lane_mean(inner, width) + hat * lane_mean(inner * hat, width)
        add(rows, scale * (inner - moved))
    return total


TOTAL_ROWS = 16037
PARTS = 32
TILE = 16
SPAN = 528
STARTS = [TILE * (TOTAL_ROWS * d // (PARTS * TILE)) for d in range(PARTS + 1)]
FIRST_PARTS = max(d for d in range(PARTS) if STARTS[d] < ROW * sum(BLOCK["ffa_out"]))
SHORTEST = min(high - first for first, high in zip(STARTS, STARTS[1:]))


def start_of(d):
    return ((TOTAL_ROWS * d) >> 9) * TILE


def gathered_layout():
    layout = []
    for core in range(2):
        layout += [[(core, 0, 0, back, 0, SPAN, 0)] for back in range(4)]
        for y, x, first, last in ((0, 1, 0, HALF), (1, 0, HALF, SPAN)):
            whole = [(core, y, x, back, 0, SPAN, 0) for back in range(4)]
            diagonal = [(core, 1, 1, back, first, last) for back in range(4)]
            layout += [[whole[0]], [whole[1]]]
            layout += [[whole[2], (*diagonal[0], SPAN)], [whole[3], (*diagonal[1], SPAN)]]
            layout += [[(*diagonal[2], 0)], [(*diagonal[3], 0)]]
    return layout


LAYOUT = gathered_layout()


def source_part(coords, piece):
    y, c, z, x = coords[0], coords[1], coords[2], coords[3]
    yy, cc, xx, zz = y ^ piece[1], c ^ piece[0], x ^ piece[2], (z + 4 - piece[3]) & 3
    return ((yy * 2 + cc) * 4 + zz) * 2 + xx


class Loads:
    def __init__(self, coords, sources, target, seams, sems):
        self.target, self.seams, self.sems = target, seams, sems
        self.here, self.joined = set(), set()
        seams[0, 0] = jnp.zeros((TILE, ROW), BF16)
        seams[PARTS, 1] = jnp.zeros((TILE, ROW), BF16)

        for soon in (True, False):
            for pieces, source in zip(LAYOUT, sources):
                for piece in pieces:
                    d = source_part(coords, piece)
                    first_ones = (d <= FIRST_PARTS) | (d == PARTS - 1)

                    @pl.when(first_ones if soon else jnp.logical_not(first_ones))
                    def _(piece=piece, source=source, d=d):
                        self.start(piece, source, d)

    def start(self, piece, source, d):
        def rows(at, size):
            return pl.ds(pl.multiple_of(at, TILE), size)

        first, last, offset = piece[4:]
        offset = offset - first
        start = start_of(d)
        length = start_of(d + 1) - start
        inner, outer = max(first, TILE), min(last, SHORTEST)
        sem = self.sems.at[d]
        pltpu.make_async_copy(
            source.at[offset + inner : offset + outer], self.target.at[rows(start + inner, outer - inner)], sem
        ).start()
        if first == 0:
            pltpu.make_async_copy(source.at[offset : offset + TILE], self.seams.at[d, 1], sem).start()
        if last == SPAN:

            @pl.when(length > SHORTEST)
            def _():
                pltpu.make_async_copy(
                    source.at[offset + SHORTEST : offset + SHORTEST + TILE],
                    self.target.at[rows(start + SHORTEST, TILE)],
                    sem,
                ).start()

            pltpu.make_async_copy(source.at[rows(offset + length, TILE)], self.seams.at[d + 1, 0], sem).start()

    def wait_part(self, d):
        if d in self.here or not 0 <= d < PARTS:
            return
        self.here.add(d)
        size = STARTS[d + 1] - STARTS[d] + TILE
        pltpu.make_async_copy(self.target.at[0:size], self.target.at[0:size], self.sems.at[d]).wait()

    def wait(self, name):
        rows = rows_of(name)
        last = min(rows.stop, STARTS[-1] + TILE)
        for d in range(PARTS + 1):
            if STARTS[d] < last and STARTS[d] + TILE > rows.start and d not in self.joined:
                self.wait_part(d - 1)
                self.wait_part(d)
                self.joined.add(d)
                self.target[STARTS[d] : STARTS[d] + TILE, :] = self.seams[d, 0] + self.seams[d, 1]
            if d < PARTS and STARTS[d] + TILE < last and STARTS[d + 1] > rows.start:
                self.wait_part(d)


class Emits:
    def __init__(self, coords, halves, sems):
        self.coords, self.halves, self.sems = coords, halves, sems
        self.pending = []

    def put(self, d, values, rows):
        core, z, x = (d // 8) % 2, (d // 2) % 4, d % 2
        kept, sent = self.halves[d // 16]
        far_x = self.coords[3] ^ x
        place = (self.coords[2] + 3 - z) & 3
        sem = self.sems.at[len(self.pending)]

        @pl.when(self.coords[1] == core)
        def _():
            pltpu.make_async_copy(values, kept.at[4 * far_x + place, rows], sem).start()

        @pl.when((self.coords[1] != core) & (far_x == 0))
        def _():
            pltpu.make_async_copy(values, sent[0].at[place, rows], sem).start()

        @pl.when((self.coords[1] != core) & (far_x == 1))
        def _():
            pltpu.make_async_copy(values, sent[1].at[place, rows], sem).start()

        self.pending.append(pltpu.make_async_copy(values, kept.at[0, rows], sem))

    def put_tensor(self, name, values):
        rows = rows_of(name)
        for d in range(PARTS):
            first, last = max(rows.start, STARTS[d]), min(rows.stop, STARTS[d] + SPAN)
            if first < last:
                self.put(d, values.at[first - rows.start : last - rows.start], slice(first - STARTS[d], last - STARTS[d]))

    def wait(self):
        for copy in self.pending:
            copy.wait()


def split_columns(raw, target, wide, stage):
    def chunk(k):
        rows = part(k, 128 * wide)
        for lane in range(4):
            stage[lane, 0 : 128 * wide, :] = raw[rows, lane * 128 : lane * 128 + 128].astype(F32)
        for c in range(wide):
            for lane in range(4):
                place = ROW * c + lane * 128
                target[part(k, 128), place : place + 128] = low(stage[lane, pl.ds(c, 128, stride=wide), :])

    each_loop(4, chunk)


def weight_columns(left, grads, wide, stage, left_t, target):
    left_t[...] = left[...].T

    def chunk(j):
        value = dot(left_t[...], grads[:, part(j, 256)])
        c, pair = j // 2, (j % 2) * 2
        for half in range(2):
            stage[pair + half, pl.ds(c, ROW, stride=wide), :] = value[:, 128 * half : 128 * half + 128]

    each(2 * wide, chunk)

    def lower(k):
        rows = part(k, ROW)
        for lane in range(4):
            target[rows, lane * 128 : lane * 128 + 128] = low(stage[lane, rows, :])

    each_loop(wide, lower)


def weight_rows(left, grads, count, left_t, target):
    def chunk(k):
        left_t[...] = left[:, part(k, ROW)].T
        for at in range(2):
            target[part(k, ROW), 256 * at : 256 * at + 256] = low(dot(left_t[...], grads[:, 256 * at : 256 * at + 256]))

    each(count, chunk)


def feed_forward(inputs, gain, w_in, w_out, nrm, act, slope, result):
    norm_rows(inputs, gain, nrm)

    def up(j):
        at = part(j, 256)
        hidden = dot(nrm[...], w_in[:, at])
        sig = jax.nn.sigmoid(hidden)
        active = hidden * sig
        act[:, at] = low(active)
        slope[:, at] = low(sig + active * (1.0 - sig))

    each(FF // 256, up)

    def down(j):
        at = part(j, 256)
        result[:, at] = inputs[:, at].astype(F32) + 0.5 * dot(act[...], w_out[:, at])

    each(2, down)


def feed_back(dout, w_in, w_out, nrm, act, slope, dhid, dnrm, stage, left_t, g_in, g_out, emits, name):
    def up(j):
        at = part(j, 256)
        grad = dot_t(dout[...], w_out[at, :])
        dhid[:, at] = low(grad * slope[:, at].astype(F32))

    each(FF // 256, up)
    weight_rows(act, dout, 4, left_t, g_out)
    emits.put_tensor(name + "_out", g_out)

    def down(j):
        at = part(j, 256)
        dnrm[:, at] = dot_t(dhid[:, 0:FF], w_in[at, :])

    each(2, down)
    weight_columns(nrm, dhid, 4, stage, left_t, g_in)
    emits.put_tensor(name + "_in", g_in)


def bucket_map():
    entry = lax.broadcasted_iota(jnp.int32, (2 * ROW, ROW), 0) // H
    far = lax.broadcasted_iota(jnp.int32, (2 * ROW, ROW), 1)
    far = jnp.where(far >= ROW // 2, far - ROW, far)
    bucket = jnp.clip(far, -(RELW // 2), RELW // 2 - 1) + RELW // 2
    return (entry == bucket).astype(F32)


def own_entries(flat):
    entry = lax.broadcasted_iota(jnp.int32, (H, 2 * ROW), 1)
    head = lax.broadcasted_iota(jnp.int32, (H, 2 * ROW), 0)
    return jnp.where(lax.rem(entry, H) == head, flat, 0.0)


def tap_row(small, tap, row, lane):
    return small[lane, pl.ds(TAPS_AT + 5 * tap + row, 1), :]


def shifted_sum(padded, at, factor):
    total = None
    for low_part in range(8):
        slab = padded[low_part : low_part + SLOTS + 24, at]
        inner = None
        for high_part in range(4):
            offset = 8 * high_part + low_part
            if offset:
                term = factor(offset) * slab[8 * high_part : 8 * high_part + SLOTS]
                inner = term if inner is None else inner + term
        total = inner if total is None else total + inner
    return total


def convolve(padded, small, first_row, width, finish):

    def chunk(j):
        at = part(j, 128)
        row, lane = first_row + j // 4, j % 4
        finish(j, at, shifted_sum(padded, at, lambda offset: tap_row(small, offset - 1, row, lane)))

    each_loop(width // 128, chunk)


def convolve_back(grads, padded, small, first_row, width, sgrad, finish):

    def chunk(j):
        at = part(j, 128)
        row, lane = first_row + j // 4, j % 4
        finish(j, at, shifted_sum(grads, at, lambda offset: tap_row(small, KER - offset, row, lane)))
        own = grads[PAD : PAD + SLOTS, at]
        for low_part in range(8):
            slab = padded[low_part : low_part + SLOTS + 24, at]
            for high_part in range(4):
                offset = 8 * high_part + low_part
                if offset:
                    tile = slab[8 * high_part : 8 * high_part + SLOTS]
                    sgrad[lane, pl.ds(TAPS_AT + 5 * (offset - 1) + row, 1), :] = fold_rows(own * tile)

    each_loop(width // 128, chunk)


def clear_margins(padded):
    padded[0:PAD, :] = jnp.zeros((PAD, padded.shape[1]), F32)
    padded[PAD + SLOTS : PADDED, :] = jnp.zeros((PAD, padded.shape[1]), F32)


def gelu_parts(hidden):
    bell = jnp.exp(-0.5 * hidden * hidden)
    spread = 1.0 + (0.3275911 * 2.0**-0.5) * jnp.abs(hidden)
    near = pl.reciprocal(spread, approx=True)
    near = near * (2.0 - spread * near)
    tail = jnp.full_like(near, 0.5 * 1.061405429)
    for factor in (-1.453152027, 1.421413741, -0.284496736, 0.254829592):
        tail = tail * near + 0.5 * factor
    tail = tail * near * bell
    below = jnp.where(hidden >= 0.0, 1.0 - tail, tail)
    return hidden * below, below + hidden * bell * ((2.0 * math.pi) ** -0.5)


def attention_forward(r, length):
    norm_rows(r.x1, r.small[1:2, :], r.nrm_t)
    r.qkv[SLOTS:KEYS, :] = jnp.zeros((KEYS - SLOTS, 3 * D), BF16)
    flat = jnp.concatenate([r.small[REL_AT : REL_AT + 1, :], r.small[REL_AT + 1 : REL_AT + 2, :]], axis=1)
    r.bias[...] = dot(low(own_entries(jnp.broadcast_to(flat, (H, 2 * ROW)))), low(bucket_map()))

    def project(j):
        at = part(j, 256)
        r.qkv[0:SLOTS, at] = low(dot(r.nrm_t[...], r.w_qkv[:, at]))

    each(3 * D // 256, project)
    valid = lax.broadcasted_iota(jnp.int32, (1, KEYS), 1) < length
    first_half = lax.broadcasted_iota(jnp.int32, (1, 128), 1) < HS

    def heads(pair):
        queries = r.qkv[0:SLOTS, part(pair, 128)]
        keys = r.qkv[:, part(pair + 4, 128)]
        values = r.qkv[:, part(pair + 8, 128)]
        outs = []
        for odd in range(2):
            head = 2 * pair + odd
            half = first_half if odd == 0 else jnp.logical_not(first_half)
            mine = jnp.where(half, queries, jnp.zeros_like(queries))
            spread = jnp.broadcast_to(r.bias[pl.ds(head, 1), :], (SLOTS, ROW))
            spread = pltpu.roll(spread, 0, 1, stride=1, stride_axis=0)[:, 0:KEYS]
            scores = jnp.where(valid, dot_t(mine, keys) * HS ** (-0.5) + spread, MASK_FILL)
            shifted = jnp.exp(scores - jnp.max(scores, axis=-1, keepdims=True))
            chances = low(shifted / jnp.sum(shifted, axis=-1, keepdims=True))
            r.probs[head] = chances
            outs.append(dot(chances, values))
        r.ctx[:, part(pair, 128)] = low(jnp.where(first_half, outs[0], outs[1]))

    each(H // 2, heads)

    def project_out(j):
        at = part(j, 256)
        r.cat[:, at] = dot(r.ctx[...], r.w[rows_of("att_out"), at])

    each(2, project_out)


def gating_forward(r, length):
    norm_rows(r.x1, r.small[2:3, :], r.nrm_c)

    def up(j):
        at = part(j, 256)
        r.hid[...] = dot(r.nrm_c[...], r.w_cg[:, at])
        for k in range(5):
            rows = part(k, 32)
            active, slope = gelu_parts(r.hid[rows, :])
            r.ug[rows, at] = active
            r.slope_c[rows, at] = low(slope)

    each_loop(CG // 256, up, 2)
    tiles = [slice(GATE + 128 * j, GATE + 128 * j + 128) for j in range(GATE // 128)]
    total = jnp.zeros((SLOTS, 128), F32)
    for at in tiles:
        total = total + r.ug[:, at]
    mean = lane_mean(total, GATE)
    total = jnp.zeros((SLOTS, 128), F32)
    for at in tiles:
        centered = r.ug[:, at] - mean
        total = total + centered * centered
    scale = lax.rsqrt(lane_mean(total, GATE) + NORM_EPS)
    r.gmean[...] = jnp.broadcast_to(mean, (SLOTS, 128))
    r.gscale[...] = jnp.broadcast_to(scale, (SLOTS, 128))
    scale = scale * valid_rows(length)
    for j, at in enumerate(tiles):
        gain = r.small[5 + j // 4 : 6 + j // 4, part(j % 4, 128)]
        r.gpad[PAD : PAD + SLOTS, part(j, 128)] = (r.ug[:, at] - mean) * scale * gain

    def finish(j, at, value):
        r.cv[:, at] = low(value)
        r.gated[:, at] = low(r.ug[:, at] * value)

    convolve(r.gpad, r.tiles, 0, GATE, finish)

    def down(j):
        r.cat[:, part(j + 2, 256)] = dot(r.gated[...], r.w[rows_of("cg_out"), part(j, 256)])

    each(2, down)


def merge_forward(r, length):
    valid = valid_rows(length)
    for j in range(8):
        at = part(j, 128)
        r.mpad[PAD : PAD + SLOTS, at] = r.cat[:, at] * valid

    def finish(j, at, value):
        r.mixed[:, at] = low(r.cat[:, at] + value)

    convolve(r.mpad, r.tiles, 3, 2 * D, finish)

    def merge(j):
        at = part(j, 256)
        r.x2[:, at] = r.x1[:, at] + dot(r.mixed[...], r.w[rows_of("merge"), at])

    each(2, merge)


def final_norm(r, length):
    gain = r.small[4:5, :]
    valid = valid_rows(length)
    total = jnp.zeros((1, D), F32)
    for k in range(2):
        rows = part(k, 80)
        hat, scale = normed(r.x3[rows, :])
        r.out[rows, :] = low(hat * gain * valid[80 * k : 80 * k + 80])
        mine = r.cot[rows, :].astype(F32) * valid[80 * k : 80 * k + 80]
        total = total + fold_rows(mine * hat)
        inner = mine * gain
        back = scale * (inner - (lane_mean(inner, D) + hat * lane_mean(inner * hat, D)))
        r.dx[rows, :] = back
        r.dout[rows, :] = low(0.5 * back)
    r.gains[4:5, :] = total


def merge_back(r, length, emits):
    for k in range(2):
        r.dout[part(k, 80), :] = low(r.dx[part(k, 80), :])
    w_merge = r.w.at[rows_of("merge")]

    def merge(j):
        at = part(j, 256)
        r.dpad[PAD : PAD + SLOTS, at] = dot_t(r.dout[...], w_merge[at, :])

    each(2 * D // 256, merge)
    weight_rows(r.mixed, r.dout, 2, r.left_t, w_merge)
    emits.put_tensor("merge", w_merge)

    def finish(j, at, value):
        r.djoin[:, at] = low(r.dpad[PAD : PAD + SLOTS, at] + value * valid_rows(length))

    convolve_back(r.dpad, r.mpad, r.tiles, 3, 2 * D, r.tgrad, finish)


def gating_back(r, length, emits):
    w_co = r.w.at[rows_of("cg_out")]

    def gate(j):
        at = part(j, 256)
        value = dot_t(r.djoin[:, D:], w_co[at, :])
        r.dhid[:, at] = low(value * r.cv[:, at].astype(F32) * r.slope_c[:, at].astype(F32))
        r.dpad[PAD : PAD + SLOTS, at] = value * r.ug[:, at]

    each(GATE // 256, gate)
    r.dout[...] = r.djoin[:, D:]
    weight_rows(r.gated, r.dout, 3, r.left_t, w_co)
    emits.put_tensor("cg_out", w_co)

    def finish(j, at, value):
        r.dgate[:, at] = value * valid_rows(length)

    convolve_back(r.dpad, r.gpad, r.tiles, 0, GATE, r.tgrad, finish)
    tiles = GATE // 128
    for quarter in range(4):
        rows = part(quarter, SLOTS // 4)
        mean, scale = r.gmean[rows, :], r.gscale[rows, :]
        total, total_hat = jnp.zeros_like(mean), jnp.zeros_like(mean)

        def parts(j, rows=rows, mean=mean, scale=scale):
            row, lane = 5 + j // 4, part(j % 4, 128)
            hat = (r.ug[rows, part(j + tiles, 128)] - mean) * scale
            grad = r.dgate[rows, part(j, 128)]
            return hat, grad, grad * r.small[row : row + 1, lane]

        for j in range(tiles):
            hat, grad, inner = parts(j)
            products = jnp.sum((grad * hat).reshape(-1, 8, 128), axis=0)
            r.gate_sums[part(j, 8), :] = products if quarter == 0 else r.gate_sums[part(j, 8), :] + products
            total = total + inner
            total_hat = total_hat + inner * hat
        total = jnp.broadcast_to(lane_mean(total, GATE), total.shape)
        total_hat = jnp.broadcast_to(lane_mean(total_hat, GATE), total.shape)
        for j in range(tiles):
            hat, _, inner = parts(j)
            far = part(j + tiles, 128)
            r.dgate[rows, part(j, 128)] = scale * (inner - total - hat * total_hat)
    for j in range(tiles):
        far = part(j + tiles, 128)
        r.dhid[:, far] = low(r.dgate[:, part(j, 128)] * r.slope_c[:, far].astype(F32))
        r.tgrad[j % 4, 5 + j // 4 : 6 + j // 4, :] = fold_rows(r.gate_sums[part(j, 8), :])

    def down(j):
        at = part(j, 256)
        r.dnrm[:, at] = dot_t(r.dhid[...], r.w_cg[at, :])

    each(2, down)
    g_cg = r.w.at[rows_of("cg_in")]
    weight_columns(r.nrm_c, r.dhid, 6, r.stage, r.left_t, g_cg)
    emits.put_tensor("cg_in", g_cg)

    def add(rows, back):
        r.dx[rows, :] += back

    r.gains[2:3, :] = norm_rows_back(r.x1, r.small[2:3, :], r.dnrm, add)


def forward_kernel(names, coords, length_ref, frames, cot, *refs):
    sources, refs = refs[: len(LAYOUT)], refs[len(LAYOUT) :]
    r = SimpleNamespace(**dict(zip(names, refs)))
    r.cot = cot
    length = length_ref[0]
    loads = Loads(coords, sources, r.w, r.seams, r.load_sems)
    kept = []

    def keep(source, target):
        copy = pltpu.make_async_copy(source, target, r.keep_sems.at[len(kept)])
        copy.start()
        kept.append(copy)

    for padded in (r.gpad, r.mpad, r.dpad):
        clear_margins(padded)
    r.tgrad[...] = jnp.zeros_like(r.tgrad)
    r.gains[...] = jnp.zeros_like(r.gains)
    loads.wait("small")
    r.small[...] = r.w[ROW * 31 : ROW * 31 + SMALL, :].astype(F32)
    for lane in range(4):
        r.tiles[lane] = r.small[:, part(lane, 128)]
    loads.wait("ffa_in")
    split_columns(r.w.at[rows_of("ffa_in")], r.w_ffa_in, 4, r.stage)
    keep(r.w_ffa_in, r.keep_ffa_in)
    loads.wait("ffa_out")
    keep(r.w.at[rows_of("ffa_out")], r.keep_ffa_out)
    feed_forward(frames, r.small[0:1, :], r.w_ffa_in, r.w.at[rows_of("ffa_out")], r.nrm, r.act, r.slope, r.x1)
    keep(r.nrm, r.keep_nrm)
    keep(r.act, r.keep_act)
    keep(r.slope, r.keep_slope)
    keep(r.x1, r.keep_x1)
    loads.wait("qkv")
    split_columns(r.w.at[rows_of("qkv")], r.w_qkv, 3, r.stage)
    keep(r.w_qkv, r.keep_qkv)
    loads.wait("att_out")
    keep(r.w.at[rows_of("att_out")], r.keep_att)
    attention_forward(r, length)
    keep(r.nrm_t, r.keep_nrm_t)
    keep(r.qkv, r.keep_heads)
    keep(r.probs, r.keep_probs)
    keep(r.ctx, r.keep_ctx)
    loads.wait("cg_in")
    split_columns(r.w.at[rows_of("cg_in")], r.w_cg, 6, r.stage)
    loads.wait("cg_out")
    gating_forward(r, length)
    loads.wait("merge")
    merge_forward(r, length)
    loads.wait("ffb_in")
    split_columns(r.w.at[rows_of("ffb_in")], r.w_ffb_in, 4, r.stage)
    loads.wait("ffb_out")
    w_out = r.w.at[rows_of("ffb_out")]
    feed_forward(r.x2, r.small[3:4, :], r.w_ffb_in, w_out, r.nrm_b, r.act_b, r.slope_b, r.x3)
    final_norm(r, length)
    emits = Emits(
        coords,
        ((r.low_kept, (r.low_near, r.low_far)), (r.high_kept, (r.high_near, r.high_far))),
        r.emit_sems,
    )
    feed_back(
        r.dout, r.w_ffb_in, w_out, r.nrm_b, r.act_b, r.slope_b, r.dhid, r.dnrm, r.stage, r.left_t,
        r.w.at[rows_of("ffb_in")], w_out, emits, "ffb",
    )

    def add(rows, back):
        r.dx[rows, :] += back

    r.gains[3:4, :] = norm_rows_back(r.x2, r.small[3:4, :], r.dnrm, add)
    merge_back(r, length, emits)
    keep(r.djoin, r.keep_djoin)
    gating_back(r, length, emits)
    keep(r.dx, r.keep_dx)
    for lane in range(4):
        at = part(lane, 128)
        r.gains[5:8, at] = r.tgrad[lane, 5:8, :]
        r.w[ROW * 31 : ROW * 31 + SMALL, at] = low(r.tgrad[lane])
    r.w[ROW * 31 : ROW * 31 + 16, :] = low(
        jnp.concatenate(
            [
                jnp.zeros((8, ROW), F32),
                jnp.concatenate([r.tgrad[lane, 8:16, :] for lane in range(4)], axis=1),
            ],
            axis=0,
        )
    )
    r.w[ROW * 31 + SMALL : ROW * 32, :] = jnp.zeros((ROW - SMALL, ROW), BF16)
    emits.put_tensor("small", r.w.at[rows_of("small")])
    for copy in kept:
        copy.wait()
    emits.wait()


def attention_back(r, emits):
    def project(j):
        at = part(j, 256)
        r.dctx[:, at] = low(dot_t(r.datt[...], r.w_att[at, :]))

    each(2, project)
    weight_rows(r.ctx, r.datt, 1, r.left_t, r.w_att)
    emits.put_tensor("att_out", r.w_att)
    first_half = lax.broadcasted_iota(jnp.int32, (1, 128), 1) < HS
    at_row = lax.broadcasted_iota(jnp.int32, (SLOTS, SLOTS), 0)
    at_column = lax.broadcasted_iota(jnp.int32, (SLOTS, SLOTS), 1)
    flip = low((at_row + at_column == SLOTS - 1).astype(F32))

    def heads(pair):
        queries = r.qkv[0:SLOTS, part(pair, 128)]
        keys = r.qkv[:, part(pair + 4, 128)]
        values = r.qkv[:, part(pair + 8, 128)]
        context = r.dctx[:, part(pair, 128)]
        q_parts, k_parts, v_parts = [], [], []
        for odd in range(2):
            head = 2 * pair + odd
            half = first_half if odd == 0 else jnp.logical_not(first_half)
            chances = r.probs[head]
            v_parts.append(t_dot(chances, context)[0:SLOTS])
            wide_chances = chances.astype(F32)
            chance_grad = dot_t(jnp.where(half, context, jnp.zeros_like(context)), values)
            inner = jnp.sum(wide_chances * chance_grad, axis=-1, keepdims=True)
            score_grad = low(wide_chances * (chance_grad - inner))
            q_parts.append(dot(score_grad, keys))
            k_parts.append(t_dot(score_grad, queries)[0:SLOTS])
            wide = jnp.concatenate([dot(flip, score_grad), jnp.zeros((SLOTS, ROW - KEYS), F32)], axis=1)
            wide = pltpu.roll(wide, ROW - SLOTS + 1, 1, stride=1, stride_axis=0)
            r.sums[pl.ds(head, 1), :] = fold_rows(wide)
        scale = HS ** (-0.5)
        r.dhid[:, part(pair, 128)] = low(jnp.where(first_half, q_parts[0], q_parts[1]) * scale)
        r.dhid[:, part(pair + 4, 128)] = low(jnp.where(first_half, k_parts[0], k_parts[1]) * scale)
        r.dhid[:, part(pair + 8, 128)] = low(jnp.where(first_half, v_parts[0], v_parts[1]))

    each(H // 2, heads)

    def down(j):
        at = part(j, 256)
        r.dnrm[:, at] = dot_t(r.dhid[:, 0 : 3 * D], r.w_qkv[at, :])

    each(2, down)

    def add(rows, back):
        r.dx[rows, :] += back
        r.dout[rows, :] = low(0.5 * r.dx[rows, :])

    r.late[1:2, :] = norm_rows_back(r.x1, r.gain_rows[1:2, :], r.dnrm, add)


def attention_weights_back(r, emits):
    weight_columns(r.nrm_t, r.dhid, 3, r.stage, r.left_t, r.g_qkv)
    emits.put_tensor("qkv", r.g_qkv)
    by_entry = lax.dot_general(
        r.sums[...],
        bucket_map(),
        (((1,), (1,)), ((), ())),
        precision=lax.Precision.HIGHEST,
        preferred_element_type=F32,
    )
    flat = fold_rows(own_entries(by_entry))
    r.late[8:9, :] = flat[:, 0:ROW]
    r.late[9:10, :] = flat[:, ROW:]


def backward_kernel(names, coords, frames, gains, gain_rows, *refs):
    r = SimpleNamespace(**dict(zip(names, refs)))
    r.gain_rows = gain_rows
    waits = {}
    for at, (name, source, target) in enumerate(
        (
            ("att", r.in_att, r.w_att),
            ("djoin", r.in_djoin.at[:, 0:D], r.datt),
            ("ctx", r.in_ctx, r.ctx),
            ("heads", r.in_heads, r.qkv),
            ("probs", r.in_probs, r.probs),
            ("qkv", r.in_qkv, r.w_qkv),
            ("x1", r.in_x1, r.x1),
            ("dx", r.in_dx, r.dx),
            ("nrm_t", r.in_nrm_t, r.nrm_t),
            ("ffa_out", r.in_ffa_out, r.w_ffa_out),
            ("slope", r.in_slope, r.slope),
            ("act", r.in_act, r.act),
            ("ffa_in", r.in_ffa_in, r.w_ffa_in),
            ("nrm", r.in_nrm, r.nrm),
        )
    ):
        waits[name] = pltpu.make_async_copy(source, target, r.load_sems.at[at])
        waits[name].start()
    r.late[...] = jnp.zeros_like(r.late)
    emits = Emits(coords, ((r.low_kept, (r.low_near, r.low_far)),), r.emit_sems)
    for name in ("att", "djoin", "ctx", "heads", "probs", "qkv", "x1", "dx"):
        waits[name].wait()
    attention_back(r, emits)
    waits["nrm_t"].wait()
    attention_weights_back(r, emits)
    for name in ("ffa_out", "slope", "act", "ffa_in", "nrm"):
        waits[name].wait()
    feed_back(
        r.dout, r.w_ffa_in, r.w_ffa_out, r.nrm, r.act, r.slope, r.dhid, r.dnrm, r.stage, r.left_t, r.g_ffa_in,
        r.w_ffa_out, emits, "ffa",
    )

    def add(rows, back):
        r.fgrad[rows, :] = low(r.dx[rows, :] + back)

    r.late[0:1, :] = norm_rows_back(frames, gain_rows[0:1, :], r.dnrm, add)
    r.late[2:8, :] = gains[2:8, :]
    emits.wait()


VM = pl.BlockSpec(memory_space=pltpu.VMEM)
SM = pl.BlockSpec(memory_space=pltpu.SMEM)
ANY = pl.BlockSpec(memory_space=pl.ANY)
WIDE, THIN = ((SLOTS, D), F32), ((SLOTS, D), BF16)
FULL = ((SLOTS, FF), BF16)
KEPT, SENT = ((8, SPAN, ROW), BF16), ((4, SPAN, ROW), BF16)

FORWARD_OUT = {
    "out": (VM, THIN),
    "gains": (VM, ((8, ROW), F32)),
    "small": (VM, ((SMALL, ROW), F32)),
    "high_kept": (ANY, KEPT),
    "high_near": (ANY, SENT),
    "high_far": (ANY, SENT),
    "low_kept": (ANY, KEPT),
    "low_near": (ANY, SENT),
    "low_far": (ANY, SENT),
    "keep_ffa_in": (ANY, ((D, FF), BF16)),
    "keep_ffa_out": (ANY, ((FF, D), BF16)),
    "keep_qkv": (ANY, ((D, 3 * D), BF16)),
    "keep_att": (ANY, ((D, D), BF16)),
    "keep_nrm": (ANY, THIN),
    "keep_act": (ANY, FULL),
    "keep_slope": (ANY, FULL),
    "keep_x1": (ANY, WIDE),
    "keep_nrm_t": (ANY, THIN),
    "keep_heads": (ANY, ((KEYS, 3 * D), BF16)),
    "keep_probs": (ANY, ((H, SLOTS, KEYS), BF16)),
    "keep_ctx": (ANY, THIN),
    "keep_djoin": (ANY, ((SLOTS, 2 * D), BF16)),
    "keep_dx": (ANY, WIDE),
}
FORWARD_SCRATCH = {
    "w": ((32 * ROW, ROW), BF16),
    "w_ffa_in": ((D, FF), BF16),
    "w_qkv": ((D, 3 * D), BF16),
    "w_cg": ((D, CG), BF16),
    "w_ffb_in": ((D, FF), BF16),
    "stage": ((4, 6 * ROW, 128), F32),
    "left_t": ((ROW, SLOTS), BF16),
    "tiles": ((4, SMALL, 128), F32),
    "tgrad": ((4, SMALL, 128), F32),
    "bias": ((H, ROW), F32),
    "nrm": THIN,
    "act": FULL,
    "slope": FULL,
    "nrm_t": THIN,
    "qkv": ((KEYS, 3 * D), BF16),
    "probs": ((H, SLOTS, KEYS), BF16),
    "ctx": THIN,
    "nrm_c": THIN,
    "hid": ((SLOTS, 256), F32),
    "ug": ((SLOTS, CG), F32),
    "slope_c": ((SLOTS, CG), BF16),
    "gmean": ((SLOTS, 128), F32),
    "gscale": ((SLOTS, 128), F32),
    "gate_sums": ((8 * GATE // 128, 128), F32),
    "gpad": ((PADDED, GATE), F32),
    "cv": ((SLOTS, GATE), BF16),
    "gated": ((SLOTS, GATE), BF16),
    "cat": ((SLOTS, 2 * D), F32),
    "mpad": ((PADDED, 2 * D), F32),
    "mixed": ((SLOTS, 2 * D), BF16),
    "nrm_b": THIN,
    "act_b": FULL,
    "slope_b": FULL,
    "dpad": ((PADDED, GATE), F32),
    "djoin": ((SLOTS, 2 * D), BF16),
    "dgate": ((SLOTS, GATE), F32),
    "dhid": ((SLOTS, CG), BF16),
    "dnrm": WIDE,
    "dout": THIN,
    "dx": WIDE,
    "x1": WIDE,
    "x2": WIDE,
    "x3": WIDE,
    "seams": ((PARTS + 1, 2, TILE, ROW), BF16),
    "load_sems": PARTS,
    "keep_sems": 16,
    "emit_sems": 40,
}
BACKWARD_IN = (
    "ffa_in", "ffa_out", "qkv", "att", "nrm", "act", "slope", "x1", "nrm_t", "heads", "probs", "ctx", "djoin", "dx",
)
PASSED = ("low_kept", "low_near", "low_far")
BACKWARD_OUT = {
    "fgrad": (VM, THIN),
    "late": (VM, ((16, ROW), F32)),
    "low_kept": (ANY, KEPT),
    "low_near": (ANY, SENT),
    "low_far": (ANY, SENT),
}
BACKWARD_SCRATCH = {
    "w_ffa_in": ((D, FF), BF16),
    "w_ffa_out": ((FF, D), BF16),
    "w_qkv": ((D, 3 * D), BF16),
    "w_att": ((D, D), BF16),
    "g_ffa_in": ((FF, D), BF16),
    "g_qkv": ((3 * D, D), BF16),
    "stage": ((4, 4 * ROW, 128), F32),
    "left_t": ((ROW, SLOTS), BF16),
    "sums": ((H, ROW), F32),
    "nrm": THIN,
    "act": FULL,
    "slope": FULL,
    "nrm_t": THIN,
    "qkv": ((KEYS, 3 * D), BF16),
    "probs": ((H, SLOTS, KEYS), BF16),
    "ctx": THIN,
    "datt": THIN,
    "dctx": THIN,
    "dhid": FULL,
    "dnrm": WIDE,
    "dout": THIN,
    "dx": WIDE,
    "x1": WIDE,
    "load_sems": 14,
    "emit_sems": 24,
}


def call(kernel, name, ins, outs, scratch, limit, aliases=None):
    return pl.pallas_call(
        kernel,
        name=name,
        in_specs=[space for space, _ in ins],
        out_specs=[space for space, _ in outs],
        out_shape=[jax.ShapeDtypeStruct(*kind) for _, kind in outs],
        scratch_shapes=[
            pltpu.SemaphoreType.DMA((each_one,)) if isinstance(each_one, int) else pltpu.VMEM(*each_one)
            for each_one in scratch
        ],
        input_output_aliases=aliases or {},
        compiler_params=pltpu.CompilerParams(vmem_limit_bytes=limit * 2**20),
    )(*[array for _, array in ins])


def forward(coords, length, frames, cot, blocks):
    def kernel(*refs):
        forward_kernel([*FORWARD_OUT, *FORWARD_SCRATCH], *refs)

    outs = call(
        kernel,
        "forward",
        [(SM, coords), (SM, length), (VM, frames), (VM, cot)] + [(ANY, block) for block in blocks],
        list(FORWARD_OUT.values()),
        list(FORWARD_SCRATCH.values()),
        58,
    )
    return dict(zip(FORWARD_OUT, outs))


def backward(coords, frames, state):
    def kernel(*refs):
        names = ["in_" + name for name in BACKWARD_IN + PASSED]
        backward_kernel([*names, *BACKWARD_OUT, *BACKWARD_SCRATCH], *refs)

    ins = [(SM, coords), (VM, frames), (VM, state["gains"]), (VM, state["small"])]
    ins += [(ANY, state["keep_" + name]) for name in BACKWARD_IN]
    ins += [(ANY, state[name]) for name in PASSED]
    outs = call(
        kernel,
        "backward",
        ins,
        list(BACKWARD_OUT.values()),
        list(BACKWARD_SCRATCH.values()),
        58,
        {len(ins) - 3 + at: 2 + at for at in range(3)},
    )
    return dict(zip(BACKWARD_OUT, outs))


def segment_bounds():
    bounds = [0]
    for extent in segment_shapes():
        bounds.append(bounds[-1] + math.prod(extent))
    return bounds


def fast_mesh():
    return lax.axis_size("dp") == 4 and lax.axis_size("fsdp") == 8


def over_x(value):
    return lax.ppermute(value, "fsdp", [(i, i ^ 1) for i in range(8)])


def over_y(value):
    return lax.ppermute(value, "dp", [(i, i ^ 2) for i in range(4)])


def over_core(value):
    return lax.ppermute(value, "dp", [(i, i ^ 1) for i in range(4)])


def round_z(value):
    return lax.ppermute(value, "fsdp", [(i, (i + 2) % 8) for i in range(8)])


def over_z(value, step):
    return lax.ppermute(value, "fsdp", [(i, i ^ (2 * step)) for i in range(8)])


def after(value, *others):
    return lax.optimization_barrier((value, *others))[0]


def shard_offset(me, shard_size):
    return me * shard_size - start_of(me) * ROW


def gather_shards(shard, me):
    shard_size = shard.shape[0]
    if not fast_mesh():
        whole = lax.all_gather(shard, AXES, axis=0, tiled=True)
        whole = jnp.pad(whole, (0, (STARTS[-1] + SPAN) * ROW - whole.shape[0])).reshape(-1, ROW)
        spans = [whole[start : start + SPAN] for start in STARTS[:-1]]
        spans = spans[:1] + [jnp.concatenate([jnp.zeros((TILE, ROW), BF16), span[TILE:]]) for span in spans[1:]]
        return [
            jnp.concatenate([spans[source_part((0, 0, 0, 0), piece)][piece[4] : piece[5]] for piece in pieces])
            for pieces in LAYOUT
        ]
    most = TILE * ROW
    padded = jnp.pad(shard, (most, SPAN * ROW - shard_size))
    span = lax.dynamic_slice(padded, (most - shard_offset(me, shard_size),), (SPAN * ROW,)).reshape(SPAN, ROW)
    own, by_x, by_y = [span], [], []
    for back in range(4):
        if back < 3:
            own.append(round_z(own[back]))
        if back < 2:
            by_x.append(over_x(own[back]))
            by_y.append(over_y(own[back]))
            own[back + 1], by_x[back], by_y[back] = lax.optimization_barrier((own[back + 1], by_x[back], by_y[back]))
        else:
            by_x.append(over_x(jnp.concatenate([own[back], by_y[back - 2][:HALF]])))
            by_y.append(over_y(jnp.concatenate([own[back], by_x[back - 2][HALF:SPAN]])))
    by_x.append(over_x(by_y[2][:HALF]))
    by_y.append(over_y(by_x[2][HALF:SPAN]))
    last_x, last_y = by_y[3][:HALF], by_x[3][HALF:SPAN]
    by_x.append(over_x(after(last_x, by_x[4])))
    by_y.append(over_y(after(last_y, by_y[4])))
    late_ones = (by_x[3], by_y[3])
    far_own = [over_core(each_one) for each_one in own[:2]] + [over_core(after(each_one, *late_ones)) for each_one in own[2:]]
    far = [far_own]
    for way in (by_x, by_y):
        far.append([over_core(way[0])] + [over_core(after(way[at], *late_ones)) for at in (1, 2)])
        far[-1] += [over_core(way[at]) for at in (3, 4, 5)]
    return own + by_x + by_y + far[0] + far[1] + far[2]


def added(*parts):
    total = parts[0].astype(F32)
    for each_one in parts[1:]:
        total = total + each_one.astype(F32)
    return total


SIDES = (slice(0, HALF), slice(HALF, SPAN))


def span_sums(coords, own_half, x, places, low_kept, low_got, high_kept, high_got, sides=None):
    count = len(places)
    pieces = [(at, rows) for at in range(count) for rows in sides or ()]

    def kernel(coords, low_kept, low_got, high_kept, high_got, *refs):
        outs, (kept, got, total, sems, out_sems) = refs[:-5], refs[-5:]
        high = coords[0] == int(own_half)
        for source, other, wanted in ((low_kept, low_got, jnp.logical_not(high)), (high_kept, high_got, high)):

            @pl.when(wanted)
            def _(source=source, other=other):
                for at, place in enumerate(places):
                    pltpu.make_async_copy(source.at[4 * x + place], kept.at[at], sems.at[2 * at]).start()
                    pltpu.make_async_copy(other.at[place], got.at[at], sems.at[2 * at + 1]).start()

        copies = []
        for at in range(count):
            pltpu.make_async_copy(low_kept.at[at], kept.at[at], sems.at[2 * at]).wait()
            pltpu.make_async_copy(low_got.at[at], got.at[at], sems.at[2 * at + 1]).wait()

            def add(k, at=at):
                rows = part(k, SPAN // 11)
                total[at, rows] = low(kept[at, rows].astype(F32) + got[at, rows].astype(F32))

            each_loop(11, add)
            if sides is None:
                copies.append(pltpu.make_async_copy(total.at[at], outs[0].at[at], out_sems.at[at]))
                copies[-1].start()
            for which, (mine, rows) in enumerate(pieces):
                if mine == at:
                    copies.append(pltpu.make_async_copy(total.at[at, rows], outs[which], out_sems.at[which]))
                    copies[-1].start()
        for copy in copies:
            copy.wait()

    spans = ((count, SPAN, ROW), BF16)
    arrays = [(ANY, each_one) for each_one in (low_kept, low_got, high_kept, high_got)]
    outs = [(ANY, ((rows.stop - rows.start, ROW), BF16)) for _, rows in pieces] or [(ANY, spans)]
    sums = call(
        kernel, "span_sums", [(SM, coords)] + arrays, outs, [spans] * 3 + [2 * count, max(count, len(pieces))], 40
    )
    return sums[0] if sides is None else [sums[len(sides) * at : len(sides) * (at + 1)] for at in range(count)]


def late_rows(late, above, below):
    gains = jnp.pad(late[0:8], ((above, below - 8), (0, 0)))
    return gains + jnp.pad(late[8:10], ((above + REL_AT, below - REL_AT - 2), (0, 0)))


def scatter_slow(state, back, shard_size, padded):
    late = back["late"]
    pieces = []
    for source, half in ((back, "low"), (state, "high")):
        for core in range(2):
            for at in range(8):
                z, x = at // 2, at % 2
                if core == 0:
                    span = source[half + "_kept"][4 * x + 3 - z]
                else:
                    span = source[half + ("_near", "_far")[x]][3 - z]
                d = len(pieces)
                pieces.append(span[: STARTS[d + 1] - STARTS[d] if d < PARTS - 1 else SPAN])
    rows = jnp.concatenate(pieces)
    first = ROW * BLOCK["small"][0]
    rows = low(rows.astype(F32) + late_rows(late, first, rows.shape[0] - first))
    flat = rows.reshape(-1)[: segment_bounds()[-1]]
    shard = lax.psum_scatter(flat, AXES, scatter_dimension=0, tiled=True)
    return jnp.pad(shard, (0, padded - shard_size)).astype(F32), lax.psum(late[0:8], AXES)


def scatter_grads(state, back, coords, me, shard_size, padded):
    if not fast_mesh():
        return scatter_slow(state, back, shard_size, padded)
    high = coords[0] == 1
    high_kept, low_kept = state["high_kept"], back["low_kept"]
    high_got = [over_core(state["high_near"]), over_core(state["high_far"])]
    low_far = over_core(back["low_far"])

    def chip_sum(own_half, x, places, sides=None):
        got = (low_far if x else low_near, high_got[x])
        return span_sums(coords, own_half, x, places, low_kept, got[0], high_kept, got[1], sides)

    late = back["late"]
    late = late + over_x(late)
    late = late + over_y(late)
    for_x, for_y = chip_sum(False, 1, (2, 3)), chip_sum(False, 1, (0, 1))
    for_x, for_y, late = lax.optimization_barrier((for_x, for_y, late))
    from_x, from_y = over_x(for_x), over_y(for_y)
    low_near = over_core(after(back["low_near"], for_x, for_y))
    late = late + over_core(late)
    late = late + over_z(late, 1)
    late = late + over_z(late, 2)
    to_x, to_y, mine = [
        chip_sum(own_half, x, range(4), SIDES) for own_half, x in ((True, 1), (False, 0), (True, 0))
    ]
    from_x, from_y, to_x, to_y, mine, late = lax.optimization_barrier((from_x, from_y, to_x, to_y, mine, late))
    running = [None, None]
    before = [(), ()]
    for at in range(4):
        for side, rows in enumerate(SIDES):
            send_x, send_y = to_x[at][side], to_y[at][side]
            if at < 2:
                send_x = low(added(send_x, from_y[at, rows]))
            else:
                send_y = low(added(send_y, from_x[at - 2, rows]))
            got_x, got_y = over_x(after(send_x, *before[side])), over_y(after(send_y, *before[side]))
            before[side] = (got_x, got_y)
            parts = [mine[at][side], got_x, got_y]
            if at:
                parts.append(round_z(running[side]))
            running[side] = added(*parts)
            if at < 3:
                running[side] = low(running[side])
    total = jnp.concatenate(running)
    first = ROW * BLOCK["small"][0] - STARTS[PARTS - 1]
    total = total + jnp.where(me == PARTS - 1, 1.0, 0.0) * late_rows(late, first, SPAN - first)
    flat = jnp.pad(total.reshape(-1), (0, max(0, TILE * ROW + padded - SPAN * ROW)))
    return lax.dynamic_slice(flat, (shard_offset(me, shard_size),), (padded,)), late[0:8]


def sum_everywhere(vector):
    if not fast_mesh():
        return lax.psum(vector, AXES)
    vector = vector + over_core(vector)
    vector = vector + over_x(vector)
    vector = vector + over_y(vector)
    vector = vector + over_z(vector, 1)
    return vector + over_z(vector, 2)


def most_segments(shard_size, devices):
    bounds = segment_bounds()
    most = 1
    for at in range(devices):
        low_end, high_end = at * shard_size, (at + 1) * shard_size
        most = max(most, sum(1 for b in bounds[1:-1] if low_end < b < high_end) + 1)
    return most


LANES = 128
CHUNK = 1024 * LANES
STRIP = 128 * LANES


def chunk_spans(segments, step):
    first, last = step * CHUNK, (step + 1) * CHUNK
    for at in range(segments.shape[0] - 2):
        start, end = segments[1 + at], segments[2 + at]
        whole = (start <= first) & (last <= end)
        some = (start < last) & (end > first) & jnp.logical_not(whole)
        yield at, whole, some, start - first, end - first


def strips(body, start=None):
    return lax.fori_loop(0, CHUNK // STRIP, lambda at, carry: body(part(at, STRIP), at * STRIP, carry), start)


def square(entries, strip):
    return entries[strip].reshape(STRIP // LANES, LANES)


def inside(place, start, end):
    row = lax.broadcasted_iota(jnp.int32, (STRIP // LANES, LANES), 0)
    place = place + row * LANES + lax.broadcasted_iota(jnp.int32, (STRIP // LANES, LANES), 1)
    return (place >= start) & (place < end)


def fold(values):
    return jnp.sum(values.reshape(-1, 8, LANES), axis=0)


def update_kernel(segments, params, first, second, grad, new_first, new_second, update, sums):
    step = pl.program_id(0)
    nothing = jnp.zeros((8, LANES), F32)

    @pl.when(step == 0)
    def _():
        sums[...] = nothing

    def move(strip, place, totals):
        grads = grad[strip]
        firsts = BETA_FIRST * first[strip] + (1.0 - BETA_FIRST) * grads
        seconds = BETA_SECOND * second[strip] + (1.0 - BETA_SECOND) * grads * grads
        new_first[strip] = firsts
        new_second[strip] = seconds
        first_hat = firsts * (1.0 / (1.0 - BETA_FIRST**STEP))
        second_hat = seconds * (1.0 / (1.0 - BETA_SECOND**STEP))
        weights = params[strip]
        change = first_hat / (jnp.sqrt(second_hat) + ADAM_EPS) + WEIGHT_DECAY * weights
        update[strip] = change
        squares = [(each_one * each_one).reshape(STRIP // LANES, LANES) for each_one in (weights, change)]
        return totals[0] + fold(squares[0]), totals[1] + fold(squares[1])

    totals = strips(move, (nothing, nothing))
    lane = lax.broadcasted_iota(jnp.int32, (1, LANES), 1)

    def add(at, totals):
        for row, total in enumerate(totals):
            total = jnp.sum(jnp.sum(total, axis=0, keepdims=True), axis=1, keepdims=True)
            sums[row : row + 1, :] += jnp.where(lane == segments[0] + at, total, 0.0)

    for at, whole, some, start, end in chunk_spans(segments, step):

        @pl.when(whole)
        def _(at=at):
            add(at, totals)

        @pl.when(some)
        def _(at=at, start=start, end=end):
            def squares(strip, place, totals):
                here = inside(place, start, end)
                own = [square(entries, strip) for entries in (params, update)]
                own = [fold(jnp.where(here, each_one * each_one, 0.0)) for each_one in own]
                return totals[0] + own[0], totals[1] + own[1]

            add(at, strips(squares, (nothing, nothing)))


def apply_kernel(segments, sums, params, update, new_params, norms):
    step = pl.program_id(0)
    roots = jnp.sqrt(sums[0:2, :])
    trust = roots[0:1, :] / (roots[1:2, :] + ADAM_EPS)
    norms[0:2, :] = roots
    norms[2:3, :] = trust
    norms[3:8, :] = jnp.zeros((5, LANES), F32)
    lane = lax.broadcasted_iota(jnp.int32, (1, LANES), 1)
    for at, whole, some, start, end in chunk_spans(segments, step):

        scale = LEARN_RATE * jnp.sum(jnp.where(lane == segments[0] + at, trust, 0.0), axis=1, keepdims=True)
        scale = jnp.broadcast_to(scale, (1, LANES))

        def moved(strip, scale=scale):
            return square(params, strip) - scale * square(update, strip)

        @pl.when(whole)
        def _(moved=moved):
            def all_of(strip, place, carry):
                new_params[strip] = moved(strip).reshape(STRIP)
                return carry

            strips(all_of, 0)

        @pl.when(some)
        def _(moved=moved, start=start, end=end):
            def part_of(strip, place, carry):
                chosen = jnp.where(inside(place, start, end), moved(strip), square(new_params, strip))
                new_params[strip] = chosen.reshape(STRIP)
                return carry

            strips(part_of, 0)


def shards(frames, lengths, cotangent, params, first_moment, second_moment):
    shard_size = params.shape[0]
    devices = lax.axis_size("dp") * lax.axis_size("fsdp")
    me = lax.axis_index(AXES)
    if fast_mesh():
        dp, fsdp = lax.axis_index("dp"), lax.axis_index("fsdp")
        coords = jnp.stack([dp // 2, dp % 2, fsdp // 2, fsdp % 2]).astype(jnp.int32)
    else:
        coords = jnp.zeros((4,), jnp.int32)
    state = forward(coords, lengths, frames[0], cotangent[0], gather_shards(low(params), me))
    back = backward(coords, frames[0], state)
    steps = -(-shard_size // CHUNK)
    size = max(shard_size, CHUNK)
    grad_shard, gain_grads = scatter_grads(state, back, coords, me, shard_size, size)

    def filled(flat):
        return jnp.pad(flat, (0, size - shard_size)) if size > shard_size else flat

    bounds = segment_bounds()
    spans = most_segments(shard_size, devices)
    shard_low = me * shard_size
    first_segment = sum((shard_low >= b).astype(jnp.int32) for b in bounds[1:-1])
    table = jnp.asarray(bounds[1:] + [bounds[-1]] * spans, jnp.int32)
    ends = jnp.clip(lax.dynamic_slice(table, (first_segment,), (spans,)) - shard_low, 0, shard_size)
    segments = jnp.concatenate([first_segment[None], jnp.zeros((1,), jnp.int32), ends]).astype(jnp.int32)
    grid = pl.BlockSpec((CHUNK,), lambda step: (step,))
    whole = pl.BlockSpec((8, LANES), lambda step: (0, 0))
    flat_kind = jax.ShapeDtypeStruct((size,), F32)
    tile_kind = jax.ShapeDtypeStruct((8, LANES), F32)
    weights = filled(params)
    new_first, new_second, update, sums = pl.pallas_call(
        update_kernel,
        name="update",
        grid=(steps,),
        in_specs=[SM] + [grid] * 4,
        out_specs=[grid] * 3 + [whole],
        out_shape=[flat_kind] * 3 + [tile_kind],
    )(segments, weights, filled(first_moment), filled(second_moment), grad_shard)
    sums = sum_everywhere(sums)
    new_params, norms = pl.pallas_call(
        apply_kernel,
        name="apply",
        grid=(steps,),
        in_specs=[SM, whole, grid, grid],
        out_specs=[grid, whole],
        out_shape=[flat_kind, tile_kind],
    )(segments, sums, weights, update)
    count = len(segment_shapes())
    return (
        state["out"].reshape(frames.shape),
        back["fgrad"].reshape(frames.shape),
        new_params[:shard_size],
        new_first[:shard_size],
        new_second[:shard_size],
        norms[0, :count],
        norms[1, :count],
        norms[2, :count],
        gain_grads.reshape(-1),
    )


def solution(mesh):
    placed = (
        P(("dp", "fsdp"), None, None),
        P(("dp", "fsdp")),
        P(("dp", "fsdp"), None, None),
        P(("dp", "fsdp")),
        P(("dp", "fsdp")),
        P(("dp", "fsdp")),
    )
    return jax.shard_map(
        shards,
        mesh=mesh,
        in_specs=placed,
        out_specs=(
            P(("dp", "fsdp"), None, None),
            P(("dp", "fsdp"), None, None),
            P(("dp", "fsdp")),
            P(("dp", "fsdp")),
            P(("dp", "fsdp")),
            P(),
            P(),
            P(),
            P(),
        ),
        check_vma=False,
    )
```

profile of v0, /device:TPU:0, one launch (start us, length us, event | category | flops | bytes accessed | tf_op | source)
XLA Modules:
  0.0 292.9 jit_solution(5848105314778586018)
XLA Ops:
  2.8 3.0 %collective-permute-start.2 = (bf16[528,512]{1,0:T(8,128)(2,1)S(1)}, bf16[528,512]{1,0:T(8,128)(2,1)S(1)}, u32[]{:S(2)}, u32[]{:S(2)}) collective-permute-start(bf16[528,512]{1,0:T(8,128)(2,1)S(1)} %reshape.49.refs_4_), channel_id=1, source_target_pairs={{0,16},{8,24},{16,0},{24,8},{1,17},{9,25},{17,1},{25,9},{2,18},{10... | collective-permute-start | bytes 1622024 | tf_op jit(solution)/shard_map/ppermute | solution.py:1038
  5.8 1.5 collective-permute-start.1
  7.3 1.6 collective-permute-start
  8.9 9.2 %collective-permute-done.2.refs_14_ = bf16[528,512]{1,0:T(8,128)(2,1)S(1)} collective-permute-done((bf16[528,512]{1,0:T(8,128)(2,1)S(1)}, bf16[528,512]{1,0:T(8,128)(2,1)S(1)}, u32[]{:S(2)}, u32[]{:S(2)}) %collective-permute-start.2) | collective-permute-done | bytes 540704 | tf_op jit(solution)/shard_map/ppermute | solution.py:1038
  18.1 1.5 collective-permute-done.1.refs_8_
  19.5 3.1 %collective-permute-done.refs_5_ = bf16[528,512]{1,0:T(8,128)(2,1)S(1)} collective-permute-done((bf16[528,512]{1,0:T(8,128)(2,1)S(1)}, bf16[528,512]{1,0:T(8,128)(2,1)S(1)}, u32[]{:S(2)}, u32[]{:S(2)}) %collective-permute-start) | collective-permute-done | bytes 540704 | tf_op jit(solution)/shard_map/ppermute | solution.py:1046
  23.7 11.6 %collective-permute-done.5.refs_15_ = bf16[528,512]{1,0:T(8,128)(2,1)} collective-permute-done((bf16[528,512]{1,0:T(8,128)(2,1)S(1)}, bf16[528,512]{1,0:T(8,128)(2,1)}, u32[]{:S(2)}, u32[]{:S(2)}) %collective-permute-start.5) | collective-permute-done | bytes 540704 | tf_op jit(solution)/shard_map/ppermute | solution.py:1038
  35.4 2.3 collective-permute-done.3.refs_6_
  37.8 1.3 collective-permute-start.7
  39.1 1.6 collective-permute-start.9
  41.7 9.1 %collective-permute-done.6.refs_7_ = bf16[528,512]{1,0:T(8,128)(2,1)S(1)} collective-permute-done((bf16[528,512]{1,0:T(8,128)(2,1)S(1)}, bf16[528,512]{1,0:T(8,128)(2,1)S(1)}, u32[]{:S(2)}, u32[]{:S(2)}) %collective-permute-start.6) | collective-permute-done | bytes 540704 | tf_op jit(solution)/shard_map/ppermute | solution.py:1046
  52.1 1.6 collective-permute-start.11
  53.7 5.0 %collective-permute-done.7.refs_10_ = bf16[784,512]{1,0:T(8,128)(2,1)S(1)} collective-permute-done((bf16[784,512]{1,0:T(8,128)(2,1)S(1)}, bf16[784,512]{1,0:T(8,128)(2,1)S(1)}, u32[]{:S(2)}, u32[]{:S(2)}) %collective-permute-start.7) | collective-permute-done | bytes 802848 | tf_op jit(solution)/shard_map/ppermute | solution.py:1034
  58.7 1.4 collective-permute-start.13
  62.6 16.9 %collective-permute-done.13.refs_18_ = bf16[272,512]{1,0:T(8,128)(2,1)S(1)} collective-permute-done((bf16[272,512]{1,0:T(8,128)(2,1)S(1)}, bf16[272,512]{1,0:T(8,128)(2,1)S(1)}, u32[]{:S(2)}, u32[]{:S(2)}) %collective-permute-start.13) | collective-permute-done | bytes 278560 | tf_op jit(solution)/shard_map/ppermute | solution.py:1038
  80.3 1.6 collective-permute-start.14
  84.0 5.3 %collective-permute-done.14.refs_19_ = bf16[272,512]{1,0:T(8,128)(2,1)S(1)} collective-permute-done((bf16[272,512]{1,0:T(8,128)(2,1)S(1)}, bf16[272,512]{1,0:T(8,128)(2,1)S(1)}, u32[]{:S(2)}, u32[]{:S(2)}) %collective-permute-start.14) | collective-permute-done | bytes 278560 | tf_op jit(solution)/shard_map/ppermute | solution.py:1038
  89.9 1.9 collective-permute-done.12.refs_13_
  91.8 1.5 collective-permute-done.24.refs_29_
  97.3 2.9 collective-permute-done.26.refs_31_
  101.1 44.0 %forward.1 = (bf16[160,512]{1,0:T(8,128)(2,1)}, f32[8,512]{1,0:T(8,128)}, f32[176,512]{1,0:T(8,128)}, bf16[8,528,512]{2,1,0:T(8,128)(2,1)}, bf16[4,528,512]{2,1,...) custom-call(s32[4]{0:T(128)} %pad_add_fusion.refs_0_.coords, ...), custom_call_target="tpu_custom_call" | custom-call | tf_op jit(solution)/shard_map/forward/pallas_call | solution.py:972
  145.4 15.4 %backward.1 = (bf16[160,512]{1,0:T(8,128)(2,1)}, f32[16,512]{1,0:T(8,128)}, bf16[8,528,512]{2,1,0:T(8,128)(2,1)}, bf16[4,528,512]{2,1,0:T(8,128)(2,1)}, bf16[4,528,512]{2,1,0:T(8,128)(2,1)}) custom-call(s32[4]{0:T(128)} %pad_add_fusion.refs_0_.coords, bf16[160,512]{1,0:T(8,128)(2,1)} %bitcast.49, ...), custom_call_target="tpu_custom_call", output_to_operand_aliasing={{2}: (18, {}), {3}: (19, {}), {4}: (20, {})} | custom-call | tf_op jit(solution)/shard_map/backward/pallas_call | solution.py:972
  161.8 3.4 %collective-permute-done.33 = f32[16,512]{1,0:T(8,128)S(1)} collective-permute-done((f32[16,512]{1,0:T(8,128)}, f32[16,512]{1,0:T(8,128)S(1)}, u32[]{:S(2)}, u32[]{:S(2)}) %collective-permute-start.33) | collective-permute-done | bytes 32800 | tf_op jit(solution)/shard_map/ppermute | solution.py:1034
  166.0 3.1 %collective-permute-start.34 = (f32[16,512]{1,0:T(8,128)S(1)}, f32[16,512]{1,0:T(8,128)S(1)}, u32[]{:S(2)}, u32[]{:S(2)}) collective-permute-start(f32[16,512]{1,0:T(8,128)S(1)} %add.199), channel_id=1, source_target_pairs={{0,16},{8,24},{16,0},{24,8},{1,17},{9,25},{17,1},{25,9},{2,18},{10... | collective-permute-start | bytes 98312 | tf_op jit(solution)/shard_map/ppermute | solution.py:1038
  169.1 1.9 collective-permute-done.34
  171.1 3.0 %copy-done = bf16[8,528,512]{2,1,0:T(8,128)(2,1)S(1)} copy-done((bf16[8,528,512]{2,1,0:T(8,128)(2,1)S(1)}, bf16[8,528,512]{2,1,0:T(8,128)(2,1)}, u32[]{:S(2)}) %copy-start) | copy-done | bytes 4325400
  174.1 2.2 span_sums.6
  176.3 3.0 %span_sums.5 = bf16[2,528,512]{2,1,0:T(8,128)(2,1)} custom-call(s32[4]{0:T(128)S(1)} %copy-done.10, bf16[8,528,512]{2,1,0:T(8,128)(2,1)S(1)} %copy-done, bf16[4,528,512]{2,1,0:T(8,128)(2,1)S(1)} %collective-permute-done.31.low_got, bf16[8,528,512]{2,1,0:T(8,128)(2,1)S(1)} %bitcast.46, bf16[4,528,512]{2,1,0:T(8,128)(2,1)} %collective-permute-done.32.high_got), custom_call_target="tpu_custom_call" | custom-call | tf_op jit(solution)/shard_map/span_sums/pallas_call | solution.py:972
  180.5 3.2 %collective-permute-done.39 = f32[16,512]{1,0:T(8,128)S(1)} collective-permute-done((f32[16,512]{1,0:T(8,128)S(1)}, f32[16,512]{1,0:T(8,128)S(1)}, u32[]{:S(2)}, u32[]{:S(2)}) %collective-permute-start.39) | collective-permute-done | bytes 32800 | tf_op jit(solution)/shard_map/ppermute | solution.py:1042
  183.7 3.9 %collective-permute-done.40 = f32[16,512]{1,0:T(8,128)S(1)} collective-permute-done((f32[16,512]{1,0:T(8,128)S(1)}, f32[16,512]{1,0:T(8,128)S(1)}, u32[]{:S(2)}, u32[]{:S(2)}) %collective-permute-start.40) | collective-permute-done | bytes 32800 | tf_op jit(solution)/shard_map/ppermute | solution.py:1050
  187.6 2.1 collective-permute-start.41
  189.7 2.2 copy-done.1
  192.0 1.6 copy-done.3
  193.6 2.6 span_sums.7
  198.2 2.4 span_sums.9
  202.8 3.1 %span_sums.8 = (bf16[256,512]{1,0:T(8,128)(2,1)S(1)}, bf16[272,512]{1,0:T(8,128)(2,1)S(1)}, bf16[256,512]{1,0:T(8,128)(2,1)S(1)}, bf16[272,512]{1,0:T(8,128)(2,1...) custom-call(s32[4]{0:T(128)S(1)} %copy-done.10, ...), custom_call_target="tpu_custom_call" | custom-call | tf_op jit(solution)/shard_map/span_sums/pallas_call | solution.py:972
  209.4 1.3 collective-permute-start.42
  213.9 1.5 collective-permute-done.43
  215.4 3.3 %collective-permute-done.42 = bf16[256,512]{1,0:T(8,128)(2,1)S(1)} collective-permute-done((bf16[256,512]{1,0:T(8,128)(2,1)S(1)}, bf16[256,512]{1,0:T(8,128)(2,1)S(1)}, u32[]{:S(2)}, u32[]{:S(2)}) %collective-permute-start.42) | collective-permute-done | bytes 262176 | tf_op jit(solution)/shard_map/ppermute | solution.py:1034
  218.7 1.3 collective-permute-start.44
  220.4 2.0 collective-permute-start.50
  222.4 2.2 collective-permute-done.53
  226.4 3.9 %collective-permute-done.44 = bf16[256,512]{1,0:T(8,128)(2,1)S(1)} collective-permute-done((bf16[256,512]{1,0:T(8,128)(2,1)S(1)}, bf16[256,512]{1,0:T(8,128)(2,1)S(1)}, u32[]{:S(2)}, u32[]{:S(2)}) %collective-permute-start.44) | collective-permute-done | bytes 262176 | tf_op jit(solution)/shard_map/ppermute | solution.py:1034
  230.3 1.9 collective-permute-start.61
  232.2 2.0 fusion.5
  238.1 3.5 %collective-permute-done.61 = bf16[272,512]{1,0:T(8,128)(2,1)S(1)} collective-permute-done((bf16[272,512]{1,0:T(8,128)(2,1)S(1)}, bf16[272,512]{1,0:T(8,128)(2,1)S(1)}, u32[]{:S(2)}, u32[]{:S(2)}) %collective-permute-start.61) | collective-permute-done | bytes 278560 | tf_op jit(solution)/shard_map/ppermute | solution.py:1046
  241.8 1.8 collective-permute-done.46
  245.7 1.3 collective-permute-start.48
  248.9 2.1 collective-permute-start.52
  251.0 2.1 collective-permute-done.58
  254.4 1.4 collective-permute-start.63
  257.0 1.8 collective-permute-done.52
  260.5 2.3 collective-permute-done.63
  263.4 1.3 dynamic_slice.11.grad
  264.7 5.3 %update.1 = (f32[256592]{0:T(1024)}, f32[256592]{0:T(1024)}, f32[256592]{0:T(1024)}, f32[8,128]{1,0:T(8,128)}) custom-call(s32[6]{0:T(128)} %pad_add_fusion.1.segments, f32[256592]{0:T(1024)} %params.3, f32[256592]{0:T(1024)} %first.1, f32[256592]{0:T(1024)} %second.1, f32[256592]{0:T(1024)} %dynamic_slice.11.grad), custom_call_target="tpu_custom_call" | custom-call | tf_op jit(solution)/shard_map/update/pallas_call | solution.py:1392
  270.0 1.4 collective-permute-done.64
  272.1 1.7 collective-permute-start.65
  273.7 1.9 collective-permute-done.65
  275.7 1.7 collective-permute-start.66
  277.4 1.9 collective-permute-done.66
  279.3 3.6 %collective-permute-done.67 = f32[8,128]{1,0:T(8,128)S(1)} collective-permute-done((f32[8,128]{1,0:T(8,128)S(1)}, f32[8,128]{1,0:T(8,128)S(1)}, u32[]{:S(2)}, u32[]{:S(2)}) %collective-permute-start.67) | collective-permute-done | bytes 4128 | tf_op jit(solution)/shard_map/ppermute | solution.py:1050
  283.9 3.5 %collective-permute-done.68 = f32[8,128]{1,0:T(8,128)S(1)} collective-permute-done((f32[8,128]{1,0:T(8,128)S(1)}, f32[8,128]{1,0:T(8,128)S(1)}, u32[]{:S(2)}, u32[]{:S(2)}) %collective-permute-start.68) | collective-permute-done | bytes 4128 | tf_op jit(solution)/shard_map/ppermute | solution.py:1050
  288.0 3.6 %apply.1 = (f32[256592]{0:T(1024)}, f32[8,128]{1,0:T(8,128)}) custom-call(s32[6]{0:T(128)} %pad_add_fusion.1.segments, f32[8,128]{1,0:T(8,128)} %add.241.sums, f32[256592]{0:T(1024)} %params.3, f32[256592]{0:T(1024)} %get-tuple-element.234.update), custom_call_target="tpu_custom_call" | custom-call | tf_op jit(solution)/shard_map/apply/pallas_call | solution.py:1401
  291.6 1.3 slice_bitcast_fusion
  (218 shorter events, 47.0 us)
Async XLA Ops:
  2.8 15.3 %collective-permute-start.2 = (bf16[528,512]{1,0:T(8,128)(2,1)S(1)}, bf16[528,512]{1,0:T(8,128)(2,1)S(1)}, u32[]{:S(2)}, u32[]{:S(2)}) collective-permute-start(bf16[528,512]{1,0:T(8,128)(2,1)S(1)} %reshape.49.refs_4_), channel_id=1, source_target_pairs={{0,16},{8,24},{16,0},{24,8},{1,17},{9,25},{17,1},{25,9},{2,18},{10... | collective-permute-start | bytes 1622024 | tf_op jit(solution)/shard_map/ppermute | solution.py:1038
  5.8 13.7 %collective-permute-start.1 = (bf16[528,512]{1,0:T(8,128)(2,1)S(1)}, bf16[528,512]{1,0:T(8,128)(2,1)S(1)}, u32[]{:S(2)}, u32[]{:S(2)}) collective-permute-start(bf16[528,512]{1,0:T(8,128)(2,1)S(1)} %reshape.49.refs_4_), channel_id=1, source_target_pairs={{0,1},{1,0},{2,3},{3,2},{4,5},{5,4},{6,7},{7,6},{8,9},{9,8},{10,11... | collective-permute-start | bytes 1622024 | tf_op jit(solution)/shard_map/ppermute | solution.py:1034
  7.3 15.3 %collective-permute-start = (bf16[528,512]{1,0:T(8,128)(2,1)S(1)}, bf16[528,512]{1,0:T(8,128)(2,1)S(1)}, u32[]{:S(2)}, u32[]{:S(2)}) collective-permute-start(bf16[528,512]{1,0:T(8,128)(2,1)S(1)} %reshape.49.refs_4_), channel_id=1, source_target_pairs={{0,2},{1,3},{2,4},{3,5},{4,6},{5,7},{6,0},{7,1},{8,10},{9,11},{10,... | collective-permute-start | bytes 1622024 | tf_op jit(solution)/shard_map/ppermute | solution.py:1046
  22.6 12.7 %collective-permute-start.5 = (bf16[528,512]{1,0:T(8,128)(2,1)S(1)}, bf16[528,512]{1,0:T(8,128)(2,1)}, u32[]{:S(2)}, u32[]{:S(2)}) collective-permute-start(bf16[528,512]{1,0:T(8,128)(2,1)S(1)} %collective-permute-done.refs_5_), channel_id=1, source_target_pairs={{0,16},{8,24},{16,0},{24,8},{1,17},{9,25},{17,1},{25,9},{2,18},{10... | collective-permute-start | bytes 1622024 | tf_op jit(solution)/shard_map/ppermute | solution.py:1038
  23.1 12.3 %collective-permute-start.4 = (bf16[528,512]{1,0:T(8,128)(2,1)S(1)}, bf16[528,512]{1,0:T(8,128)(2,1)S(1)}, u32[]{:S(2)}, u32[]{:S(2)}) collective-permute-start(bf16[528,512]{1,0:T(8,128)(2,1)S(1)} %collective-permute-done.refs_5_), channel_id=1, source_target_pairs={{0,1},{1,0},{2,3},{3,2},{4,5},{5,4},{6,7},{7,6},{8,9},{9,8},{10,11... | collective-permute-start | bytes 1622024 | tf_op jit(solution)/shard_map/ppermute | solution.py:1034
  23.6 14.1 %collective-permute-start.3 = (bf16[528,512]{1,0:T(8,128)(2,1)S(1)}, bf16[528,512]{1,0:T(8,128)(2,1)S(1)}, u32[]{:S(2)}, u32[]{:S(2)}) collective-permute-start(bf16[528,512]{1,0:T(8,128)(2,1)S(1)} %collective-permute-done.refs_5_), channel_id=1, source_target_pairs={{0,2},{1,3},{2,4},{3,5},{4,6},{5,7},{6,0},{7,1},{8,10},{9,11},{10,... | collective-permute-start | bytes 1622024 | tf_op jit(solution)/shard_map/ppermute | solution.py:1046
  37.7 13.1 %collective-permute-start.6 = (bf16[528,512]{1,0:T(8,128)(2,1)S(1)}, bf16[528,512]{1,0:T(8,128)(2,1)S(1)}, u32[]{:S(2)}, u32[]{:S(2)}) collective-permute-start(bf16[528,512]{1,0:T(8,128)(2,1)S(1)} %collective-permute-done.3.refs_6_), channel_id=1, source_target_pairs={{0,2},{1,3},{2,4},{3,5},{4,6},{5,7},{6,0},{7,1},{8,10},{9,11},{10,... | collective-permute-start | bytes 1622024 | tf_op jit(solution)/shard_map/ppermute | solution.py:1046
  37.8 20.9 %collective-permute-start.7 = (bf16[784,512]{1,0:T(8,128)(2,1)S(1)}, bf16[784,512]{1,0:T(8,128)(2,1)S(1)}, u32[]{:S(2)}, u32[]{:S(2)}) collective-permute-start(bf16[784,512]{1,0:T(8,128)(2,1)S(1)} %pad_maximum_fusion.2), channel_id=1, source_target_pairs={{0,1},{1,0},{2,3},{3,2},{4,5},{5,4},{6,7},{7,6},{8,9},{9,8},{10,11... | collective-permute-start | bytes 2408456 | tf_op jit(solution)/shard_map/ppermute | solution.py:1034
  39.1 21.4 %collective-permute-start.9 = (bf16[800,512]{1,0:T(8,128)(2,1)S(1)}, bf16[800,512]{1,0:T(8,128)(2,1)}, u32[]{:S(2)}, u32[]{:S(2)}) collective-permute-start(bf16[800,512]{1,0:T(8,128)(2,1)S(1)} %pad_maximum_fusion), channel_id=1, source_target_pairs={{0,16},{8,24},{16,0},{24,8},{1,17},{9,25},{17,1},{25,9},{2,18},{10... | collective-permute-start | bytes 2457608 | tf_op jit(solution)/shard_map/ppermute | solution.py:1038
  40.7 21.8 %collective-permute-start.15 = (bf16[528,512]{1,0:T(8,128)(2,1)S(1)}, bf16[528,512]{1,0:T(8,128)(2,1)S(1)}, u32[]{:S(2)}, u32[]{:S(2)}) collective-permute-start(bf16[528,512]{1,0:T(8,128)(2,1)S(1)} %reshape.49.refs_4_), channel_id=1, source_target_pairs={{0,8},{8,0},{16,24},{24,16},{1,9},{9,1},{17,25},{25,17},{2,10},{10... | collective-permute-start | bytes 1622024 | tf_op jit(solution)/shard_map/ppermute | solution.py:1042
  50.9 29.2 %collective-permute-start.8 = (bf16[784,512]{1,0:T(8,128)(2,1)S(1)}, bf16[784,512]{1,0:T(8,128)(2,1)S(1)}, u32[]{:S(2)}, u32[]{:S(2)}) collective-permute-start(bf16[784,512]{1,0:T(8,128)(2,1)S(1)} %pad_maximum_fusion.3), channel_id=1, source_target_pairs={{0,1},{1,0},{2,3},{3,2},{4,5},{5,4},{6,7},{7,6},{8,9},{9,8},{10,11... | collective-permute-start | bytes 2408456 | tf_op jit(solution)/shard_map/ppermute | solution.py:1034
  52.1 29.8 %collective-permute-start.11 = (bf16[800,512]{1,0:T(8,128)(2,1)S(1)}, bf16[800,512]{1,0:T(8,128)(2,1)}, u32[]{:S(2)}, u32[]{:S(2)}) collective-permute-start(bf16[800,512]{1,0:T(8,128)(2,1)S(1)} %pad_maximum_fusion.1), channel_id=1, source_target_pairs={{0,16},{8,24},{16,0},{24,8},{1,17},{9,25},{17,1},{25,9},{2,18},{10... | collective-permute-start | bytes 2457608 | tf_op jit(solution)/shard_map/ppermute | solution.py:1038
  58.7 20.9 %collective-permute-start.13 = (bf16[272,512]{1,0:T(8,128)(2,1)S(1)}, bf16[272,512]{1,0:T(8,128)(2,1)S(1)}, u32[]{:S(2)}, u32[]{:S(2)}) collective-permute-start(bf16[272,512]{1,0:T(8,128)(2,1)S(1)} %slice.87), channel_id=1, source_target_pairs={{0,16},{8,24},{16,0},{24,8},{1,17},{9,25},{17,1},{25,9},{2,18},{10... | collective-permute-start | bytes 835592 | tf_op jit(solution)/shard_map/ppermute | solution.py:1038
  61.5 18.1 %collective-permute-start.10 = (bf16[256,512]{1,0:T(8,128)(2,1)S(1)}, bf16[256,512]{1,0:T(8,128)(2,1)S(1)}, u32[]{:S(2)}, u32[]{:S(2)}) collective-permute-start(bf16[256,512]{1,0:T(8,128)(2,1)S(1)} %slice.85), channel_id=1, source_target_pairs={{0,1},{1,0},{2,3},{3,2},{4,5},{5,4},{6,7},{7,6},{8,9},{9,8},{10,11... | collective-permute-start | bytes 786440 | tf_op jit(solution)/shard_map/ppermute | solution.py:1034
  62.6 17.7 %collective-permute-start.19 = (bf16[528,512]{1,0:T(8,128)(2,1)S(1)}, bf16[528,512]{1,0:T(8,128)(2,1)S(1)}, u32[]{:S(2)}, u32[]{:S(2)}) collective-permute-start(bf16[528,512]{1,0:T(8,128)(2,1)S(1)} %collective-permute-done.1.refs_8_), channel_id=1, source_target_pairs={{0,8},{8,0},{16,24},{24,16},{1,9},{9,1},{17,25},{25,17},{2,10},{10... | collective-permute-start | bytes 1622024 | tf_op jit(solution)/shard_map/ppermute | solution.py:1042
  79.6 3.9 %collective-permute-start.16 = (bf16[528,512]{1,0:T(8,128)(2,1)S(1)}, bf16[528,512]{1,0:T(8,128)(2,1)S(1)}, u32[]{:S(2)}, u32[]{:S(2)}) collective-permute-start(bf16[528,512]{1,0:T(8,128)(2,1)S(1)} %collective-permute-done.refs_5_), channel_id=1, source_target_pairs={{0,8},{8,0},{16,24},{24,16},{1,9},{9,1},{17,25},{25,17},{2,10},{10... | collective-permute-start | bytes 1622024 | tf_op jit(solution)/shard_map/ppermute | solution.py:1042
  80.1 3.8 %collective-permute-start.23 = (bf16[256,512]{1,0:T(8,128)(2,1)S(1)}, bf16[256,512]{1,0:T(8,128)(2,1)}, u32[]{:S(2)}, u32[]{:S(2)}) collective-permute-start(bf16[256,512]{1,0:T(8,128)(2,1)S(1)} %collective-permute-done.10.refs_12_), channel_id=1, source_target_pairs={{0,8},{8,0},{16,24},{24,16},{1,9},{9,1},{17,25},{25,17},{2,10},{10... | collective-permute-start | bytes 786440 | tf_op jit(solution)/shard_map/ppermute | solution.py:1042
  80.3 9.1 %collective-permute-start.14 = (bf16[272,512]{1,0:T(8,128)(2,1)S(1)}, bf16[272,512]{1,0:T(8,128)(2,1)S(1)}, u32[]{:S(2)}, u32[]{:S(2)}) collective-permute-start(bf16[272,512]{1,0:T(8,128)(2,1)S(1)} %slice.88), channel_id=1, source_target_pairs={{0,16},{8,24},{16,0},{24,8},{1,17},{9,25},{17,1},{25,9},{2,18},{10... | collective-permute-start | bytes 835592 | tf_op jit(solution)/shard_map/ppermute | solution.py:1038
  81.9 7.5 %collective-permute-start.29 = (bf16[272,512]{1,0:T(8,128)(2,1)S(1)}, bf16[272,512]{1,0:T(8,128)(2,1)S(1)}, u32[]{:S(2)}, u32[]{:S(2)}) collective-permute-start(bf16[272,512]{1,0:T(8,128)(2,1)S(1)} %collective-permute-done.13.refs_18_), channel_id=1, source_target_pairs={{0,8},{8,0},{16,24},{24,16},{1,9},{9,1},{17,25},{25,17},{2,10},{10... | collective-permute-start | bytes 835592 | tf_op jit(solution)/shard_map/ppermute | solution.py:1042
  83.0 10.9 %collective-permute-start.17 = (bf16[528,512]{1,0:T(8,128)(2,1)S(1)}, bf16[528,512]{1,0:T(8,128)(2,1)S(1)}, u32[]{:S(2)}, u32[]{:S(2)}) collective-permute-start(bf16[528,512]{1,0:T(8,128)(2,1)S(1)} %collective-permute-done.3.refs_6_), channel_id=1, source_target_pairs={{0,8},{8,0},{16,24},{24,16},{1,9},{9,1},{17,25},{25,17},{2,10},{10... | collective-permute-start | bytes 1622024 | tf_op jit(solution)/shard_map/ppermute | solution.py:1042
  83.4 8.4 %collective-permute-start.12 = (bf16[256,512]{1,0:T(8,128)(2,1)S(1)}, bf16[256,512]{1,0:T(8,128)(2,1)S(1)}, u32[]{:S(2)}, u32[]{:S(2)}) collective-permute-start(bf16[256,512]{1,0:T(8,128)(2,1)S(1)} %slice.86), channel_id=1, source_target_pairs={{0,1},{1,0},{2,3},{3,2},{4,5},{5,4},{6,7},{7,6},{8,9},{9,8},{10,11... | collective-permute-start | bytes 786440 | tf_op jit(solution)/shard_map/ppermute | solution.py:1034
  84.0 10.0 %collective-permute-start.18 = (bf16[528,512]{1,0:T(8,128)(2,1)S(1)}, bf16[528,512]{1,0:T(8,128)(2,1)S(1)}, u32[]{:S(2)}, u32[]{:S(2)}) collective-permute-start(bf16[528,512]{1,0:T(8,128)(2,1)S(1)} %collective-permute-done.6.refs_7_), channel_id=1, source_target_pairs={{0,8},{8,0},{16,24},{24,16},{1,9},{9,1},{17,25},{25,17},{2,10},{10... | collective-permute-start | bytes 1622024 | tf_op jit(solution)/shard_map/ppermute | solution.py:1042
  89.3 4.2 %collective-permute-start.30 = (bf16[272,512]{1,0:T(8,128)(2,1)S(1)}, bf16[272,512]{1,0:T(8,128)(2,1)S(1)}, u32[]{:S(2)}, u32[]{:S(2)}) collective-permute-start(bf16[272,512]{1,0:T(8,128)(2,1)S(1)} %collective-permute-done.14.refs_19_), channel_id=1, source_target_pairs={{0,8},{8,0},{16,24},{24,16},{1,9},{9,1},{17,25},{25,17},{2,10},{10... | collective-permute-start | bytes 835592 | tf_op jit(solution)/shard_map/ppermute | solution.py:1042
  89.4 5.0 %collective-permute-start.20 = (bf16[528,512]{1,0:T(8,128)(2,1)S(1)}, bf16[528,512]{1,0:T(8,128)(2,1)S(1)}, u32[]{:S(2)}, u32[]{:S(2)}) collective-permute-start(bf16[528,512]{1,0:T(8,128)(2,1)S(1)} %collective-permute-done.4.refs_9_), channel_id=1, source_target_pairs={{0,8},{8,0},{16,24},{24,16},{1,9},{9,1},{17,25},{25,17},{2,10},{10... | collective-permute-start | bytes 1622024 | tf_op jit(solution)/shard_map/ppermute | solution.py:1042
  93.3 6.9 %collective-permute-start.28 = (bf16[800,512]{1,0:T(8,128)(2,1)}, bf16[800,512]{1,0:T(8,128)(2,1)}, u32[]{:S(2)}, u32[]{:S(2)}) collective-permute-start(bf16[800,512]{1,0:T(8,128)(2,1)} %collective-permute-done.11.refs_17_), channel_id=1, source_target_pairs={{0,8},{8,0},{16,24},{24,16},{1,9},{9,1},{17,25},{25,17},{2,10},{10... | collective-permute-start | bytes 2457608 | tf_op jit(solution)/shard_map/ppermute | solution.py:1042
  93.5 6.8 %collective-permute-start.27 = (bf16[800,512]{1,0:T(8,128)(2,1)}, bf16[800,512]{1,0:T(8,128)(2,1)}, u32[]{:S(2)}, u32[]{:S(2)}) collective-permute-start(bf16[800,512]{1,0:T(8,128)(2,1)} %collective-permute-done.9.refs_16_), channel_id=1, source_target_pairs={{0,8},{8,0},{16,24},{24,16},{1,9},{9,1},{17,25},{25,17},{2,10},{10... | collective-permute-start | bytes 2457608 | tf_op jit(solution)/shard_map/ppermute | solution.py:1042
  93.9 6.4 %collective-permute-start.22 = (bf16[784,512]{1,0:T(8,128)(2,1)S(1)}, bf16[784,512]{1,0:T(8,128)(2,1)}, u32[]{:S(2)}, u32[]{:S(2)}) collective-permute-start(bf16[784,512]{1,0:T(8,128)(2,1)S(1)} %collective-permute-done.8.refs_11_), channel_id=1, source_target_pairs={{0,8},{8,0},{16,24},{24,16},{1,9},{9,1},{17,25},{25,17},{2,10},{10... | collective-permute-start | bytes 2408456 | tf_op jit(solution)/shard_map/ppermute | solution.py:1042
  94.0 6.3 %collective-permute-start.21 = (bf16[784,512]{1,0:T(8,128)(2,1)S(1)}, bf16[784,512]{1,0:T(8,128)(2,1)S(1)}, u32[]{:S(2)}, u32[]{:S(2)}) collective-permute-start(bf16[784,512]{1,0:T(8,128)(2,1)S(1)} %collective-permute-done.7.refs_10_), channel_id=1, source_target_pairs={{0,8},{8,0},{16,24},{24,16},{1,9},{9,1},{17,25},{25,17},{2,10},{10... | collective-permute-start | bytes 2408456 | tf_op jit(solution)/shard_map/ppermute | solution.py:1042
  95.7 4.6 %collective-permute-start.26 = (bf16[528,512]{1,0:T(8,128)(2,1)}, bf16[528,512]{1,0:T(8,128)(2,1)}, u32[]{:S(2)}, u32[]{:S(2)}) collective-permute-start(bf16[528,512]{1,0:T(8,128)(2,1)} %collective-permute-done.5.refs_15_), channel_id=1, source_target_pairs={{0,8},{8,0},{16,24},{24,16},{1,9},{9,1},{17,25},{25,17},{2,10},{10... | collective-permute-start | bytes 1622024 | tf_op jit(solution)/shard_map/ppermute | solution.py:1042
  145.1 25.9 %collective-permute-start.32 = (bf16[4,528,512]{2,1,0:T(8,128)(2,1)}, bf16[4,528,512]{2,1,0:T(8,128)(2,1)}, u32[]{:S(2)}, u32[]{:S(2)}) collective-permute-start(bf16[4,528,512]{2,1,0:T(8,128)(2,1)} %get-tuple-element.162), channel_id=1, source_target_pairs={{0,8},{8,0},{16,24},{24,16},{1,9},{9,1},{17,25},{25,17},{2,10},{10... | collective-permute-start | bytes 6488072 | tf_op jit(solution)/shard_map/ppermute | solution.py:1042
  160.7 10.3 %collective-permute-start.31 = (bf16[4,528,512]{2,1,0:T(8,128)(2,1)}, bf16[4,528,512]{2,1,0:T(8,128)(2,1)S(1)}, u32[]{:S(2)}, u32[]{:S(2)}) collective-permute-start(bf16[4,528,512]{2,1,0:T(8,128)(2,1)} %get-tuple-element.160), channel_id=1, source_target_pairs={{0,8},{8,0},{16,24},{24,16},{1,9},{9,1},{17,25},{25,17},{2,10},{10... | collective-permute-start | bytes 6488072 | tf_op jit(solution)/shard_map/ppermute | solution.py:1042
  161.1 4.1 %collective-permute-start.33 = (f32[16,512]{1,0:T(8,128)}, f32[16,512]{1,0:T(8,128)S(1)}, u32[]{:S(2)}, u32[]{:S(2)}) collective-permute-start(f32[16,512]{1,0:T(8,128)} %get-tuple-element.163), channel_id=1, source_target_pairs={{0,1},{1,0},{2,3},{3,2},{4,5},{5,4},{6,7},{7,6},{8,9},{9,8},{10,11... | collective-permute-start | bytes 98312 | tf_op jit(solution)/shard_map/ppermute | solution.py:1034
  166.0 5.0 %collective-permute-start.34 = (f32[16,512]{1,0:T(8,128)S(1)}, f32[16,512]{1,0:T(8,128)S(1)}, u32[]{:S(2)}, u32[]{:S(2)}) collective-permute-start(f32[16,512]{1,0:T(8,128)S(1)} %add.199), channel_id=1, source_target_pairs={{0,16},{8,24},{16,0},{24,8},{1,17},{9,25},{17,1},{25,9},{2,18},{10... | collective-permute-start | bytes 98312 | tf_op jit(solution)/shard_map/ppermute | solution.py:1038
  169.1 29.1 %collective-permute-start.38 = (bf16[4,528,512]{2,1,0:T(8,128)(2,1)}, bf16[4,528,512]{2,1,0:T(8,128)(2,1)}, u32[]{:S(2)}, u32[]{:S(2)}) collective-permute-start(bf16[4,528,512]{2,1,0:T(8,128)(2,1)} %get-tuple-element.176), channel_id=1, source_target_pairs={{0,8},{8,0},{16,24},{24,16},{1,9},{9,1},{17,25},{25,17},{2,10},{10... | collective-permute-start | bytes 6488072 | tf_op jit(solution)/shard_map/ppermute | solution.py:1042
  179.3 18.9 %collective-permute-start.37 = (bf16[4,528,512]{2,1,0:T(8,128)(2,1)}, bf16[4,528,512]{2,1,0:T(8,128)(2,1)S(1)}, u32[]{:S(2)}, u32[]{:S(2)}) collective-permute-start(bf16[4,528,512]{2,1,0:T(8,128)(2,1)} %get-tuple-element.175), channel_id=1, source_target_pairs={{0,8},{8,0},{16,24},{24,16},{1,9},{9,1},{17,25},{25,17},{2,10},{10... | collective-permute-start | bytes 6488072 | tf_op jit(solution)/shard_map/ppermute | solution.py:1042
  179.4 26.6 %collective-permute-start.35 = (bf16[2,528,512]{2,1,0:T(8,128)(2,1)}, bf16[2,528,512]{2,1,0:T(8,128)(2,1)}, u32[]{:S(2)}, u32[]{:S(2)}) collective-permute-start(bf16[2,528,512]{2,1,0:T(8,128)(2,1)} %span_sums.5), channel_id=1, source_target_pairs={{0,1},{1,0},{2,3},{3,2},{4,5},{5,4},{6,7},{7,6},{8,9},{9,8},{10,11... | collective-permute-start | bytes 3244040 | tf_op jit(solution)/shard_map/ppermute | solution.py:1034
  180.2 26.0 %collective-permute-start.36 = (bf16[2,528,512]{2,1,0:T(8,128)(2,1)S(1)}, bf16[2,528,512]{2,1,0:T(8,128)(2,1)}, u32[]{:S(2)}, u32[]{:S(2)}) collective-permute-start(bf16[2,528,512]{2,1,0:T(8,128)(2,1)S(1)} %span_sums.6), channel_id=1, source_target_pairs={{0,16},{8,24},{16,0},{24,8},{1,17},{9,25},{17,1},{25,9},{2,18},{10... | collective-permute-start | bytes 3244040 | tf_op jit(solution)/shard_map/ppermute | solution.py:1038
  183.6 3.9 %collective-permute-start.40 = (f32[16,512]{1,0:T(8,128)S(1)}, f32[16,512]{1,0:T(8,128)S(1)}, u32[]{:S(2)}, u32[]{:S(2)}) collective-permute-start(f32[16,512]{1,0:T(8,128)S(1)} %add.201), channel_id=1, source_target_pairs={{0,2},{1,3},{2,0},{3,1},{4,6},{5,7},{6,4},{7,5},{8,10},{9,11},{10,... | collective-permute-start | bytes 98312 | tf_op jit(solution)/shard_map/ppermute | solution.py:1050
  187.6 10.0 %collective-permute-start.41 = (f32[16,512]{1,0:T(8,128)S(1)}, f32[16,512]{1,0:T(8,128)S(1)}, u32[]{:S(2)}, u32[]{:S(2)}) collective-permute-start(f32[16,512]{1,0:T(8,128)S(1)} %add.202), channel_id=1, source_target_pairs={{0,4},{1,5},{2,6},{3,7},{4,0},{5,1},{6,2},{7,3},{8,12},{9,13},{10,... | collective-permute-start | bytes 98312 | tf_op jit(solution)/shard_map/ppermute | solution.py:1050
  206.2 9.2 %collective-permute-start.43 = (bf16[256,512]{1,0:T(8,128)(2,1)S(1)}, bf16[256,512]{1,0:T(8,128)(2,1)S(1)}, u32[]{:S(2)}, u32[]{:S(2)}) collective-permute-start(bf16[256,512]{1,0:T(8,128)(2,1)S(1)} %get-tuple-element.200), channel_id=1, source_target_pairs={{0,16},{8,24},{16,0},{24,8},{1,17},{9,25},{17,1},{25,9},{2,18},{10... | collective-permute-start | bytes 786440 | tf_op jit(solution)/shard_map/ppermute | solution.py:1038
  207.0 15.5 %collective-permute-start.54 = (bf16[272,512]{1,0:T(8,128)(2,1)S(1)}, bf16[272,512]{1,0:T(8,128)(2,1)S(1)}, u32[]{:S(2)}, u32[]{:S(2)}) collective-permute-start(bf16[272,512]{1,0:T(8,128)(2,1)S(1)} %get-tuple-element.219), channel_id=1, source_target_pairs={{0,16},{8,24},{16,0},{24,8},{1,17},{9,25},{17,1},{25,9},{2,18},{10... | collective-permute-start | bytes 835592 | tf_op jit(solution)/shard_map/ppermute | solution.py:1038
  209.4 9.3 %collective-permute-start.42 = (bf16[256,512]{1,0:T(8,128)(2,1)S(1)}, bf16[256,512]{1,0:T(8,128)(2,1)S(1)}, u32[]{:S(2)}, u32[]{:S(2)}) collective-permute-start(bf16[256,512]{1,0:T(8,128)(2,1)S(1)} %get-tuple-element.242), channel_id=1, source_target_pairs={{0,1},{1,0},{2,3},{3,2},{4,5},{5,4},{6,7},{7,6},{8,9},{9,8},{10,11... | collective-permute-start | bytes 786440 | tf_op jit(solution)/shard_map/ppermute | solution.py:1034
  211.9 12.7 %collective-permute-start.53 = (bf16[272,512]{1,0:T(8,128)(2,1)S(1)}, bf16[272,512]{1,0:T(8,128)(2,1)S(1)}, u32[]{:S(2)}, u32[]{:S(2)}) collective-permute-start(bf16[272,512]{1,0:T(8,128)(2,1)S(1)} %get-tuple-element.246), channel_id=1, source_target_pairs={{0,1},{1,0},{2,3},{3,2},{4,5},{5,4},{6,7},{7,6},{8,9},{9,8},{10,11... | collective-permute-start | bytes 835592 | tf_op jit(solution)/shard_map/ppermute | solution.py:1034
  218.7 11.6 %collective-permute-start.44 = (bf16[256,512]{1,0:T(8,128)(2,1)S(1)}, bf16[256,512]{1,0:T(8,128)(2,1)S(1)}, u32[]{:S(2)}, u32[]{:S(2)}) collective-permute-start(bf16[256,512]{1,0:T(8,128)(2,1)S(1)} %get-tuple-element.201), channel_id=1, source_target_pairs={{0,1},{1,0},{2,3},{3,2},{4,5},{5,4},{6,7},{7,6},{8,9},{9,8},{10,11... | collective-permute-start | bytes 786440 | tf_op jit(solution)/shard_map/ppermute | solution.py:1034
  220.0 14.2 %collective-permute-start.45 = (bf16[256,512]{1,0:T(8,128)(2,1)S(1)}, bf16[256,512]{1,0:T(8,128)(2,1)S(1)}, u32[]{:S(2)}, u32[]{:S(2)}) collective-permute-start(bf16[256,512]{1,0:T(8,128)(2,1)S(1)} %get-tuple-element.203), channel_id=1, source_target_pairs={{0,16},{8,24},{16,0},{24,8},{1,17},{9,25},{17,1},{25,9},{2,18},{10... | collective-permute-start | bytes 786440 | tf_op jit(solution)/shard_map/ppermute | solution.py:1038
  220.4 14.6 %collective-permute-start.50 = (bf16[256,512]{1,0:T(8,128)(2,1)S(1)}, bf16[256,512]{1,0:T(8,128)(2,1)S(1)}, u32[]{:S(2)}, u32[]{:S(2)}) collective-permute-start(bf16[256,512]{1,0:T(8,128)(2,1)S(1)} %add_convert_fusion.5), channel_id=1, source_target_pairs={{0,2},{1,3},{2,4},{3,5},{4,6},{5,7},{6,0},{7,1},{8,10},{9,11},{10,... | collective-permute-start | bytes 786440 | tf_op jit(solution)/shard_map/ppermute | solution.py:1046
  224.7 11.6 %collective-permute-start.55 = (bf16[272,512]{1,0:T(8,128)(2,1)S(1)}, bf16[272,512]{1,0:T(8,128)(2,1)S(1)}, u32[]{:S(2)}, u32[]{:S(2)}) collective-permute-start(bf16[272,512]{1,0:T(8,128)(2,1)S(1)} %get-tuple-element.220), channel_id=1, source_target_pairs={{0,1},{1,0},{2,3},{3,2},{4,5},{5,4},{6,7},{7,6},{8,9},{9,8},{10,11... | collective-permute-start | bytes 835592 | tf_op jit(solution)/shard_map/ppermute | solution.py:1034
  226.0 11.1 %collective-permute-start.56 = (bf16[272,512]{1,0:T(8,128)(2,1)S(1)}, bf16[272,512]{1,0:T(8,128)(2,1)S(1)}, u32[]{:S(2)}, u32[]{:S(2)}) collective-permute-start(bf16[272,512]{1,0:T(8,128)(2,1)S(1)} %get-tuple-element.222), channel_id=1, source_target_pairs={{0,16},{8,24},{16,0},{24,8},{1,17},{9,25},{17,1},{25,9},{2,18},{10... | collective-permute-start | bytes 835592 | tf_op jit(solution)/shard_map/ppermute | solution.py:1038
  230.3 11.3 %collective-permute-start.61 = (bf16[272,512]{1,0:T(8,128)(2,1)S(1)}, bf16[272,512]{1,0:T(8,128)(2,1)S(1)}, u32[]{:S(2)}, u32[]{:S(2)}) collective-permute-start(bf16[272,512]{1,0:T(8,128)(2,1)S(1)} %add_convert_fusion.2), channel_id=1, source_target_pairs={{0,2},{1,3},{2,4},{3,5},{4,6},{5,7},{6,0},{7,1},{8,10},{9,11},{10,... | collective-permute-start | bytes 835592 | tf_op jit(solution)/shard_map/ppermute | solution.py:1046
  234.1 9.4 %collective-permute-start.46 = (bf16[256,512]{1,0:T(8,128)(2,1)S(1)}, bf16[256,512]{1,0:T(8,128)(2,1)}, u32[]{:S(2)}, u32[]{:S(2)}) collective-permute-start(bf16[256,512]{1,0:T(8,128)(2,1)S(1)} %get-tuple-element.204), channel_id=1, source_target_pairs={{0,1},{1,0},{2,3},{3,2},{4,5},{5,4},{6,7},{7,6},{8,9},{9,8},{10,11... | collective-permute-start | bytes 786440 | tf_op jit(solution)/shard_map/ppermute | solution.py:1034
  235.8 11.1 %collective-permute-start.51 = (bf16[256,512]{1,0:T(8,128)(2,1)}, bf16[256,512]{1,0:T(8,128)(2,1)}, u32[]{:S(2)}, u32[]{:S(2)}) collective-permute-start(bf16[256,512]{1,0:T(8,128)(2,1)} %add_convert_fusion.4), channel_id=1, source_target_pairs={{0,2},{1,3},{2,4},{3,5},{4,6},{5,7},{6,0},{7,1},{8,10},{9,11},{10,... | collective-permute-start | bytes 786440 | tf_op jit(solution)/shard_map/ppermute | solution.py:1046
  236.3 9.4 %collective-permute-start.47 = (bf16[256,512]{1,0:T(8,128)(2,1)}, bf16[256,512]{1,0:T(8,128)(2,1)}, u32[]{:S(2)}, u32[]{:S(2)}) collective-permute-start(bf16[256,512]{1,0:T(8,128)(2,1)} %get-tuple-element.207), channel_id=1, source_target_pairs={{0,16},{8,24},{16,0},{24,8},{1,17},{9,25},{17,1},{25,9},{2,18},{10... | collective-permute-start | bytes 786440 | tf_op jit(solution)/shard_map/ppermute | solution.py:1038
  237.0 11.9 %collective-permute-start.57 = (bf16[272,512]{1,0:T(8,128)(2,1)}, bf16[272,512]{1,0:T(8,128)(2,1)S(1)}, u32[]{:S(2)}, u32[]{:S(2)}) collective-permute-start(bf16[272,512]{1,0:T(8,128)(2,1)} %get-tuple-element.223), channel_id=1, source_target_pairs={{0,1},{1,0},{2,3},{3,2},{4,5},{5,4},{6,7},{7,6},{8,9},{9,8},{10,11... | collective-permute-start | bytes 835592 | tf_op jit(solution)/shard_map/ppermute | solution.py:1034
  241.7 12.2 %collective-permute-start.62 = (bf16[272,512]{1,0:T(8,128)(2,1)S(1)}, bf16[272,512]{1,0:T(8,128)(2,1)S(1)}, u32[]{:S(2)}, u32[]{:S(2)}) collective-permute-start(bf16[272,512]{1,0:T(8,128)(2,1)S(1)} %add_convert_fusion.1), channel_id=1, source_target_pairs={{0,2},{1,3},{2,4},{3,5},{4,6},{5,7},{6,0},{7,1},{8,10},{9,11},{10,... | collective-permute-start | bytes 835592 | tf_op jit(solution)/shard_map/ppermute | solution.py:1046
  243.6 9.6 %collective-permute-start.58 = (bf16[272,512]{1,0:T(8,128)(2,1)S(1)}, bf16[272,512]{1,0:T(8,128)(2,1)S(1)}, u32[]{:S(2)}, u32[]{:S(2)}) collective-permute-start(bf16[272,512]{1,0:T(8,128)(2,1)S(1)} %get-tuple-element.225), channel_id=1, source_target_pairs={{0,16},{8,24},{16,0},{24,8},{1,17},{9,25},{17,1},{25,9},{2,18},{10... | collective-permute-start | bytes 835592 | tf_op jit(solution)/shard_map/ppermute | solution.py:1038
  245.7 8.7 %collective-permute-start.48 = (bf16[256,512]{1,0:T(8,128)(2,1)S(1)}, bf16[256,512]{1,0:T(8,128)(2,1)S(1)}, u32[]{:S(2)}, u32[]{:S(2)}) collective-permute-start(bf16[256,512]{1,0:T(8,128)(2,1)S(1)} %copy-done.14), channel_id=1, source_target_pairs={{0,1},{1,0},{2,3},{3,2},{4,5},{5,4},{6,7},{7,6},{8,9},{9,8},{10,11... | collective-permute-start | bytes 786440 | tf_op jit(solution)/shard_map/ppermute | solution.py:1034
  247.0 10.0 %collective-permute-start.49 = (bf16[256,512]{1,0:T(8,128)(2,1)}, bf16[256,512]{1,0:T(8,128)(2,1)S(1)}, u32[]{:S(2)}, u32[]{:S(2)}) collective-permute-start(bf16[256,512]{1,0:T(8,128)(2,1)} %get-tuple-element.210), channel_id=1, source_target_pairs={{0,16},{8,24},{16,0},{24,8},{1,17},{9,25},{17,1},{25,9},{2,18},{10... | collective-permute-start | bytes 786440 | tf_op jit(solution)/shard_map/ppermute | solution.py:1038
  248.9 9.9 %collective-permute-start.52 = (bf16[256,512]{1,0:T(8,128)(2,1)S(1)}, bf16[256,512]{1,0:T(8,128)(2,1)S(1)}, u32[]{:S(2)}, u32[]{:S(2)}) collective-permute-start(bf16[256,512]{1,0:T(8,128)(2,1)S(1)} %add_convert_fusion.3), channel_id=1, source_target_pairs={{0,2},{1,3},{2,4},{3,5},{4,6},{5,7},{6,0},{7,1},{8,10},{9,11},{10,... | collective-permute-start | bytes 786440 | tf_op jit(solution)/shard_map/ppermute | solution.py:1046
  253.2 6.5 %collective-permute-start.59 = (bf16[272,512]{1,0:T(8,128)(2,1)S(1)}, bf16[272,512]{1,0:T(8,128)(2,1)S(1)}, u32[]{:S(2)}, u32[]{:S(2)}) collective-permute-start(bf16[272,512]{1,0:T(8,128)(2,1)S(1)} %copy-done.12), channel_id=1, source_target_pairs={{0,1},{1,0},{2,3},{3,2},{4,5},{5,4},{6,7},{7,6},{8,9},{9,8},{10,11... | collective-permute-start | bytes 835592 | tf_op jit(solution)/shard_map/ppermute | solution.py:1034
  254.0 6.5 %collective-permute-start.60 = (bf16[272,512]{1,0:T(8,128)(2,1)S(1)}, bf16[272,512]{1,0:T(8,128)(2,1)S(1)}, u32[]{:S(2)}, u32[]{:S(2)}) collective-permute-start(bf16[272,512]{1,0:T(8,128)(2,1)S(1)} %get-tuple-element.228), channel_id=1, source_target_pairs={{0,16},{8,24},{16,0},{24,8},{1,17},{9,25},{17,1},{25,9},{2,18},{10... | collective-permute-start | bytes 835592 | tf_op jit(solution)/shard_map/ppermute | solution.py:1038
  254.4 8.4 %collective-permute-start.63 = (bf16[272,512]{1,0:T(8,128)(2,1)S(1)}, bf16[272,512]{1,0:T(8,128)(2,1)S(1)}, u32[]{:S(2)}, u32[]{:S(2)}) collective-permute-start(bf16[272,512]{1,0:T(8,128)(2,1)S(1)} %add_convert_fusion), channel_id=1, source_target_pairs={{0,2},{1,3},{2,4},{3,5},{4,6},{5,7},{6,0},{7,1},{8,10},{9,11},{10,... | collective-permute-start | bytes 835592 | tf_op jit(solution)/shard_map/ppermute | solution.py:1046
  272.1 3.6 %collective-permute-start.65 = (f32[8,128]{1,0:T(8,128)S(1)}, f32[8,128]{1,0:T(8,128)S(1)}, u32[]{:S(2)}, u32[]{:S(2)}) collective-permute-start(f32[8,128]{1,0:T(8,128)S(1)} %add.237), channel_id=1, source_target_pairs={{0,1},{1,0},{2,3},{3,2},{4,5},{5,4},{6,7},{7,6},{8,9},{9,8},{10,11... | collective-permute-start | bytes 12296 | tf_op jit(solution)/shard_map/ppermute | solution.py:1034
  275.7 3.6 %collective-permute-start.66 = (f32[8,128]{1,0:T(8,128)S(1)}, f32[8,128]{1,0:T(8,128)S(1)}, u32[]{:S(2)}, u32[]{:S(2)}) collective-permute-start(f32[8,128]{1,0:T(8,128)S(1)} %add.238), channel_id=1, source_target_pairs={{0,16},{8,24},{16,0},{24,8},{1,17},{9,25},{17,1},{25,9},{2,18},{10... | collective-permute-start | bytes 12296 | tf_op jit(solution)/shard_map/ppermute | solution.py:1038
  282.9 4.5 %collective-permute-start.68 = (f32[8,128]{1,0:T(8,128)S(1)}, f32[8,128]{1,0:T(8,128)S(1)}, u32[]{:S(2)}, u32[]{:S(2)}) collective-permute-start(f32[8,128]{1,0:T(8,128)S(1)} %add.240), channel_id=1, source_target_pairs={{0,4},{1,5},{2,6},{3,7},{4,0},{5,1},{6,2},{7,3},{8,12},{9,13},{10,... | collective-permute-start | bytes 12296 | tf_op jit(solution)/shard_map/ppermute | solution.py:1050
  (49 other events, 735.0 us)
where the time goes:
time: 294 us; the launch traced here: 293 us
  waiting for transfers between devices  122 us (41%)
  Pallas kernels  81.5 us (28%)
  starting transfers between devices  53.4 us (18%)
  local copies, waits for them, and re-layouts  19.9 us (7%)
  other arithmetic  14 us (5%)
    pallas_call x7, Pallas kernels, call(): pl.pallas_call(kernel, name=name, in_specs=[space for space, _ in ins], o...  72.7 us
    ppermute x17, waiting for transfers between devices, over_y(): return lax.ppermute(value, 'dp', [(i, i ^ 2) for i in range(4)])  53.8 us
    ppermute x17, waiting for transfers between devices, over_x(): return lax.ppermute(value, 'fsdp', [(i, i ^ 1) for i in range(8)])  26.3 us
    ppermute x9, waiting for transfers between devices, round_z(): return lax.ppermute(value, 'fsdp', [(i, (i + 2) % 8) for i in range(8)])  22.1 us
    ppermute x17, starting transfers between devices, over_y(): return lax.ppermute(value, 'dp', [(i, i ^ 2) for i in range(4)])  20 us
    ppermute x17, starting transfers between devices, over_x(): return lax.ppermute(value, 'fsdp', [(i, i ^ 1) for i in range(8)])  17.9 us
    unnamed x89, local copies, waits for them, and re-layouts  13.4 us
    ppermute x4, waiting for transfers between devices, over_z(): return lax.ppermute(value, 'fsdp', [(i, i ^ 2 * step) for i in range(8)])  11 us
  transfers between devices with their start and end apart: 69, of which 38 were waited for; matrix products, arithmetic and copies ran while one was open for 5% of the time, Pallas kernels for 10%

commit v1 on v0

--- a/solution.py
+++ b/solution.py
@@ -314,7 +314,7 @@
         for lane in range(4):
             target[rows, lane * 128 : lane * 128 + 128] = low(stage[lane, rows, :])
 
-    each_loop(wide, lower)
+    each(wide, lower)
 
 
 def weight_rows(left, grads, count, left_t, target):
@@ -1092,7 +1092,7 @@
     far_own = [over_core(each_one) for each_one in own[:2]] + [over_core(after(each_one, *late_ones)) for each_one in own[2:]]
     far = [far_own]
     for way in (by_x, by_y):
-        far.append([over_core(way[0])] + [over_core(after(way[at], *late_ones)) for at in (1, 2)])
+        far.append([over_core(way[0]), over_core(way[1]), over_core(after(way[2], *late_ones))])
         far[-1] += [over_core(way[at]) for at in (3, 4, 5)]
     return own + by_x + by_y + far[0] + far[1] + far[2]
 
@@ -1107,9 +1107,13 @@
 SIDES = (slice(0, HALF), slice(HALF, SPAN))
 
 
-def span_sums(coords, own_half, x, places, low_kept, low_got, high_kept, high_got, sides=None):
+HBM = pl.BlockSpec(memory_space=pltpu.HBM)
+
+
+def span_sums(coords, own_half, x, places, low_kept, low_got, high_kept, high_got, sides):
     count = len(places)
-    pieces = [(at, rows) for at in range(count) for rows in sides or ()]
+    together = sides if isinstance(sides, int) else 0
+    pieces = [(at, rows) for at in range(count) for rows in (() if together else sides)]
 
     def kernel(coords, low_kept, low_got, high_kept, high_got, *refs):
         outs, (kept, got, total, sems, out_sems) = refs[:-5], refs[-5:]
@@ -1132,8 +1136,9 @@
                 total[at, rows] = low(kept[at, rows].astype(F32) + got[at, rows].astype(F32))
 
             each_loop(11, add)
-            if sides is None:
-                copies.append(pltpu.make_async_copy(total.at[at], outs[0].at[at], out_sems.at[at]))
+            if together:
+                out = outs[at // together].at[at % together]
+                copies.append(pltpu.make_async_copy(total.at[at], out, out_sems.at[at]))
                 copies[-1].start()
             for which, (mine, rows) in enumerate(pieces):
                 if mine == at:
@@ -1143,12 +1148,15 @@
             copy.wait()
 
     spans = ((count, SPAN, ROW), BF16)
-    arrays = [(ANY, each_one) for each_one in (low_kept, low_got, high_kept, high_got)]
-    outs = [(ANY, ((rows.stop - rows.start, ROW), BF16)) for _, rows in pieces] or [(ANY, spans)]
+    arrays = [(HBM, low_kept), (ANY, low_got), (HBM, high_kept), (ANY, high_got)]
+    if together:
+        outs = [(ANY, ((together, SPAN, ROW), BF16))] * (count // together)
+    else:
+        outs = [(ANY, ((rows.stop - rows.start, ROW), BF16)) for _, rows in pieces]
     sums = call(
-        kernel, "span_sums", [(SM, coords)] + arrays, outs, [spans] * 3 + [2 * count, max(count, len(pieces))], 40
+        kernel, "span_sums", [(SM, coords)] + arrays, outs, [spans] * 3 + [2 * count, max(count, len(pieces))], 56
     )
-    return sums[0] if sides is None else [sums[len(sides) * at : len(sides) * (at + 1)] for at in range(count)]
+    return sums if together else [sums[len(sides) * at : len(sides) * (at + 1)] for at in range(count)]
 
 
 def late_rows(late, above, below):
@@ -1185,24 +1193,23 @@
     high_got = [over_core(state["high_near"]), over_core(state["high_far"])]
     low_far = over_core(back["low_far"])
 
-    def chip_sum(own_half, x, places, sides=None):
+    def chip_sum(own_half, x, places, sides):
         got = (low_far if x else low_near, high_got[x])
         return span_sums(coords, own_half, x, places, low_kept, got[0], high_kept, got[1], sides)
 
-    late = back["late"]
-    late = late + over_x(late)
-    late = late + over_y(late)
-    for_x, for_y = chip_sum(False, 1, (2, 3)), chip_sum(False, 1, (0, 1))
-    for_x, for_y, late = lax.optimization_barrier((for_x, for_y, late))
+    for_y, for_x = chip_sum(False, 1, range(4), 2)
     from_x, from_y = over_x(for_x), over_y(for_y)
     low_near = over_core(after(back["low_near"], for_x, for_y))
+    to_x, to_y, mine = [
+        chip_sum(own_half, x, range(4), SIDES) for own_half, x in ((True, 1), (False, 0), (True, 0))
+    ]
+    late = after(back["late"], mine[3][1], to_x[3][1], to_y[3][1])
     late = late + over_core(late)
     late = late + over_z(late, 1)
     late = late + over_z(late, 2)
-    to_x, to_y, mine = [
-        chip_sum(own_half, x, range(4), SIDES) for own_half, x in ((True, 1), (False, 0), (True, 0))
-    ]
     from_x, from_y, to_x, to_y, mine, late = lax.optimization_barrier((from_x, from_y, to_x, to_y, mine, late))
+    late = late + over_x(late)
+    late = late + over_y(late)
     running = [None, None]
     before = [(), ()]
     for at in range(4):

time: 294 us -> 286 us (0.973)
  local copies, waits for them, and re-layouts: 19.9 us -> 9.33 us
  waiting for transfers between devices: 122 us -> 129 us
  other arithmetic: 14 us -> 9.4 us
    unnamed x89 -> x107, local copies, waits for them, and re-layouts: 13.4 us -> 4.83 us
    ppermute x9, waiting for transfers between devices: 22.1 us -> 26.6 us  [round_z(): return lax.ppermute(value, 'fsdp', [(i, (i + 2) % 8) for i in range(8)])]
    convert_element_type x11, other arithmetic: 9.38 us -> 5.45 us  [low(): return values.astype(BF16)]
    pallas_call x7 -> x6, Pallas kernels: 72.7 us -> 74.2 us  [call(): pl.pallas_call(kernel, name=name, in_specs=[space for space, _ in ins], o...]
  transfers between devices with their start and end apart: 69 -> 69, of which waited for: 38 -> 35; matrix products, arithmetic and copies ran while one was open for 5% -> 3% of each run, Pallas kernels for 10% -> 11%
where the time goes in v1:
time: 286 us; the launch traced here: 285 us
  waiting for transfers between devices  129 us (45%)
  Pallas kernels  83.1 us (29%)
  starting transfers between devices  52.2 us (18%)
  other arithmetic  9.4 us (3%)
  local copies, waits for them, and re-layouts  9.33 us (3%)
    pallas_call x6, Pallas kernels, call(): pl.pallas_call(kernel, name=name, in_specs=[space for space, _ in ins], o...  74.2 us
    ppermute x17, waiting for transfers between devices, over_y(): return lax.ppermute(value, 'dp', [(i, i ^ 2) for i in range(4)])  52.6 us
    ppermute x17, waiting for transfers between devices, over_x(): return lax.ppermute(value, 'fsdp', [(i, i ^ 1) for i in range(8)])  26.9 us
    ppermute x9, waiting for transfers between devices, round_z(): return lax.ppermute(value, 'fsdp', [(i, (i + 2) % 8) for i in range(8)])  26.6 us
    ppermute x17, starting transfers between devices, over_y(): return lax.ppermute(value, 'dp', [(i, i ^ 2) for i in range(4)])  19.1 us
    ppermute x17, starting transfers between devices, over_x(): return lax.ppermute(value, 'fsdp', [(i, i ^ 1) for i in range(8)])  18.1 us
    ppermute x4, waiting for transfers between devices, over_z(): return lax.ppermute(value, 'fsdp', [(i, i ^ 2 * step) for i in range(8)])  12.5 us
    ppermute x22, waiting for transfers between devices, over_core(): return lax.ppermute(value, 'dp', [(i, i ^ 1) for i in range(4)])  10.4 us
  transfers between devices with their start and end apart: 69, of which 35 were waited for; matrix products, arithmetic and copies ran while one was open for 3% of the time, Pallas kernels for 11%

profile of v1, /device:TPU:0, one launch (start us, length us, event | category | flops | bytes accessed | tf_op | source)
XLA Modules:
  0.0 285.3 jit_solution(14210970159608631361)
XLA Ops:
  0.7 1.3 convert_element_type.246
  2.8 3.0 %collective-permute-start.2 = (bf16[528,512]{1,0:T(8,128)(2,1)S(1)}, bf16[528,512]{1,0:T(8,128)(2,1)S(1)}, u32[]{:S(2)}, u32[]{:S(2)}) collective-permute-start(bf16[528,512]{1,0:T(8,128)(2,1)S(1)} %reshape.49.refs_4_), channel_id=1, source_target_pairs={{0,16},{8,24},{16,0},{24,8},{1,17},{9,25},{17,1},{25,9},{2,18},{10... | collective-permute-start | bytes 1622024 | tf_op jit(solution)/shard_map/ppermute | solution.py:1038
  5.8 1.5 collective-permute-start.1
  7.3 1.6 collective-permute-start
  8.9 9.2 %collective-permute-done.2.refs_14_ = bf16[528,512]{1,0:T(8,128)(2,1)S(1)} collective-permute-done((bf16[528,512]{1,0:T(8,128)(2,1)S(1)}, bf16[528,512]{1,0:T(8,128)(2,1)S(1)}, u32[]{:S(2)}, u32[]{:S(2)}) %collective-permute-start.2) | collective-permute-done | bytes 540704 | tf_op jit(solution)/shard_map/ppermute | solution.py:1038
  18.1 1.5 collective-permute-done.1.refs_8_
  19.5 3.1 %collective-permute-done.refs_5_ = bf16[528,512]{1,0:T(8,128)(2,1)S(1)} collective-permute-done((bf16[528,512]{1,0:T(8,128)(2,1)S(1)}, bf16[528,512]{1,0:T(8,128)(2,1)S(1)}, u32[]{:S(2)}, u32[]{:S(2)}) %collective-permute-start) | collective-permute-done | bytes 540704 | tf_op jit(solution)/shard_map/ppermute | solution.py:1046
  23.7 11.5 %collective-permute-done.5.refs_15_ = bf16[528,512]{1,0:T(8,128)(2,1)S(1)} collective-permute-done((bf16[528,512]{1,0:T(8,128)(2,1)S(1)}, bf16[528,512]{1,0:T(8,128)(2,1)S(1)}, u32[]{:S(2)}, u32[]{:S(2)}) %collective-permute-start.5) | collective-permute-done | bytes 540704 | tf_op jit(solution)/shard_map/ppermute | solution.py:1038
  35.4 2.3 collective-permute-done.3.refs_6_
  37.8 1.3 collective-permute-start.7
  39.2 1.6 collective-permute-start.9
  40.8 10.1 %collective-permute-done.6.refs_7_ = bf16[528,512]{1,0:T(8,128)(2,1)S(1)} collective-permute-done((bf16[528,512]{1,0:T(8,128)(2,1)S(1)}, bf16[528,512]{1,0:T(8,128)(2,1)S(1)}, u32[]{:S(2)}, u32[]{:S(2)}) %collective-permute-start.6) | collective-permute-done | bytes 540704 | tf_op jit(solution)/shard_map/ppermute | solution.py:1046
  52.1 6.6 %collective-permute-done.7.refs_10_ = bf16[784,512]{1,0:T(8,128)(2,1)S(1)} collective-permute-done((bf16[784,512]{1,0:T(8,128)(2,1)S(1)}, bf16[784,512]{1,0:T(8,128)(2,1)S(1)}, u32[]{:S(2)}, u32[]{:S(2)}) %collective-permute-start.7) | collective-permute-done | bytes 802848 | tf_op jit(solution)/shard_map/ppermute | solution.py:1034
  58.7 1.3 collective-permute-start.11
  60.8 1.3 collective-permute-start.10
  62.2 17.3 %collective-permute-done.13.refs_18_ = bf16[272,512]{1,0:T(8,128)(2,1)S(1)} collective-permute-done((bf16[272,512]{1,0:T(8,128)(2,1)S(1)}, bf16[272,512]{1,0:T(8,128)(2,1)S(1)}, u32[]{:S(2)}, u32[]{:S(2)}) %collective-permute-start.13) | collective-permute-done | bytes 278560 | tf_op jit(solution)/shard_map/ppermute | solution.py:1038
  80.3 1.6 collective-permute-start.14
  84.1 5.2 %collective-permute-done.14.refs_19_ = bf16[272,512]{1,0:T(8,128)(2,1)S(1)} collective-permute-done((bf16[272,512]{1,0:T(8,128)(2,1)S(1)}, bf16[272,512]{1,0:T(8,128)(2,1)S(1)}, u32[]{:S(2)}, u32[]{:S(2)}) %collective-permute-start.14) | collective-permute-done | bytes 278560 | tf_op jit(solution)/shard_map/ppermute | solution.py:1038
  89.4 1.9 collective-permute-done.12.refs_13_
  96.2 2.2 collective-permute-done.18.refs_23_
  98.5 43.2 %forward.1 = (bf16[160,512]{1,0:T(8,128)(2,1)}, f32[8,512]{1,0:T(8,128)}, f32[176,512]{1,0:T(8,128)}, bf16[8,528,512]{2,1,0:T(8,128)(2,1)}, bf16[4,528,512]{2,1,...) custom-call(s32[4]{0:T(128)} %pad_add_fusion.refs_0_.coords, ...), custom_call_target="tpu_custom_call" | custom-call | tf_op jit(solution)/shard_map/forward/pallas_call | solution.py:972
  142.0 14.7 %backward.1 = (bf16[160,512]{1,0:T(8,128)(2,1)}, f32[16,512]{1,0:T(8,128)}, bf16[8,528,512]{2,1,0:T(8,128)(2,1)}, bf16[4,528,512]{2,1,0:T(8,128)(2,1)}, bf16[4,528,512]{2,1,0:T(8,128)(2,1)}) custom-call(s32[4]{0:T(128)} %pad_add_fusion.refs_0_.coords, bf16[160,512]{1,0:T(8,128)(2,1)} %bitcast.47, ...), custom_call_target="tpu_custom_call", output_to_operand_aliasing={{2}: (18, {}), {3}: (19, {}), {4}: (20, {})} | custom-call | tf_op jit(solution)/shard_map/backward/pallas_call | solution.py:972
  157.3 4.7 %collective-permute-done.31.low_got = bf16[4,528,512]{2,1,0:T(8,128)(2,1)} collective-permute-done((bf16[4,528,512]{2,1,0:T(8,128)(2,1)}, bf16[4,528,512]{2,1,0:T(8,128)(2,1)}, u32[]{:S(2)}, u32[]{:S(2)}) %collective-permute-start.31) | collective-permute-done | bytes 2162720 | tf_op jit(solution)/shard_map/ppermute | solution.py:1042
  162.0 4.0 %span_sums.4 = (bf16[2,528,512]{2,1,0:T(8,128)(2,1)}, bf16[2,528,512]{2,1,0:T(8,128)(2,1)}) custom-call(s32[4]{0:T(128)} %pad_add_fusion.refs_0_.coords, bf16[8,528,512]{2,1,0:T(8,128)(2,1)} %get-tuple-element.155.low_kept, bf16[4,528,512]{2,1,0:T(8,128)(2,1)} %collective-permute-done.31.low_got, bf16[8,528,512]{2,1,0:T(8,128)(2,1)} %get-tuple-element.157.high_kept, ...), custom_call_target="tpu_custom_call" | custom-call | tf_op jit(solution)/shard_map/span_sums/pallas_call | solution.py:972
  166.4 2.4 collective-permute-start.33
  168.8 2.9 %collective-permute-start.34 = (bf16[2,528,512]{2,1,0:T(8,128)(2,1)}, bf16[2,528,512]{2,1,0:T(8,128)(2,1)}, u32[]{:S(2)}, u32[]{:S(2)}) collective-permute-start(bf16[2,528,512]{2,1,0:T(8,128)(2,1)} %get-tuple-element.160), channel_id=1, source_target_pairs={{0,16},{8,24},{16,0},{24,8},{1,17},{9,25},{17,1},{25,9},{2,18},{10... | collective-permute-start | bytes 3244040 | tf_op jit(solution)/shard_map/ppermute | solution.py:1038
  171.7 4.0 %span_sums.5 = (bf16[256,512]{1,0:T(8,128)(2,1)}, bf16[272,512]{1,0:T(8,128)(2,1)}, bf16[256,512]{1,0:T(8,128)(2,1)}, bf16[272,512]{1,0:T(8,128)(2,1)}, bf16[256...) custom-call(s32[4]{0:T(128)} %pad_add_fusion.refs_0_.coords, ...), custom_call_target="tpu_custom_call" | custom-call | tf_op jit(solution)/shard_map/span_sums/pallas_call | solution.py:972
  175.8 1.4 copy-done.1
  177.1 1.3 copy-done.2
  178.4 4.0 %span_sums.7 = (bf16[256,512]{1,0:T(8,128)(2,1)}, bf16[272,512]{1,0:T(8,128)(2,1)}, bf16[256,512]{1,0:T(8,128)(2,1)}, bf16[272,512]{1,0:T(8,128)(2,1)}, bf16[256...) custom-call(s32[4]{0:T(128)} %pad_add_fusion.refs_0_.coords, ...), custom_call_target="tpu_custom_call" | custom-call | tf_op jit(solution)/shard_map/span_sums/pallas_call | solution.py:972
  182.5 4.4 %span_sums.6 = (bf16[256,512]{1,0:T(8,128)(2,1)}, bf16[272,512]{1,0:T(8,128)(2,1)}, bf16[256,512]{1,0:T(8,128)(2,1)}, bf16[272,512]{1,0:T(8,128)(2,1)}, bf16[256...) custom-call(s32[4]{0:T(128)} %pad_add_fusion.refs_0_.coords, ...), custom_call_target="tpu_custom_call" | custom-call | tf_op jit(solution)/shard_map/span_sums/pallas_call | solution.py:972
  186.9 1.2 collective-permute-done.37
  188.2 3.9 %collective-permute-done.38 = f32[16,512]{1,0:T(8,128)S(1)} collective-permute-done((f32[16,512]{1,0:T(8,128)S(1)}, f32[16,512]{1,0:T(8,128)S(1)}, u32[]{:S(2)}, u32[]{:S(2)}) %collective-permute-start.38) | collective-permute-done | bytes 32800 | tf_op jit(solution)/shard_map/ppermute | solution.py:1050
  192.1 2.3 collective-permute-start.39
  194.5 2.4 collective-permute-done.39
  196.9 1.3 collective-permute-start.62
  198.9 1.4 collective-permute-start.52
  200.2 1.2 fusion.8
  202.3 1.2 fusion.4
  203.5 1.3 collective-permute-start.51
  205.0 2.6 collective-permute-done.41
  207.6 3.1 %collective-permute-done.40 = bf16[256,512]{1,0:T(8,128)(2,1)S(1)} collective-permute-done((bf16[256,512]{1,0:T(8,128)(2,1)S(1)}, bf16[256,512]{1,0:T(8,128)(2,1)S(1)}, u32[]{:S(2)}, u32[]{:S(2)}) %collective-permute-start.40) | collective-permute-done | bytes 262176 | tf_op jit(solution)/shard_map/ppermute | solution.py:1034
  213.5 1.5 collective-permute-start.48
  214.9 1.8 collective-permute-done.51
  218.4 3.9 %collective-permute-done.42 = bf16[256,512]{1,0:T(8,128)(2,1)S(1)} collective-permute-done((bf16[256,512]{1,0:T(8,128)(2,1)S(1)}, bf16[256,512]{1,0:T(8,128)(2,1)S(1)}, u32[]{:S(2)}, u32[]{:S(2)}) %collective-permute-start.42) | collective-permute-done | bytes 262176 | tf_op jit(solution)/shard_map/ppermute | solution.py:1034
  222.3 1.3 collective-permute-start.59
  225.9 1.8 collective-permute-done.53
  227.7 1.9 collective-permute-start.49
  229.6 4.1 %collective-permute-done.59 = bf16[272,512]{1,0:T(8,128)(2,1)S(1)} collective-permute-done((bf16[272,512]{1,0:T(8,128)(2,1)S(1)}, bf16[272,512]{1,0:T(8,128)(2,1)S(1)}, u32[]{:S(2)}, u32[]{:S(2)}) %collective-permute-start.59) | collective-permute-done | bytes 278560 | tf_op jit(solution)/shard_map/ppermute | solution.py:1046
  234.6 1.3 collective-permute-start.56
  239.7 3.3 %collective-permute-done.55 = bf16[272,512]{1,0:T(8,128)(2,1)S(1)} collective-permute-done((bf16[272,512]{1,0:T(8,128)(2,1)}, bf16[272,512]{1,0:T(8,128)(2,1)S(1)}, u32[]{:S(2)}, u32[]{:S(2)}) %collective-permute-start.55) | collective-permute-done | bytes 278560 | tf_op jit(solution)/shard_map/ppermute | solution.py:1034
  245.0 1.7 collective-permute-start.58
  247.8 3.4 %collective-permute-done.50 = bf16[256,512]{1,0:T(8,128)(2,1)S(1)} collective-permute-done((bf16[256,512]{1,0:T(8,128)(2,1)S(1)}, bf16[256,512]{1,0:T(8,128)(2,1)S(1)}, u32[]{:S(2)}, u32[]{:S(2)}) %collective-permute-start.50) | collective-permute-done | bytes 262176 | tf_op jit(solution)/shard_map/ppermute | solution.py:1046
  251.6 3.7 %collective-permute-done.61 = bf16[272,512]{1,0:T(8,128)(2,1)S(1)} collective-permute-done((bf16[272,512]{1,0:T(8,128)(2,1)S(1)}, bf16[272,512]{1,0:T(8,128)(2,1)S(1)}, u32[]{:S(2)}, u32[]{:S(2)}) %collective-permute-start.61) | collective-permute-done | bytes 278560 | tf_op jit(solution)/shard_map/ppermute | solution.py:1046
  255.8 1.3 dynamic_slice.11.grad
  257.1 5.3 %update.1 = (f32[256592]{0:T(1024)}, f32[256592]{0:T(1024)}, f32[256592]{0:T(1024)}, f32[8,128]{1,0:T(8,128)}) custom-call(s32[6]{0:T(128)} %pad_add_fusion.1.segments, f32[256592]{0:T(1024)} %params.3, f32[256592]{0:T(1024)} %first.1, f32[256592]{0:T(1024)} %second.1, f32[256592]{0:T(1024)} %dynamic_slice.11.grad), custom_call_target="tpu_custom_call" | custom-call | tf_op jit(solution)/shard_map/update/pallas_call | solution.py:1399
  262.4 1.4 collective-permute-done.64
  265.4 2.7 collective-permute-done.65
  268.6 3.1 %collective-permute-done.66 = f32[8,128]{1,0:T(8,128)S(1)} collective-permute-done((f32[8,128]{1,0:T(8,128)S(1)}, f32[8,128]{1,0:T(8,128)S(1)}, u32[]{:S(2)}, u32[]{:S(2)}) %collective-permute-start.66) | collective-permute-done | bytes 4128 | tf_op jit(solution)/shard_map/ppermute | solution.py:1038
  271.7 3.6 %collective-permute-done.67 = f32[8,128]{1,0:T(8,128)S(1)} collective-permute-done((f32[8,128]{1,0:T(8,128)S(1)}, f32[8,128]{1,0:T(8,128)S(1)}, u32[]{:S(2)}, u32[]{:S(2)}) %collective-permute-start.67) | collective-permute-done | bytes 4128 | tf_op jit(solution)/shard_map/ppermute | solution.py:1050
  275.3 1.2 collective-permute-start.68
  277.2 2.7 collective-permute-done.68
  280.4 3.6 %apply.1 = (f32[256592]{0:T(1024)}, f32[8,128]{1,0:T(8,128)}) custom-call(s32[6]{0:T(128)} %pad_add_fusion.1.segments, f32[8,128]{1,0:T(8,128)} %add.241.sums, f32[256592]{0:T(1024)} %params.3, f32[256592]{0:T(1024)} %get-tuple-element.230.update), custom_call_target="tpu_custom_call" | custom-call | tf_op jit(solution)/shard_map/apply/pallas_call | solution.py:1408
  284.0 1.3 slice_bitcast_fusion
  (234 shorter events, 33.2 us)
Async XLA Ops:
  2.8 15.3 %collective-permute-start.2 = (bf16[528,512]{1,0:T(8,128)(2,1)S(1)}, bf16[528,512]{1,0:T(8,128)(2,1)S(1)}, u32[]{:S(2)}, u32[]{:S(2)}) collective-permute-start(bf16[528,512]{1,0:T(8,128)(2,1)S(1)} %reshape.49.refs_4_), channel_id=1, source_target_pairs={{0,16},{8,24},{16,0},{24,8},{1,17},{9,25},{17,1},{25,9},{2,18},{10... | collective-permute-start | bytes 1622024 | tf_op jit(solution)/shard_map/ppermute | solution.py:1038
  5.8 13.7 %collective-permute-start.1 = (bf16[528,512]{1,0:T(8,128)(2,1)S(1)}, bf16[528,512]{1,0:T(8,128)(2,1)S(1)}, u32[]{:S(2)}, u32[]{:S(2)}) collective-permute-start(bf16[528,512]{1,0:T(8,128)(2,1)S(1)} %reshape.49.refs_4_), channel_id=1, source_target_pairs={{0,1},{1,0},{2,3},{3,2},{4,5},{5,4},{6,7},{7,6},{8,9},{9,8},{10,11... | collective-permute-start | bytes 1622024 | tf_op jit(solution)/shard_map/ppermute | solution.py:1034
  7.3 15.3 %collective-permute-start = (bf16[528,512]{1,0:T(8,128)(2,1)S(1)}, bf16[528,512]{1,0:T(8,128)(2,1)S(1)}, u32[]{:S(2)}, u32[]{:S(2)}) collective-permute-start(bf16[528,512]{1,0:T(8,128)(2,1)S(1)} %reshape.49.refs_4_), channel_id=1, source_target_pairs={{0,2},{1,3},{2,4},{3,5},{4,6},{5,7},{6,0},{7,1},{8,10},{9,11},{10,... | collective-permute-start | bytes 1622024 | tf_op jit(solution)/shard_map/ppermute | solution.py:1046
  22.6 12.6 %collective-permute-start.5 = (bf16[528,512]{1,0:T(8,128)(2,1)S(1)}, bf16[528,512]{1,0:T(8,128)(2,1)S(1)}, u32[]{:S(2)}, u32[]{:S(2)}) collective-permute-start(bf16[528,512]{1,0:T(8,128)(2,1)S(1)} %collective-permute-done.refs_5_), channel_id=1, source_target_pairs={{0,16},{8,24},{16,0},{24,8},{1,17},{9,25},{17,1},{25,9},{2,18},{10... | collective-permute-start | bytes 1622024 | tf_op jit(solution)/shard_map/ppermute | solution.py:1038
  23.1 12.3 %collective-permute-start.4 = (bf16[528,512]{1,0:T(8,128)(2,1)S(1)}, bf16[528,512]{1,0:T(8,128)(2,1)S(1)}, u32[]{:S(2)}, u32[]{:S(2)}) collective-permute-start(bf16[528,512]{1,0:T(8,128)(2,1)S(1)} %collective-permute-done.refs_5_), channel_id=1, source_target_pairs={{0,1},{1,0},{2,3},{3,2},{4,5},{5,4},{6,7},{7,6},{8,9},{9,8},{10,11... | collective-permute-start | bytes 1622024 | tf_op jit(solution)/shard_map/ppermute | solution.py:1034
  23.6 14.1 %collective-permute-start.3 = (bf16[528,512]{1,0:T(8,128)(2,1)S(1)}, bf16[528,512]{1,0:T(8,128)(2,1)S(1)}, u32[]{:S(2)}, u32[]{:S(2)}) collective-permute-start(bf16[528,512]{1,0:T(8,128)(2,1)S(1)} %collective-permute-done.refs_5_), channel_id=1, source_target_pairs={{0,2},{1,3},{2,4},{3,5},{4,6},{5,7},{6,0},{7,1},{8,10},{9,11},{10,... | collective-permute-start | bytes 1622024 | tf_op jit(solution)/shard_map/ppermute | solution.py:1046
  37.7 13.1 %collective-permute-start.6 = (bf16[528,512]{1,0:T(8,128)(2,1)S(1)}, bf16[528,512]{1,0:T(8,128)(2,1)S(1)}, u32[]{:S(2)}, u32[]{:S(2)}) collective-permute-start(bf16[528,512]{1,0:T(8,128)(2,1)S(1)} %collective-permute-done.3.refs_6_), channel_id=1, source_target_pairs={{0,2},{1,3},{2,4},{3,5},{4,6},{5,7},{6,0},{7,1},{8,10},{9,11},{10,... | collective-permute-start | bytes 1622024 | tf_op jit(solution)/shard_map/ppermute | solution.py:1046
  37.8 20.9 %collective-permute-start.7 = (bf16[784,512]{1,0:T(8,128)(2,1)S(1)}, bf16[784,512]{1,0:T(8,128)(2,1)S(1)}, u32[]{:S(2)}, u32[]{:S(2)}) collective-permute-start(bf16[784,512]{1,0:T(8,128)(2,1)S(1)} %pad_maximum_fusion.2), channel_id=1, source_target_pairs={{0,1},{1,0},{2,3},{3,2},{4,5},{5,4},{6,7},{7,6},{8,9},{9,8},{10,11... | collective-permute-start | bytes 2408456 | tf_op jit(solution)/shard_map/ppermute | solution.py:1034
  39.2 20.8 %collective-permute-start.9 = (bf16[800,512]{1,0:T(8,128)(2,1)S(1)}, bf16[800,512]{1,0:T(8,128)(2,1)S(1)}, u32[]{:S(2)}, u32[]{:S(2)}) collective-permute-start(bf16[800,512]{1,0:T(8,128)(2,1)S(1)} %pad_maximum_fusion), channel_id=1, source_target_pairs={{0,16},{8,24},{16,0},{24,8},{1,17},{9,25},{17,1},{25,9},{2,18},{10... | collective-permute-start | bytes 2457608 | tf_op jit(solution)/shard_map/ppermute | solution.py:1038
  40.8 20.1 %collective-permute-start.15 = (bf16[528,512]{1,0:T(8,128)(2,1)S(1)}, bf16[528,512]{1,0:T(8,128)(2,1)S(1)}, u32[]{:S(2)}, u32[]{:S(2)}) collective-permute-start(bf16[528,512]{1,0:T(8,128)(2,1)S(1)} %reshape.49.refs_4_), channel_id=1, source_target_pairs={{0,8},{8,0},{16,24},{24,16},{1,9},{9,1},{17,25},{25,17},{2,10},{10... | collective-permute-start | bytes 1622024 | tf_op jit(solution)/shard_map/ppermute | solution.py:1042
  50.9 29.3 %collective-permute-start.8 = (bf16[784,512]{1,0:T(8,128)(2,1)S(1)}, bf16[784,512]{1,0:T(8,128)(2,1)S(1)}, u32[]{:S(2)}, u32[]{:S(2)}) collective-permute-start(bf16[784,512]{1,0:T(8,128)(2,1)S(1)} %pad_maximum_fusion.3), channel_id=1, source_target_pairs={{0,1},{1,0},{2,3},{3,2},{4,5},{5,4},{6,7},{7,6},{8,9},{9,8},{10,11... | collective-permute-start | bytes 2408456 | tf_op jit(solution)/shard_map/ppermute | solution.py:1034
  52.0 10.2 %collective-permute-start.19 = (bf16[528,512]{1,0:T(8,128)(2,1)S(1)}, bf16[528,512]{1,0:T(8,128)(2,1)S(1)}, u32[]{:S(2)}, u32[]{:S(2)}) collective-permute-start(bf16[528,512]{1,0:T(8,128)(2,1)S(1)} %collective-permute-done.1.refs_8_), channel_id=1, source_target_pairs={{0,8},{8,0},{16,24},{24,16},{1,9},{9,1},{17,25},{25,17},{2,10},{10... | collective-permute-start | bytes 1622024 | tf_op jit(solution)/shard_map/ppermute | solution.py:1042
  58.7 21.6 %collective-permute-start.11 = (bf16[800,512]{1,0:T(8,128)(2,1)S(1)}, bf16[800,512]{1,0:T(8,128)(2,1)}, u32[]{:S(2)}, u32[]{:S(2)}) collective-permute-start(bf16[800,512]{1,0:T(8,128)(2,1)S(1)} %pad_maximum_fusion.1), channel_id=1, source_target_pairs={{0,16},{8,24},{16,0},{24,8},{1,17},{9,25},{17,1},{25,9},{2,18},{10... | collective-permute-start | bytes 2457608 | tf_op jit(solution)/shard_map/ppermute | solution.py:1038
  60.0 19.6 %collective-permute-start.13 = (bf16[272,512]{1,0:T(8,128)(2,1)S(1)}, bf16[272,512]{1,0:T(8,128)(2,1)S(1)}, u32[]{:S(2)}, u32[]{:S(2)}) collective-permute-start(bf16[272,512]{1,0:T(8,128)(2,1)S(1)} %slice.87), channel_id=1, source_target_pairs={{0,16},{8,24},{16,0},{24,8},{1,17},{9,25},{17,1},{25,9},{2,18},{10... | collective-permute-start | bytes 835592 | tf_op jit(solution)/shard_map/ppermute | solution.py:1038
  60.8 18.7 %collective-permute-start.10 = (bf16[256,512]{1,0:T(8,128)(2,1)S(1)}, bf16[256,512]{1,0:T(8,128)(2,1)S(1)}, u32[]{:S(2)}, u32[]{:S(2)}) collective-permute-start(bf16[256,512]{1,0:T(8,128)(2,1)S(1)} %slice.85), channel_id=1, source_target_pairs={{0,1},{1,0},{2,3},{3,2},{4,5},{5,4},{6,7},{7,6},{8,9},{9,8},{10,11... | collective-permute-start | bytes 786440 | tf_op jit(solution)/shard_map/ppermute | solution.py:1034
  62.2 20.7 %collective-permute-start.25 = (bf16[528,512]{1,0:T(8,128)(2,1)S(1)}, bf16[528,512]{1,0:T(8,128)(2,1)S(1)}, u32[]{:S(2)}, u32[]{:S(2)}) collective-permute-start(bf16[528,512]{1,0:T(8,128)(2,1)S(1)} %collective-permute-done.2.refs_14_), channel_id=1, source_target_pairs={{0,8},{8,0},{16,24},{24,16},{1,9},{9,1},{17,25},{25,17},{2,10},{10... | collective-permute-start | bytes 1622024 | tf_op jit(solution)/shard_map/ppermute | solution.py:1042
  79.6 3.9 %collective-permute-start.16 = (bf16[528,512]{1,0:T(8,128)(2,1)S(1)}, bf16[528,512]{1,0:T(8,128)(2,1)S(1)}, u32[]{:S(2)}, u32[]{:S(2)}) collective-permute-start(bf16[528,512]{1,0:T(8,128)(2,1)S(1)} %collective-permute-done.refs_5_), channel_id=1, source_target_pairs={{0,8},{8,0},{16,24},{24,16},{1,9},{9,1},{17,25},{25,17},{2,10},{10... | collective-permute-start | bytes 1622024 | tf_op jit(solution)/shard_map/ppermute | solution.py:1042
  79.6 3.9 %collective-permute-start.20 = (bf16[528,512]{1,0:T(8,128)(2,1)S(1)}, bf16[528,512]{1,0:T(8,128)(2,1)S(1)}, u32[]{:S(2)}, u32[]{:S(2)}) collective-permute-start(bf16[528,512]{1,0:T(8,128)(2,1)S(1)} %collective-permute-done.4.refs_9_), channel_id=1, source_target_pairs={{0,8},{8,0},{16,24},{24,16},{1,9},{9,1},{17,25},{25,17},{2,10},{10... | collective-permute-start | bytes 1622024 | tf_op jit(solution)/shard_map/ppermute | solution.py:1042
  80.2 3.8 %collective-permute-start.26 = (bf16[528,512]{1,0:T(8,128)(2,1)S(1)}, bf16[528,512]{1,0:T(8,128)(2,1)S(1)}, u32[]{:S(2)}, u32[]{:S(2)}) collective-permute-start(bf16[528,512]{1,0:T(8,128)(2,1)S(1)} %collective-permute-done.5.refs_15_), channel_id=1, source_target_pairs={{0,8},{8,0},{16,24},{24,16},{1,9},{9,1},{17,25},{25,17},{2,10},{10... | collective-permute-start | bytes 1622024 | tf_op jit(solution)/shard_map/ppermute | solution.py:1042
  80.3 9.1 %collective-permute-start.14 = (bf16[272,512]{1,0:T(8,128)(2,1)S(1)}, bf16[272,512]{1,0:T(8,128)(2,1)S(1)}, u32[]{:S(2)}, u32[]{:S(2)}) collective-permute-start(bf16[272,512]{1,0:T(8,128)(2,1)S(1)} %slice.88), channel_id=1, source_target_pairs={{0,16},{8,24},{16,0},{24,8},{1,17},{9,25},{17,1},{25,9},{2,18},{10... | collective-permute-start | bytes 835592 | tf_op jit(solution)/shard_map/ppermute | solution.py:1038
  82.9 8.5 %collective-permute-start.12 = (bf16[256,512]{1,0:T(8,128)(2,1)S(1)}, bf16[256,512]{1,0:T(8,128)(2,1)S(1)}, u32[]{:S(2)}, u32[]{:S(2)}) collective-permute-start(bf16[256,512]{1,0:T(8,128)(2,1)S(1)} %slice.86), channel_id=1, source_target_pairs={{0,1},{1,0},{2,3},{3,2},{4,5},{5,4},{6,7},{7,6},{8,9},{9,8},{10,11... | collective-permute-start | bytes 786440 | tf_op jit(solution)/shard_map/ppermute | solution.py:1034
  83.5 8.4 %collective-permute-start.29 = (bf16[272,512]{1,0:T(8,128)(2,1)S(1)}, bf16[272,512]{1,0:T(8,128)(2,1)S(1)}, u32[]{:S(2)}, u32[]{:S(2)}) collective-permute-start(bf16[272,512]{1,0:T(8,128)(2,1)S(1)} %collective-permute-done.13.refs_18_), channel_id=1, source_target_pairs={{0,8},{8,0},{16,24},{24,16},{1,9},{9,1},{17,25},{25,17},{2,10},{10... | collective-permute-start | bytes 835592 | tf_op jit(solution)/shard_map/ppermute | solution.py:1042
  83.5 7.8 %collective-permute-start.23 = (bf16[256,512]{1,0:T(8,128)(2,1)S(1)}, bf16[256,512]{1,0:T(8,128)(2,1)S(1)}, u32[]{:S(2)}, u32[]{:S(2)}) collective-permute-start(bf16[256,512]{1,0:T(8,128)(2,1)S(1)} %collective-permute-done.10.refs_12_), channel_id=1, source_target_pairs={{0,8},{8,0},{16,24},{24,16},{1,9},{9,1},{17,25},{25,17},{2,10},{10... | collective-permute-start | bytes 786440 | tf_op jit(solution)/shard_map/ppermute | solution.py:1042
  84.0 9.4 %collective-permute-start.17 = (bf16[528,512]{1,0:T(8,128)(2,1)S(1)}, bf16[528,512]{1,0:T(8,128)(2,1)S(1)}, u32[]{:S(2)}, u32[]{:S(2)}) collective-permute-start(bf16[528,512]{1,0:T(8,128)(2,1)S(1)} %collective-permute-done.3.refs_6_), channel_id=1, source_target_pairs={{0,8},{8,0},{16,24},{24,16},{1,9},{9,1},{17,25},{25,17},{2,10},{10... | collective-permute-start | bytes 1622024 | tf_op jit(solution)/shard_map/ppermute | solution.py:1042
  89.4 3.6 %collective-permute-start.30 = (bf16[272,512]{1,0:T(8,128)(2,1)S(1)}, bf16[272,512]{1,0:T(8,128)(2,1)S(1)}, u32[]{:S(2)}, u32[]{:S(2)}) collective-permute-start(bf16[272,512]{1,0:T(8,128)(2,1)S(1)} %collective-permute-done.14.refs_19_), channel_id=1, source_target_pairs={{0,8},{8,0},{16,24},{24,16},{1,9},{9,1},{17,25},{25,17},{2,10},{10... | collective-permute-start | bytes 835592 | tf_op jit(solution)/shard_map/ppermute | solution.py:1042
  91.4 7.1 %collective-permute-start.28 = (bf16[800,512]{1,0:T(8,128)(2,1)}, bf16[800,512]{1,0:T(8,128)(2,1)}, u32[]{:S(2)}, u32[]{:S(2)}) collective-permute-start(bf16[800,512]{1,0:T(8,128)(2,1)} %collective-permute-done.11.refs_17_), channel_id=1, source_target_pairs={{0,8},{8,0},{16,24},{24,16},{1,9},{9,1},{17,25},{25,17},{2,10},{10... | collective-permute-start | bytes 2457608 | tf_op jit(solution)/shard_map/ppermute | solution.py:1042
  91.9 6.6 %collective-permute-start.27 = (bf16[800,512]{1,0:T(8,128)(2,1)S(1)}, bf16[800,512]{1,0:T(8,128)(2,1)}, u32[]{:S(2)}, u32[]{:S(2)}) collective-permute-start(bf16[800,512]{1,0:T(8,128)(2,1)S(1)} %collective-permute-done.9.refs_16_), channel_id=1, source_target_pairs={{0,8},{8,0},{16,24},{24,16},{1,9},{9,1},{17,25},{25,17},{2,10},{10... | collective-permute-start | bytes 2457608 | tf_op jit(solution)/shard_map/ppermute | solution.py:1042
  92.9 5.5 %collective-permute-start.22 = (bf16[784,512]{1,0:T(8,128)(2,1)S(1)}, bf16[784,512]{1,0:T(8,128)(2,1)}, u32[]{:S(2)}, u32[]{:S(2)}) collective-permute-start(bf16[784,512]{1,0:T(8,128)(2,1)S(1)} %collective-permute-done.8.refs_11_), channel_id=1, source_target_pairs={{0,8},{8,0},{16,24},{24,16},{1,9},{9,1},{17,25},{25,17},{2,10},{10... | collective-permute-start | bytes 2408456 | tf_op jit(solution)/shard_map/ppermute | solution.py:1042
  93.0 5.4 %collective-permute-start.21 = (bf16[784,512]{1,0:T(8,128)(2,1)S(1)}, bf16[784,512]{1,0:T(8,128)(2,1)}, u32[]{:S(2)}, u32[]{:S(2)}) collective-permute-start(bf16[784,512]{1,0:T(8,128)(2,1)S(1)} %collective-permute-done.7.refs_10_), channel_id=1, source_target_pairs={{0,8},{8,0},{16,24},{24,16},{1,9},{9,1},{17,25},{25,17},{2,10},{10... | collective-permute-start | bytes 2408456 | tf_op jit(solution)/shard_map/ppermute | solution.py:1042
  94.6 3.9 %collective-permute-start.18 = (bf16[528,512]{1,0:T(8,128)(2,1)S(1)}, bf16[528,512]{1,0:T(8,128)(2,1)}, u32[]{:S(2)}, u32[]{:S(2)}) collective-permute-start(bf16[528,512]{1,0:T(8,128)(2,1)S(1)} %collective-permute-done.6.refs_7_), channel_id=1, source_target_pairs={{0,8},{8,0},{16,24},{24,16},{1,9},{9,1},{17,25},{25,17},{2,10},{10... | collective-permute-start | bytes 1622024 | tf_op jit(solution)/shard_map/ppermute | solution.py:1042
  141.7 15.6 %collective-permute-start.32 = (bf16[4,528,512]{2,1,0:T(8,128)(2,1)}, bf16[4,528,512]{2,1,0:T(8,128)(2,1)S(1)}, u32[]{:S(2)}, u32[]{:S(2)}) collective-permute-start(bf16[4,528,512]{2,1,0:T(8,128)(2,1)} %get-tuple-element.158), channel_id=1, source_target_pairs={{0,8},{8,0},{16,24},{24,16},{1,9},{9,1},{17,25},{25,17},{2,10},{10... | collective-permute-start | bytes 6488072 | tf_op jit(solution)/shard_map/ppermute | solution.py:1042
  156.7 5.3 %collective-permute-start.31 = (bf16[4,528,512]{2,1,0:T(8,128)(2,1)}, bf16[4,528,512]{2,1,0:T(8,128)(2,1)}, u32[]{:S(2)}, u32[]{:S(2)}) collective-permute-start(bf16[4,528,512]{2,1,0:T(8,128)(2,1)} %get-tuple-element.156), channel_id=1, source_target_pairs={{0,8},{8,0},{16,24},{24,16},{1,9},{9,1},{17,25},{25,17},{2,10},{10... | collective-permute-start | bytes 6488072 | tf_op jit(solution)/shard_map/ppermute | solution.py:1042
  157.0 18.7 %collective-permute-start.36 = (bf16[4,528,512]{2,1,0:T(8,128)(2,1)}, bf16[4,528,512]{2,1,0:T(8,128)(2,1)S(1)}, u32[]{:S(2)}, u32[]{:S(2)}) collective-permute-start(bf16[4,528,512]{2,1,0:T(8,128)(2,1)} %get-tuple-element.171), channel_id=1, source_target_pairs={{0,8},{8,0},{16,24},{24,16},{1,9},{9,1},{17,25},{25,17},{2,10},{10... | collective-permute-start | bytes 6488072 | tf_op jit(solution)/shard_map/ppermute | solution.py:1042
  166.0 9.8 %collective-permute-start.35 = (bf16[4,528,512]{2,1,0:T(8,128)(2,1)}, bf16[4,528,512]{2,1,0:T(8,128)(2,1)S(1)}, u32[]{:S(2)}, u32[]{:S(2)}) collective-permute-start(bf16[4,528,512]{2,1,0:T(8,128)(2,1)} %get-tuple-element.170), channel_id=1, source_target_pairs={{0,8},{8,0},{16,24},{24,16},{1,9},{9,1},{17,25},{25,17},{2,10},{10... | collective-permute-start | bytes 6488072 | tf_op jit(solution)/shard_map/ppermute | solution.py:1042
  166.4 30.5 %collective-permute-start.33 = (bf16[2,528,512]{2,1,0:T(8,128)(2,1)}, bf16[2,528,512]{2,1,0:T(8,128)(2,1)S(1)}, u32[]{:S(2)}, u32[]{:S(2)}) collective-permute-start(bf16[2,528,512]{2,1,0:T(8,128)(2,1)} %get-tuple-element.159), channel_id=1, source_target_pairs={{0,1},{1,0},{2,3},{3,2},{4,5},{5,4},{6,7},{7,6},{8,9},{9,8},{10,11... | collective-permute-start | bytes 3244040 | tf_op jit(solution)/shard_map/ppermute | solution.py:1034
  168.8 28.1 %collective-permute-start.34 = (bf16[2,528,512]{2,1,0:T(8,128)(2,1)}, bf16[2,528,512]{2,1,0:T(8,128)(2,1)}, u32[]{:S(2)}, u32[]{:S(2)}) collective-permute-start(bf16[2,528,512]{2,1,0:T(8,128)(2,1)} %get-tuple-element.160), channel_id=1, source_target_pairs={{0,16},{8,24},{16,0},{24,8},{1,17},{9,25},{17,1},{25,9},{2,18},{10... | collective-permute-start | bytes 3244040 | tf_op jit(solution)/shard_map/ppermute | solution.py:1038
  188.2 3.9 %collective-permute-start.38 = (f32[16,512]{1,0:T(8,128)S(1)}, f32[16,512]{1,0:T(8,128)S(1)}, u32[]{:S(2)}, u32[]{:S(2)}) collective-permute-start(f32[16,512]{1,0:T(8,128)S(1)} %add.199), channel_id=1, source_target_pairs={{0,2},{1,3},{2,0},{3,1},{4,6},{5,7},{6,4},{7,5},{8,10},{9,11},{10,... | collective-permute-start | bytes 98312 | tf_op jit(solution)/shard_map/ppermute | solution.py:1050
  192.1 4.8 %collective-permute-start.39 = (f32[16,512]{1,0:T(8,128)S(1)}, f32[16,512]{1,0:T(8,128)S(1)}, u32[]{:S(2)}, u32[]{:S(2)}) collective-permute-start(f32[16,512]{1,0:T(8,128)S(1)} %add.200), channel_id=1, source_target_pairs={{0,4},{1,5},{2,6},{3,7},{4,0},{5,1},{6,2},{7,3},{8,12},{9,13},{10,... | collective-permute-start | bytes 98312 | tf_op jit(solution)/shard_map/ppermute | solution.py:1050
  196.9 20.7 %collective-permute-start.62 = (f32[16,512]{1,0:T(8,128)S(1)}, f32[16,512]{1,0:T(8,128)S(1)}, u32[]{:S(2)}, u32[]{:S(2)}) collective-permute-start(f32[16,512]{1,0:T(8,128)S(1)} %add.201), channel_id=1, source_target_pairs={{0,1},{1,0},{2,3},{3,2},{4,5},{5,4},{6,7},{7,6},{8,9},{9,8},{10,11... | collective-permute-start | bytes 98312 | tf_op jit(solution)/shard_map/ppermute | solution.py:1034
  198.2 9.4 %collective-permute-start.41 = (bf16[256,512]{1,0:T(8,128)(2,1)}, bf16[256,512]{1,0:T(8,128)(2,1)S(1)}, u32[]{:S(2)}, u32[]{:S(2)}) collective-permute-start(bf16[256,512]{1,0:T(8,128)(2,1)} %get-tuple-element.196), channel_id=1, source_target_pairs={{0,16},{8,24},{16,0},{24,8},{1,17},{9,25},{17,1},{25,9},{2,18},{10... | collective-permute-start | bytes 786440 | tf_op jit(solution)/shard_map/ppermute | solution.py:1038
  198.9 14.6 %collective-permute-start.52 = (bf16[272,512]{1,0:T(8,128)(2,1)}, bf16[272,512]{1,0:T(8,128)(2,1)S(1)}, u32[]{:S(2)}, u32[]{:S(2)}) collective-permute-start(bf16[272,512]{1,0:T(8,128)(2,1)} %get-tuple-element.215), channel_id=1, source_target_pairs={{0,16},{8,24},{16,0},{24,8},{1,17},{9,25},{17,1},{25,9},{2,18},{10... | collective-permute-start | bytes 835592 | tf_op jit(solution)/shard_map/ppermute | solution.py:1038
  201.4 9.3 %collective-permute-start.40 = (bf16[256,512]{1,0:T(8,128)(2,1)S(1)}, bf16[256,512]{1,0:T(8,128)(2,1)S(1)}, u32[]{:S(2)}, u32[]{:S(2)}) collective-permute-start(bf16[256,512]{1,0:T(8,128)(2,1)S(1)} %get-tuple-element.238), channel_id=1, source_target_pairs={{0,1},{1,0},{2,3},{3,2},{4,5},{5,4},{6,7},{7,6},{8,9},{9,8},{10,11... | collective-permute-start | bytes 786440 | tf_op jit(solution)/shard_map/ppermute | solution.py:1034
  203.5 13.2 %collective-permute-start.51 = (bf16[272,512]{1,0:T(8,128)(2,1)S(1)}, bf16[272,512]{1,0:T(8,128)(2,1)S(1)}, u32[]{:S(2)}, u32[]{:S(2)}) collective-permute-start(bf16[272,512]{1,0:T(8,128)(2,1)S(1)} %get-tuple-element.242), channel_id=1, source_target_pairs={{0,1},{1,0},{2,3},{3,2},{4,5},{5,4},{6,7},{7,6},{8,9},{9,8},{10,11... | collective-permute-start | bytes 835592 | tf_op jit(solution)/shard_map/ppermute | solution.py:1034
  210.7 11.6 %collective-permute-start.42 = (bf16[256,512]{1,0:T(8,128)(2,1)S(1)}, bf16[256,512]{1,0:T(8,128)(2,1)S(1)}, u32[]{:S(2)}, u32[]{:S(2)}) collective-permute-start(bf16[256,512]{1,0:T(8,128)(2,1)S(1)} %get-tuple-element.197), channel_id=1, source_target_pairs={{0,1},{1,0},{2,3},{3,2},{4,5},{5,4},{6,7},{7,6},{8,9},{9,8},{10,11... | collective-permute-start | bytes 786440 | tf_op jit(solution)/shard_map/ppermute | solution.py:1034
  211.6 13.0 %collective-permute-start.43 = (bf16[256,512]{1,0:T(8,128)(2,1)S(1)}, bf16[256,512]{1,0:T(8,128)(2,1)S(1)}, u32[]{:S(2)}, u32[]{:S(2)}) collective-permute-start(bf16[256,512]{1,0:T(8,128)(2,1)S(1)} %copy-done.51), channel_id=1, source_target_pairs={{0,16},{8,24},{16,0},{24,8},{1,17},{9,25},{17,1},{25,9},{2,18},{10... | collective-permute-start | bytes 786440 | tf_op jit(solution)/shard_map/ppermute | solution.py:1038
  213.5 11.2 %collective-permute-start.48 = (bf16[256,512]{1,0:T(8,128)(2,1)S(1)}, bf16[256,512]{1,0:T(8,128)(2,1)S(1)}, u32[]{:S(2)}, u32[]{:S(2)}) collective-permute-start(bf16[256,512]{1,0:T(8,128)(2,1)S(1)} %add_convert_fusion.5), channel_id=1, source_target_pairs={{0,2},{1,3},{2,4},{3,5},{4,6},{5,7},{6,0},{7,1},{8,10},{9,11},{10,... | collective-permute-start | bytes 786440 | tf_op jit(solution)/shard_map/ppermute | solution.py:1046
  216.7 11.0 %collective-permute-start.53 = (bf16[272,512]{1,0:T(8,128)(2,1)S(1)}, bf16[272,512]{1,0:T(8,128)(2,1)S(1)}, u32[]{:S(2)}, u32[]{:S(2)}) collective-permute-start(bf16[272,512]{1,0:T(8,128)(2,1)S(1)} %get-tuple-element.216), channel_id=1, source_target_pairs={{0,1},{1,0},{2,3},{3,2},{4,5},{5,4},{6,7},{7,6},{8,9},{9,8},{10,11... | collective-permute-start | bytes 835592 | tf_op jit(solution)/shard_map/ppermute | solution.py:1034
  217.7 11.9 %collective-permute-start.54 = (bf16[272,512]{1,0:T(8,128)(2,1)S(1)}, bf16[272,512]{1,0:T(8,128)(2,1)S(1)}, u32[]{:S(2)}, u32[]{:S(2)}) collective-permute-start(bf16[272,512]{1,0:T(8,128)(2,1)S(1)} %copy-done.49), channel_id=1, source_target_pairs={{0,16},{8,24},{16,0},{24,8},{1,17},{9,25},{17,1},{25,9},{2,18},{10... | collective-permute-start | bytes 835592 | tf_op jit(solution)/shard_map/ppermute | solution.py:1038
  222.3 11.3 %collective-permute-start.59 = (bf16[272,512]{1,0:T(8,128)(2,1)S(1)}, bf16[272,512]{1,0:T(8,128)(2,1)S(1)}, u32[]{:S(2)}, u32[]{:S(2)}) collective-permute-start(bf16[272,512]{1,0:T(8,128)(2,1)S(1)} %add_convert_fusion.2), channel_id=1, source_target_pairs={{0,2},{1,3},{2,4},{3,5},{4,6},{5,7},{6,0},{7,1},{8,10},{9,11},{10,... | collective-permute-start | bytes 835592 | tf_op jit(solution)/shard_map/ppermute | solution.py:1046
  224.6 9.9 %collective-permute-start.63 = (f32[16,512]{1,0:T(8,128)S(1)}, f32[16,512]{1,0:T(8,128)S(1)}, u32[]{:S(2)}, u32[]{:S(2)}) collective-permute-start(f32[16,512]{1,0:T(8,128)S(1)} %add.232), channel_id=1, source_target_pairs={{0,16},{8,24},{16,0},{24,8},{1,17},{9,25},{17,1},{25,9},{2,18},{10... | collective-permute-start | bytes 98312 | tf_op jit(solution)/shard_map/ppermute | solution.py:1038
  224.7 9.9 %collective-permute-start.44 = (bf16[256,512]{1,0:T(8,128)(2,1)S(1)}, bf16[256,512]{1,0:T(8,128)(2,1)S(1)}, u32[]{:S(2)}, u32[]{:S(2)}) collective-permute-start(bf16[256,512]{1,0:T(8,128)(2,1)S(1)} %copy-done.50), channel_id=1, source_target_pairs={{0,1},{1,0},{2,3},{3,2},{4,5},{5,4},{6,7},{7,6},{8,9},{9,8},{10,11... | collective-permute-start | bytes 786440 | tf_op jit(solution)/shard_map/ppermute | solution.py:1034
  227.7 11.4 %collective-permute-start.49 = (bf16[256,512]{1,0:T(8,128)(2,1)S(1)}, bf16[256,512]{1,0:T(8,128)(2,1)S(1)}, u32[]{:S(2)}, u32[]{:S(2)}) collective-permute-start(bf16[256,512]{1,0:T(8,128)(2,1)S(1)} %add_convert_fusion.4), channel_id=1, source_target_pairs={{0,2},{1,3},{2,4},{3,5},{4,6},{5,7},{6,0},{7,1},{8,10},{9,11},{10,... | collective-permute-start | bytes 786440 | tf_op jit(solution)/shard_map/ppermute | solution.py:1046
  229.6 8.7 %collective-permute-start.45 = (bf16[256,512]{1,0:T(8,128)(2,1)}, bf16[256,512]{1,0:T(8,128)(2,1)S(1)}, u32[]{:S(2)}, u32[]{:S(2)}) collective-permute-start(bf16[256,512]{1,0:T(8,128)(2,1)} %get-tuple-element.203), channel_id=1, source_target_pairs={{0,16},{8,24},{16,0},{24,8},{1,17},{9,25},{17,1},{25,9},{2,18},{10... | collective-permute-start | bytes 786440 | tf_op jit(solution)/shard_map/ppermute | solution.py:1038
  233.7 9.3 %collective-permute-start.55 = (bf16[272,512]{1,0:T(8,128)(2,1)}, bf16[272,512]{1,0:T(8,128)(2,1)S(1)}, u32[]{:S(2)}, u32[]{:S(2)}) collective-permute-start(bf16[272,512]{1,0:T(8,128)(2,1)} %get-tuple-element.219), channel_id=1, source_target_pairs={{0,1},{1,0},{2,3},{3,2},{4,5},{5,4},{6,7},{7,6},{8,9},{9,8},{10,11... | collective-permute-start | bytes 835592 | tf_op jit(solution)/shard_map/ppermute | solution.py:1034
  234.5 10.5 %collective-permute-start.60 = (bf16[272,512]{1,0:T(8,128)(2,1)S(1)}, bf16[272,512]{1,0:T(8,128)(2,1)S(1)}, u32[]{:S(2)}, u32[]{:S(2)}) collective-permute-start(bf16[272,512]{1,0:T(8,128)(2,1)S(1)} %add_convert_fusion.1), channel_id=1, source_target_pairs={{0,2},{1,3},{2,4},{3,5},{4,6},{5,7},{6,0},{7,1},{8,10},{9,11},{10,... | collective-permute-start | bytes 835592 | tf_op jit(solution)/shard_map/ppermute | solution.py:1046
  234.6 9.6 %collective-permute-start.56 = (bf16[272,512]{1,0:T(8,128)(2,1)S(1)}, bf16[272,512]{1,0:T(8,128)(2,1)S(1)}, u32[]{:S(2)}, u32[]{:S(2)}) collective-permute-start(bf16[272,512]{1,0:T(8,128)(2,1)S(1)} %get-tuple-element.221), channel_id=1, source_target_pairs={{0,16},{8,24},{16,0},{24,8},{1,17},{9,25},{17,1},{25,9},{2,18},{10... | collective-permute-start | bytes 835592 | tf_op jit(solution)/shard_map/ppermute | solution.py:1038
  238.3 8.5 %collective-permute-start.46 = (bf16[256,512]{1,0:T(8,128)(2,1)}, bf16[256,512]{1,0:T(8,128)(2,1)S(1)}, u32[]{:S(2)}, u32[]{:S(2)}) collective-permute-start(bf16[256,512]{1,0:T(8,128)(2,1)} %get-tuple-element.204), channel_id=1, source_target_pairs={{0,1},{1,0},{2,3},{3,2},{4,5},{5,4},{6,7},{7,6},{8,9},{9,8},{10,11... | collective-permute-start | bytes 786440 | tf_op jit(solution)/shard_map/ppermute | solution.py:1034
  239.1 8.7 %collective-permute-start.47 = (bf16[256,512]{1,0:T(8,128)(2,1)}, bf16[256,512]{1,0:T(8,128)(2,1)S(1)}, u32[]{:S(2)}, u32[]{:S(2)}) collective-permute-start(bf16[256,512]{1,0:T(8,128)(2,1)} %get-tuple-element.206), channel_id=1, source_target_pairs={{0,16},{8,24},{16,0},{24,8},{1,17},{9,25},{17,1},{25,9},{2,18},{10... | collective-permute-start | bytes 786440 | tf_op jit(solution)/shard_map/ppermute | solution.py:1038
  243.0 8.2 %collective-permute-start.50 = (bf16[256,512]{1,0:T(8,128)(2,1)S(1)}, bf16[256,512]{1,0:T(8,128)(2,1)S(1)}, u32[]{:S(2)}, u32[]{:S(2)}) collective-permute-start(bf16[256,512]{1,0:T(8,128)(2,1)S(1)} %add_convert_fusion.3), channel_id=1, source_target_pairs={{0,2},{1,3},{2,4},{3,5},{4,6},{5,7},{6,0},{7,1},{8,10},{9,11},{10,... | collective-permute-start | bytes 786440 | tf_op jit(solution)/shard_map/ppermute | solution.py:1046
  244.2 7.2 %collective-permute-start.57 = (bf16[272,512]{1,0:T(8,128)(2,1)}, bf16[272,512]{1,0:T(8,128)(2,1)S(1)}, u32[]{:S(2)}, u32[]{:S(2)}) collective-permute-start(bf16[272,512]{1,0:T(8,128)(2,1)} %get-tuple-element.222), channel_id=1, source_target_pairs={{0,1},{1,0},{2,3},{3,2},{4,5},{5,4},{6,7},{7,6},{8,9},{9,8},{10,11... | collective-permute-start | bytes 835592 | tf_op jit(solution)/shard_map/ppermute | solution.py:1034
  245.0 6.5 %collective-permute-start.58 = (bf16[272,512]{1,0:T(8,128)(2,1)S(1)}, bf16[272,512]{1,0:T(8,128)(2,1)S(1)}, u32[]{:S(2)}, u32[]{:S(2)}) collective-permute-start(bf16[272,512]{1,0:T(8,128)(2,1)S(1)} %get-tuple-element.224), channel_id=1, source_target_pairs={{0,16},{8,24},{16,0},{24,8},{1,17},{9,25},{17,1},{25,9},{2,18},{10... | collective-permute-start | bytes 835592 | tf_op jit(solution)/shard_map/ppermute | solution.py:1038
  246.9 8.4 %collective-permute-start.61 = (bf16[272,512]{1,0:T(8,128)(2,1)S(1)}, bf16[272,512]{1,0:T(8,128)(2,1)S(1)}, u32[]{:S(2)}, u32[]{:S(2)}) collective-permute-start(bf16[272,512]{1,0:T(8,128)(2,1)S(1)} %add_convert_fusion), channel_id=1, source_target_pairs={{0,2},{1,3},{2,4},{3,5},{4,6},{5,7},{6,0},{7,1},{8,10},{9,11},{10,... | collective-permute-start | bytes 835592 | tf_op jit(solution)/shard_map/ppermute | solution.py:1046
  264.5 3.6 %collective-permute-start.65 = (f32[8,128]{1,0:T(8,128)S(1)}, f32[8,128]{1,0:T(8,128)S(1)}, u32[]{:S(2)}, u32[]{:S(2)}) collective-permute-start(f32[8,128]{1,0:T(8,128)S(1)} %add.237), channel_id=1, source_target_pairs={{0,1},{1,0},{2,3},{3,2},{4,5},{5,4},{6,7},{7,6},{8,9},{9,8},{10,11... | collective-permute-start | bytes 12296 | tf_op jit(solution)/shard_map/ppermute | solution.py:1034
  275.3 4.5 %collective-permute-start.68 = (f32[8,128]{1,0:T(8,128)S(1)}, f32[8,128]{1,0:T(8,128)S(1)}, u32[]{:S(2)}, u32[]{:S(2)}) collective-permute-start(f32[8,128]{1,0:T(8,128)S(1)} %add.240), channel_id=1, source_target_pairs={{0,4},{1,5},{2,6},{3,7},{4,0},{5,1},{6,2},{7,3},{8,12},{9,13},{10,... | collective-permute-start | bytes 12296 | tf_op jit(solution)/shard_map/ppermute | solution.py:1050
  (58 other events, 931.8 us)

commit v2 on v1

--- a/solution.py
+++ b/solution.py
@@ -170,7 +170,7 @@
             diagonal = [(core, 1, 1, back, first, last) for back in range(4)]
             layout += [[whole[0]], [whole[1]]]
             layout += [[whole[2], (*diagonal[0], SPAN)], [whole[3], (*diagonal[1], SPAN)]]
-            layout += [[(*diagonal[2], 0)], [(*diagonal[3], 0)]]
+            layout += [[(*diagonal[2], 0), (*diagonal[3], last - first)]]
     return layout
 
 
@@ -496,7 +496,7 @@
             r.ug[rows, at] = active
             r.slope_c[rows, at] = low(slope)
 
-    each_loop(CG // 256, up, 2)
+    each_loop(CG // 256, up, 4)
     tiles = [slice(GATE + 128 * j, GATE + 128 * j + 128) for j in range(GATE // 128)]
     total = jnp.zeros((SLOTS, 128), F32)
     for at in tiles:
@@ -1083,17 +1083,14 @@
         else:
             by_x.append(over_x(jnp.concatenate([own[back], by_y[back - 2][:HALF]])))
             by_y.append(over_y(jnp.concatenate([own[back], by_x[back - 2][HALF:SPAN]])))
-    by_x.append(over_x(by_y[2][:HALF]))
-    by_y.append(over_y(by_x[2][HALF:SPAN]))
-    last_x, last_y = by_y[3][:HALF], by_x[3][HALF:SPAN]
-    by_x.append(over_x(after(last_x, by_x[4])))
-    by_y.append(over_y(after(last_y, by_y[4])))
+    by_x.append(over_x(jnp.concatenate([by_y[2][:HALF], by_y[3][:HALF]])))
+    by_y.append(over_y(jnp.concatenate([by_x[2][HALF:SPAN], by_x[3][HALF:SPAN]])))
     late_ones = (by_x[3], by_y[3])
     far_own = [over_core(each_one) for each_one in own[:2]] + [over_core(after(each_one, *late_ones)) for each_one in own[2:]]
     far = [far_own]
     for way in (by_x, by_y):
         far.append([over_core(way[0]), over_core(way[1]), over_core(after(way[2], *late_ones))])
-        far[-1] += [over_core(way[at]) for at in (3, 4, 5)]
+        far[-1] += [over_core(way[at]) for at in (3, 4)]
     return own + by_x + by_y + far[0] + far[1] + far[2]
 
 
@@ -1332,13 +1329,12 @@
             add(at, strips(squares, (nothing, nothing)))
 
 
-def apply_kernel(segments, sums, params, update, new_params, norms):
+def apply_kernel(segments, sums, params, update, new_params, *norms):
     step = pl.program_id(0)
     roots = jnp.sqrt(sums[0:2, :])
     trust = roots[0:1, :] / (roots[1:2, :] + ADAM_EPS)
-    norms[0:2, :] = roots
-    norms[2:3, :] = trust
-    norms[3:8, :] = jnp.zeros((5, LANES), F32)
+    for out, row in zip(norms, (roots[0:1, :], roots[1:2, :], trust)):
+        out[...] = row.reshape(LANES)[: out.shape[0]]
     lane = lax.broadcasted_iota(jnp.int32, (1, LANES), 1)
     for at, whole, some, start, end in chunk_spans(segments, step):
 
@@ -1405,24 +1401,22 @@
         out_shape=[flat_kind] * 3 + [tile_kind],
     )(segments, weights, filled(first_moment), filled(second_moment), grad_shard)
     sums = sum_everywhere(sums)
-    new_params, norms = pl.pallas_call(
+    count = len(segment_shapes())
+    new_params, *norms = pl.pallas_call(
         apply_kernel,
         name="apply",
         grid=(steps,),
         in_specs=[SM, whole, grid, grid],
-        out_specs=[grid, whole],
-        out_shape=[flat_kind, tile_kind],
+        out_specs=[grid] + [pl.BlockSpec((count,), lambda step: (0,))] * 3,
+        out_shape=[flat_kind] + [jax.ShapeDtypeStruct((count,), F32)] * 3,
     )(segments, sums, weights, update)
-    count = len(segment_shapes())
     return (
         state["out"].reshape(frames.shape),
         back["fgrad"].reshape(frames.shape),
         new_params[:shard_size],
         new_first[:shard_size],
         new_second[:shard_size],
-        norms[0, :count],
-        norms[1, :count],
-        norms[2, :count],
+        *norms,
         gain_grads.reshape(-1),
     )
 

time: 286 us -> 284 us (level)
  starting transfers between devices: 52.2 us -> 49.2 us
    ppermute x17 -> x16, waiting for transfers between devices: 26.9 us -> 48.7 us  [over_x(): return lax.ppermute(value, 'fsdp', [(i, i ^ 1) for i in range(8)])]
    ppermute x17 -> x16, waiting for transfers between devices: 52.6 us -> 31.9 us  [over_y(): return lax.ppermute(value, 'dp', [(i, i ^ 2) for i in range(4)])]
    ppermute x17 -> x16, starting transfers between devices: 18.1 us -> 16.2 us  [over_x(): return lax.ppermute(value, 'fsdp', [(i, i ^ 1) for i in range(8)])]
    unnamed x107 -> x101, local copies, waits for them, and re-layouts: 4.83 us -> 6.05 us
    ppermute x17 -> x16, starting transfers between devices: 19.1 us -> 19.6 us  [over_y(): return lax.ppermute(value, 'dp', [(i, i ^ 2) for i in range(4)])]
    ppermute x22 -> x20, waiting for transfers between devices: 10.4 us -> 10.6 us  [over_core(): return lax.ppermute(value, 'dp', [(i, i ^ 1) for i in range(4)])]
  transfers between devices with their start and end apart: 69 -> 65, of which waited for: 35 -> 35; matrix products, arithmetic and copies ran while one was open for 3% -> 3% of each run, Pallas kernels for 11% -> 11%
where the time goes in v2:
time: 284 us; the launch traced here: 283 us
  waiting for transfers between devices  131 us (46%)
  Pallas kernels  82.2 us (29%)
  starting transfers between devices  49.2 us (17%)
  other arithmetic  9.44 us (3%)
  local copies, waits for them, and re-layouts  9.24 us (3%)
    pallas_call x6, Pallas kernels, call(): pl.pallas_call(kernel, name=name, in_specs=[space for space, _ in ins], o...  73.4 us
    ppermute x16, waiting for transfers between devices, over_x(): return lax.ppermute(value, 'fsdp', [(i, i ^ 1) for i in range(8)])  48.7 us
    ppermute x16, waiting for transfers between devices, over_y(): return lax.ppermute(value, 'dp', [(i, i ^ 2) for i in range(4)])  31.9 us
    ppermute x9, waiting for transfers between devices, round_z(): return lax.ppermute(value, 'fsdp', [(i, (i + 2) % 8) for i in range(8)])  26.6 us
    ppermute x16, starting transfers between devices, over_y(): return lax.ppermute(value, 'dp', [(i, i ^ 2) for i in range(4)])  19.6 us
    ppermute x16, starting transfers between devices, over_x(): return lax.ppermute(value, 'fsdp', [(i, i ^ 1) for i in range(8)])  16.2 us
    ppermute x4, waiting for transfers between devices, over_z(): return lax.ppermute(value, 'fsdp', [(i, i ^ 2 * step) for i in range(8)])  13.3 us
    ppermute x20, waiting for transfers between devices, over_core(): return lax.ppermute(value, 'dp', [(i, i ^ 1) for i in range(4)])  10.6 us
  transfers between devices with their start and end apart: 65, of which 35 were waited for; matrix products, arithmetic and copies ran while one was open for 3% of the time, Pallas kernels for 11%

profile of v2, /device:TPU:0, one launch (start us, length us, event | category | flops | bytes accessed | tf_op | source)
XLA Modules:
  0.0 283.4 jit_solution(11137554154812602081)
XLA Ops:
  0.7 1.3 convert_element_type.246
  2.8 3.0 %collective-permute-start.2 = (bf16[528,512]{1,0:T(8,128)(2,1)S(1)}, bf16[528,512]{1,0:T(8,128)(2,1)S(1)}, u32[]{:S(2)}, u32[]{:S(2)}) collective-permute-start(bf16[528,512]{1,0:T(8,128)(2,1)S(1)} %reshape.49.refs_4_), channel_id=1, source_target_pairs={{0,16},{8,24},{16,0},{24,8},{1,17},{9,25},{17,1},{25,9},{2,18},{10... | collective-permute-start | bytes 1622024 | tf_op jit(solution)/shard_map/ppermute | solution.py:1038
  5.8 1.5 collective-permute-start.1
  7.3 1.6 collective-permute-start
  8.9 9.2 %collective-permute-done.2.refs_13_ = bf16[528,512]{1,0:T(8,128)(2,1)S(1)} collective-permute-done((bf16[528,512]{1,0:T(8,128)(2,1)S(1)}, bf16[528,512]{1,0:T(8,128)(2,1)S(1)}, u32[]{:S(2)}, u32[]{:S(2)}) %collective-permute-start.2) | collective-permute-done | bytes 540704 | tf_op jit(solution)/shard_map/ppermute | solution.py:1038
  18.1 1.5 collective-permute-done.1.refs_8_
  19.5 3.1 %collective-permute-done.refs_5_ = bf16[528,512]{1,0:T(8,128)(2,1)S(1)} collective-permute-done((bf16[528,512]{1,0:T(8,128)(2,1)S(1)}, bf16[528,512]{1,0:T(8,128)(2,1)S(1)}, u32[]{:S(2)}, u32[]{:S(2)}) %collective-permute-start) | collective-permute-done | bytes 540704 | tf_op jit(solution)/shard_map/ppermute | solution.py:1046
  23.6 11.5 %collective-permute-done.5.refs_14_ = bf16[528,512]{1,0:T(8,128)(2,1)S(1)} collective-permute-done((bf16[528,512]{1,0:T(8,128)(2,1)S(1)}, bf16[528,512]{1,0:T(8,128)(2,1)S(1)}, u32[]{:S(2)}, u32[]{:S(2)}) %collective-permute-start.5) | collective-permute-done | bytes 540704 | tf_op jit(solution)/shard_map/ppermute | solution.py:1038
  35.4 2.3 collective-permute-done.3.refs_6_
  37.8 1.3 collective-permute-start.7
  39.2 1.6 collective-permute-start.9
  40.8 10.0 %collective-permute-done.6.refs_7_ = bf16[528,512]{1,0:T(8,128)(2,1)S(1)} collective-permute-done((bf16[528,512]{1,0:T(8,128)(2,1)S(1)}, bf16[528,512]{1,0:T(8,128)(2,1)S(1)}, u32[]{:S(2)}, u32[]{:S(2)}) %collective-permute-start.6) | collective-permute-done | bytes 540704 | tf_op jit(solution)/shard_map/ppermute | solution.py:1046
  50.9 1.1 collective-permute-start.8
  52.1 1.6 collective-permute-start.10
  54.1 4.6 %collective-permute-done.7.refs_10_ = bf16[784,512]{1,0:T(8,128)(2,1)S(1)} collective-permute-done((bf16[784,512]{1,0:T(8,128)(2,1)S(1)}, bf16[784,512]{1,0:T(8,128)(2,1)S(1)}, u32[]{:S(2)}, u32[]{:S(2)}) %collective-permute-start.7) | collective-permute-done | bytes 802848 | tf_op jit(solution)/shard_map/ppermute | solution.py:1034
  59.3 12.8 %collective-permute-done.8.refs_11_ = bf16[784,512]{1,0:T(8,128)(2,1)S(1)} collective-permute-done((bf16[784,512]{1,0:T(8,128)(2,1)S(1)}, bf16[784,512]{1,0:T(8,128)(2,1)S(1)}, u32[]{:S(2)}, u32[]{:S(2)}) %collective-permute-start.8) | collective-permute-done | bytes 802848 | tf_op jit(solution)/shard_map/ppermute | solution.py:1034
  72.1 1.7 collective-permute-done.10.refs_16_
  74.9 1.6 collective-permute-start.12
  78.0 13.0 %collective-permute-done.11.refs_12_ = bf16[512,512]{1,0:T(8,128)(2,1)} collective-permute-done((bf16[512,512]{1,0:T(8,128)(2,1)S(1)}, bf16[512,512]{1,0:T(8,128)(2,1)}, u32[]{:S(2)}, u32[]{:S(2)}) %collective-permute-start.11) | collective-permute-done | bytes 524320 | tf_op jit(solution)/shard_map/ppermute | solution.py:1034
  95.1 2.3 collective-permute-done.19.refs_24_
  98.5 42.5 %forward.1 = (bf16[160,512]{1,0:T(8,128)(2,1)}, f32[8,512]{1,0:T(8,128)}, f32[176,512]{1,0:T(8,128)}, bf16[8,528,512]{2,1,0:T(8,128)(2,1)}, bf16[4,528,512]{2,1,...) custom-call(s32[4]{0:T(128)} %pad_add_fusion.refs_0_.coords, ...), custom_call_target="tpu_custom_call" | custom-call | tf_op jit(solution)/shard_map/forward/pallas_call | solution.py:972
  141.2 14.6 %backward.1 = (bf16[160,512]{1,0:T(8,128)(2,1)}, f32[16,512]{1,0:T(8,128)}, bf16[8,528,512]{2,1,0:T(8,128)(2,1)}, bf16[4,528,512]{2,1,0:T(8,128)(2,1)}, bf16[4,528,512]{2,1,0:T(8,128)(2,1)}) custom-call(s32[4]{0:T(128)} %pad_add_fusion.refs_0_.coords, bf16[160,512]{1,0:T(8,128)(2,1)} %bitcast.41, ...), custom_call_target="tpu_custom_call", output_to_operand_aliasing={{2}: (18, {}), {3}: (19, {}), {4}: (20, {})} | custom-call | tf_op jit(solution)/shard_map/backward/pallas_call | solution.py:972
  156.5 5.4 %collective-permute-done.27.low_got = bf16[4,528,512]{2,1,0:T(8,128)(2,1)} collective-permute-done((bf16[4,528,512]{2,1,0:T(8,128)(2,1)}, bf16[4,528,512]{2,1,0:T(8,128)(2,1)}, u32[]{:S(2)}, u32[]{:S(2)}) %collective-permute-start.27) | collective-permute-done | bytes 2162720 | tf_op jit(solution)/shard_map/ppermute | solution.py:1042
  161.9 4.0 %span_sums.4 = (bf16[2,528,512]{2,1,0:T(8,128)(2,1)}, bf16[2,528,512]{2,1,0:T(8,128)(2,1)}) custom-call(s32[4]{0:T(128)} %pad_add_fusion.refs_0_.coords, bf16[8,528,512]{2,1,0:T(8,128)(2,1)} %get-tuple-element.153.low_kept, bf16[4,528,512]{2,1,0:T(8,128)(2,1)} %collective-permute-done.27.low_got, bf16[8,528,512]{2,1,0:T(8,128)(2,1)} %get-tuple-element.155.high_kept, ...), custom_call_target="tpu_custom_call" | custom-call | tf_op jit(solution)/shard_map/span_sums/pallas_call | solution.py:972
  166.3 1.7 collective-permute-start.29
  168.0 3.1 %collective-permute-start.30 = (bf16[2,528,512]{2,1,0:T(8,128)(2,1)}, bf16[2,528,512]{2,1,0:T(8,128)(2,1)}, u32[]{:S(2)}, u32[]{:S(2)}) collective-permute-start(bf16[2,528,512]{2,1,0:T(8,128)(2,1)} %get-tuple-element.158), channel_id=1, source_target_pairs={{0,16},{8,24},{16,0},{24,8},{1,17},{9,25},{17,1},{25,9},{2,18},{10... | collective-permute-start | bytes 3244040 | tf_op jit(solution)/shard_map/ppermute | solution.py:1038
  171.1 4.0 %span_sums.5 = (bf16[256,512]{1,0:T(8,128)(2,1)}, bf16[272,512]{1,0:T(8,128)(2,1)}, bf16[256,512]{1,0:T(8,128)(2,1)}, bf16[272,512]{1,0:T(8,128)(2,1)}, bf16[256...) custom-call(s32[4]{0:T(128)} %pad_add_fusion.refs_0_.coords, ...), custom_call_target="tpu_custom_call" | custom-call | tf_op jit(solution)/shard_map/span_sums/pallas_call | solution.py:972
  175.1 1.3 copy-done.1
  176.4 1.3 copy-done.2
  177.8 4.0 %span_sums.7 = (bf16[256,512]{1,0:T(8,128)(2,1)}, bf16[272,512]{1,0:T(8,128)(2,1)}, bf16[256,512]{1,0:T(8,128)(2,1)}, bf16[272,512]{1,0:T(8,128)(2,1)}, bf16[256...) custom-call(s32[4]{0:T(128)} %pad_add_fusion.refs_0_.coords, ...), custom_call_target="tpu_custom_call" | custom-call | tf_op jit(solution)/shard_map/span_sums/pallas_call | solution.py:972
  181.8 4.4 %span_sums.6 = (bf16[256,512]{1,0:T(8,128)(2,1)}, bf16[272,512]{1,0:T(8,128)(2,1)}, bf16[256,512]{1,0:T(8,128)(2,1)}, bf16[272,512]{1,0:T(8,128)(2,1)}, bf16[256...) custom-call(s32[4]{0:T(128)} %pad_add_fusion.refs_0_.coords, ...), custom_call_target="tpu_custom_call" | custom-call | tf_op jit(solution)/shard_map/span_sums/pallas_call | solution.py:972
  186.3 1.2 collective-permute-done.33
  187.5 3.9 %collective-permute-done.34 = f32[16,512]{1,0:T(8,128)S(1)} collective-permute-done((f32[16,512]{1,0:T(8,128)S(1)}, f32[16,512]{1,0:T(8,128)S(1)}, u32[]{:S(2)}, u32[]{:S(2)}) %collective-permute-start.34) | collective-permute-done | bytes 32800 | tf_op jit(solution)/shard_map/ppermute | solution.py:1050
  191.4 2.0 collective-permute-start.35
  193.4 2.8 collective-permute-done.35
  196.3 1.1 collective-permute-start.58
  198.1 1.3 collective-permute-start.48
  199.4 1.2 fusion.8
  200.6 1.0 collective-permute-start.36
  201.6 1.2 fusion.4
  202.9 1.1 collective-permute-start.47
  204.2 2.6 collective-permute-done.37
  206.8 3.1 %collective-permute-done.36 = bf16[256,512]{1,0:T(8,128)(2,1)S(1)} collective-permute-done((bf16[256,512]{1,0:T(8,128)(2,1)S(1)}, bf16[256,512]{1,0:T(8,128)(2,1)S(1)}, u32[]{:S(2)}, u32[]{:S(2)}) %collective-permute-start.36) | collective-permute-done | bytes 262176 | tf_op jit(solution)/shard_map/ppermute | solution.py:1034
  212.6 1.3 collective-permute-start.44
  213.9 2.0 collective-permute-done.47
  217.8 3.7 %collective-permute-done.38 = bf16[256,512]{1,0:T(8,128)(2,1)S(1)} collective-permute-done((bf16[256,512]{1,0:T(8,128)(2,1)S(1)}, bf16[256,512]{1,0:T(8,128)(2,1)S(1)}, u32[]{:S(2)}, u32[]{:S(2)}) %collective-permute-start.38) | collective-permute-done | bytes 262176 | tf_op jit(solution)/shard_map/ppermute | solution.py:1034
  221.5 1.1 collective-permute-start.55
  224.8 2.2 collective-permute-done.49
  227.0 1.6 collective-permute-start.45
  228.6 3.8 %collective-permute-done.55 = bf16[272,512]{1,0:T(8,128)(2,1)S(1)} collective-permute-done((bf16[272,512]{1,0:T(8,128)(2,1)S(1)}, bf16[272,512]{1,0:T(8,128)(2,1)S(1)}, u32[]{:S(2)}, u32[]{:S(2)}) %collective-permute-start.55) | collective-permute-done | bytes 278560 | tf_op jit(solution)/shard_map/ppermute | solution.py:1046
  233.4 1.6 collective-permute-start.52
  239.1 2.9 %collective-permute-done.51 = bf16[272,512]{1,0:T(8,128)(2,1)S(1)} collective-permute-done((bf16[272,512]{1,0:T(8,128)(2,1)}, bf16[272,512]{1,0:T(8,128)(2,1)S(1)}, u32[]{:S(2)}, u32[]{:S(2)}) %collective-permute-start.51) | collective-permute-done | bytes 278560 | tf_op jit(solution)/shard_map/ppermute | solution.py:1034
  242.0 1.1 collective-permute-done.52
  244.0 2.1 collective-permute-start.54
  246.8 3.4 %collective-permute-done.46 = bf16[256,512]{1,0:T(8,128)(2,1)S(1)} collective-permute-done((bf16[256,512]{1,0:T(8,128)(2,1)S(1)}, bf16[256,512]{1,0:T(8,128)(2,1)S(1)}, u32[]{:S(2)}, u32[]{:S(2)}) %collective-permute-start.46) | collective-permute-done | bytes 262176 | tf_op jit(solution)/shard_map/ppermute | solution.py:1046
  250.6 4.0 %collective-permute-done.57 = bf16[272,512]{1,0:T(8,128)(2,1)S(1)} collective-permute-done((bf16[272,512]{1,0:T(8,128)(2,1)S(1)}, bf16[272,512]{1,0:T(8,128)(2,1)S(1)}, u32[]{:S(2)}, u32[]{:S(2)}) %collective-permute-start.57) | collective-permute-done | bytes 278560 | tf_op jit(solution)/shard_map/ppermute | solution.py:1046
  255.2 1.3 dynamic_slice.11.grad
  256.5 5.3 %update.1 = (f32[256592]{0:T(1024)}, f32[256592]{0:T(1024)}, f32[256592]{0:T(1024)}, f32[8,128]{1,0:T(8,128)}) custom-call(s32[6]{0:T(128)} %pad_add_fusion.1.segments, f32[256592]{0:T(1024)} %params.3, f32[256592]{0:T(1024)} %first.1, f32[256592]{0:T(1024)} %second.1, f32[256592]{0:T(1024)} %dynamic_slice.11.grad), custom_call_target="tpu_custom_call" | custom-call | tf_op jit(solution)/shard_map/update/pallas_call | solution.py:1395
  261.8 1.4 collective-permute-done.60
  264.8 2.7 collective-permute-done.61
  267.6 3.5 %collective-permute-done.62 = f32[8,128]{1,0:T(8,128)S(1)} collective-permute-done((f32[8,128]{1,0:T(8,128)S(1)}, f32[8,128]{1,0:T(8,128)S(1)}, u32[]{:S(2)}, u32[]{:S(2)}) %collective-permute-start.62) | collective-permute-done | bytes 4128 | tf_op jit(solution)/shard_map/ppermute | solution.py:1038
  271.1 3.6 %collective-permute-done.63 = f32[8,128]{1,0:T(8,128)S(1)} collective-permute-done((f32[8,128]{1,0:T(8,128)S(1)}, f32[8,128]{1,0:T(8,128)S(1)}, u32[]{:S(2)}, u32[]{:S(2)}) %collective-permute-start.63) | collective-permute-done | bytes 4128 | tf_op jit(solution)/shard_map/ppermute | solution.py:1050
  276.2 3.0 %collective-permute-done.64 = f32[8,128]{1,0:T(8,128)S(1)} collective-permute-done((f32[8,128]{1,0:T(8,128)S(1)}, f32[8,128]{1,0:T(8,128)S(1)}, u32[]{:S(2)}, u32[]{:S(2)}) %collective-permute-start.64) | collective-permute-done | bytes 4128 | tf_op jit(solution)/shard_map/ppermute | solution.py:1050
  279.8 3.5 %apply.1 = (f32[256592]{0:T(1024)}, f32[12]{0:T(128)}, f32[12]{0:T(128)}, f32[12]{0:T(128)}) custom-call(s32[6]{0:T(128)} %pad_add_fusion.1.segments, f32[8,128]{1,0:T(8,128)} %add.241.sums, f32[256592]{0:T(1024)} %params.3, f32[256592]{0:T(1024)} %get-tuple-element.228.update), custom_call_target="tpu_custom_call" | custom-call | tf_op jit(solution)/shard_map/apply/pallas_call | solution.py:1405
  (222 shorter events, 30.7 us)
Async XLA Ops:
  2.8 15.3 %collective-permute-start.2 = (bf16[528,512]{1,0:T(8,128)(2,1)S(1)}, bf16[528,512]{1,0:T(8,128)(2,1)S(1)}, u32[]{:S(2)}, u32[]{:S(2)}) collective-permute-start(bf16[528,512]{1,0:T(8,128)(2,1)S(1)} %reshape.49.refs_4_), channel_id=1, source_target_pairs={{0,16},{8,24},{16,0},{24,8},{1,17},{9,25},{17,1},{25,9},{2,18},{10... | collective-permute-start | bytes 1622024 | tf_op jit(solution)/shard_map/ppermute | solution.py:1038
  5.8 13.7 %collective-permute-start.1 = (bf16[528,512]{1,0:T(8,128)(2,1)S(1)}, bf16[528,512]{1,0:T(8,128)(2,1)S(1)}, u32[]{:S(2)}, u32[]{:S(2)}) collective-permute-start(bf16[528,512]{1,0:T(8,128)(2,1)S(1)} %reshape.49.refs_4_), channel_id=1, source_target_pairs={{0,1},{1,0},{2,3},{3,2},{4,5},{5,4},{6,7},{7,6},{8,9},{9,8},{10,11... | collective-permute-start | bytes 1622024 | tf_op jit(solution)/shard_map/ppermute | solution.py:1034
  7.3 15.3 %collective-permute-start = (bf16[528,512]{1,0:T(8,128)(2,1)S(1)}, bf16[528,512]{1,0:T(8,128)(2,1)S(1)}, u32[]{:S(2)}, u32[]{:S(2)}) collective-permute-start(bf16[528,512]{1,0:T(8,128)(2,1)S(1)} %reshape.49.refs_4_), channel_id=1, source_target_pairs={{0,2},{1,3},{2,4},{3,5},{4,6},{5,7},{6,0},{7,1},{8,10},{9,11},{10,... | collective-permute-start | bytes 1622024 | tf_op jit(solution)/shard_map/ppermute | solution.py:1046
  22.6 12.6 %collective-permute-start.5 = (bf16[528,512]{1,0:T(8,128)(2,1)S(1)}, bf16[528,512]{1,0:T(8,128)(2,1)S(1)}, u32[]{:S(2)}, u32[]{:S(2)}) collective-permute-start(bf16[528,512]{1,0:T(8,128)(2,1)S(1)} %collective-permute-done.refs_5_), channel_id=1, source_target_pairs={{0,16},{8,24},{16,0},{24,8},{1,17},{9,25},{17,1},{25,9},{2,18},{10... | collective-permute-start | bytes 1622024 | tf_op jit(solution)/shard_map/ppermute | solution.py:1038
  23.1 12.3 %collective-permute-start.4 = (bf16[528,512]{1,0:T(8,128)(2,1)S(1)}, bf16[528,512]{1,0:T(8,128)(2,1)S(1)}, u32[]{:S(2)}, u32[]{:S(2)}) collective-permute-start(bf16[528,512]{1,0:T(8,128)(2,1)S(1)} %collective-permute-done.refs_5_), channel_id=1, source_target_pairs={{0,1},{1,0},{2,3},{3,2},{4,5},{5,4},{6,7},{7,6},{8,9},{9,8},{10,11... | collective-permute-start | bytes 1622024 | tf_op jit(solution)/shard_map/ppermute | solution.py:1034
  23.6 14.1 %collective-permute-start.3 = (bf16[528,512]{1,0:T(8,128)(2,1)S(1)}, bf16[528,512]{1,0:T(8,128)(2,1)S(1)}, u32[]{:S(2)}, u32[]{:S(2)}) collective-permute-start(bf16[528,512]{1,0:T(8,128)(2,1)S(1)} %collective-permute-done.refs_5_), channel_id=1, source_target_pairs={{0,2},{1,3},{2,4},{3,5},{4,6},{5,7},{6,0},{7,1},{8,10},{9,11},{10,... | collective-permute-start | bytes 1622024 | tf_op jit(solution)/shard_map/ppermute | solution.py:1046
  37.7 13.1 %collective-permute-start.6 = (bf16[528,512]{1,0:T(8,128)(2,1)S(1)}, bf16[528,512]{1,0:T(8,128)(2,1)S(1)}, u32[]{:S(2)}, u32[]{:S(2)}) collective-permute-start(bf16[528,512]{1,0:T(8,128)(2,1)S(1)} %collective-permute-done.3.refs_6_), channel_id=1, source_target_pairs={{0,2},{1,3},{2,4},{3,5},{4,6},{5,7},{6,0},{7,1},{8,10},{9,11},{10,... | collective-permute-start | bytes 1622024 | tf_op jit(solution)/shard_map/ppermute | solution.py:1046
  37.8 20.9 %collective-permute-start.7 = (bf16[784,512]{1,0:T(8,128)(2,1)S(1)}, bf16[784,512]{1,0:T(8,128)(2,1)S(1)}, u32[]{:S(2)}, u32[]{:S(2)}) collective-permute-start(bf16[784,512]{1,0:T(8,128)(2,1)S(1)} %pad_maximum_fusion.2), channel_id=1, source_target_pairs={{0,1},{1,0},{2,3},{3,2},{4,5},{5,4},{6,7},{7,6},{8,9},{9,8},{10,11... | collective-permute-start | bytes 2408456 | tf_op jit(solution)/shard_map/ppermute | solution.py:1034
  39.2 19.5 %collective-permute-start.9 = (bf16[800,512]{1,0:T(8,128)(2,1)S(1)}, bf16[800,512]{1,0:T(8,128)(2,1)S(1)}, u32[]{:S(2)}, u32[]{:S(2)}) collective-permute-start(bf16[800,512]{1,0:T(8,128)(2,1)S(1)} %pad_maximum_fusion), channel_id=1, source_target_pairs={{0,16},{8,24},{16,0},{24,8},{1,17},{9,25},{17,1},{25,9},{2,18},{10... | collective-permute-start | bytes 2457608 | tf_op jit(solution)/shard_map/ppermute | solution.py:1038
  50.9 21.2 %collective-permute-start.8 = (bf16[784,512]{1,0:T(8,128)(2,1)S(1)}, bf16[784,512]{1,0:T(8,128)(2,1)S(1)}, u32[]{:S(2)}, u32[]{:S(2)}) collective-permute-start(bf16[784,512]{1,0:T(8,128)(2,1)S(1)} %pad_maximum_fusion.3), channel_id=1, source_target_pairs={{0,1},{1,0},{2,3},{3,2},{4,5},{5,4},{6,7},{7,6},{8,9},{9,8},{10,11... | collective-permute-start | bytes 2408456 | tf_op jit(solution)/shard_map/ppermute | solution.py:1034
  52.0 1.9 collective-permute-start.13
  52.1 21.7 %collective-permute-start.10 = (bf16[800,512]{1,0:T(8,128)(2,1)S(1)}, bf16[800,512]{1,0:T(8,128)(2,1)}, u32[]{:S(2)}, u32[]{:S(2)}) collective-permute-start(bf16[800,512]{1,0:T(8,128)(2,1)S(1)} %pad_maximum_fusion.1), channel_id=1, source_target_pairs={{0,16},{8,24},{16,0},{24,8},{1,17},{9,25},{17,1},{25,9},{2,18},{10... | collective-permute-start | bytes 2457608 | tf_op jit(solution)/shard_map/ppermute | solution.py:1038
  53.9 20.9 %collective-permute-start.17 = (bf16[528,512]{1,0:T(8,128)(2,1)S(1)}, bf16[528,512]{1,0:T(8,128)(2,1)S(1)}, u32[]{:S(2)}, u32[]{:S(2)}) collective-permute-start(bf16[528,512]{1,0:T(8,128)(2,1)S(1)} %collective-permute-done.1.refs_8_), channel_id=1, source_target_pairs={{0,8},{8,0},{16,24},{24,16},{1,9},{9,1},{17,25},{25,17},{2,10},{10... | collective-permute-start | bytes 1622024 | tf_op jit(solution)/shard_map/ppermute | solution.py:1042
  58.7 17.8 %collective-permute-start.22 = (bf16[528,512]{1,0:T(8,128)(2,1)S(1)}, bf16[528,512]{1,0:T(8,128)(2,1)S(1)}, u32[]{:S(2)}, u32[]{:S(2)}) collective-permute-start(bf16[528,512]{1,0:T(8,128)(2,1)S(1)} %collective-permute-done.2.refs_13_), channel_id=1, source_target_pairs={{0,8},{8,0},{16,24},{24,16},{1,9},{9,1},{17,25},{25,17},{2,10},{10... | collective-permute-start | bytes 1622024 | tf_op jit(solution)/shard_map/ppermute | solution.py:1042
  58.8 18.1 %collective-permute-start.14 = (bf16[528,512]{1,0:T(8,128)(2,1)S(1)}, bf16[528,512]{1,0:T(8,128)(2,1)S(1)}, u32[]{:S(2)}, u32[]{:S(2)}) collective-permute-start(bf16[528,512]{1,0:T(8,128)(2,1)S(1)} %collective-permute-done.refs_5_), channel_id=1, source_target_pairs={{0,8},{8,0},{16,24},{24,16},{1,9},{9,1},{17,25},{25,17},{2,10},{10... | collective-permute-start | bytes 1622024 | tf_op jit(solution)/shard_map/ppermute | solution.py:1042
  72.1 5.3 %collective-permute-start.18 = (bf16[528,512]{1,0:T(8,128)(2,1)S(1)}, bf16[528,512]{1,0:T(8,128)(2,1)S(1)}, u32[]{:S(2)}, u32[]{:S(2)}) collective-permute-start(bf16[528,512]{1,0:T(8,128)(2,1)S(1)} %collective-permute-done.4.refs_9_), channel_id=1, source_target_pairs={{0,8},{8,0},{16,24},{24,16},{1,9},{9,1},{17,25},{25,17},{2,10},{10... | collective-permute-start | bytes 1622024 | tf_op jit(solution)/shard_map/ppermute | solution.py:1042
  73.8 3.7 %collective-permute-start.23 = (bf16[528,512]{1,0:T(8,128)(2,1)S(1)}, bf16[528,512]{1,0:T(8,128)(2,1)S(1)}, u32[]{:S(2)}, u32[]{:S(2)}) collective-permute-start(bf16[528,512]{1,0:T(8,128)(2,1)S(1)} %copy-done.13), channel_id=1, source_target_pairs={{0,8},{8,0},{16,24},{24,16},{1,9},{9,1},{17,25},{25,17},{2,10},{10... | collective-permute-start | bytes 1622024 | tf_op jit(solution)/shard_map/ppermute | solution.py:1042
  74.9 16.2 %collective-permute-start.12 = (bf16[544,512]{1,0:T(8,128)(2,1)S(1)}, bf16[544,512]{1,0:T(8,128)(2,1)}, u32[]{:S(2)}, u32[]{:S(2)}) collective-permute-start(bf16[544,512]{1,0:T(8,128)(2,1)S(1)} %pad_maximum_fusion.4), channel_id=1, source_target_pairs={{0,16},{8,24},{16,0},{24,8},{1,17},{9,25},{17,1},{25,9},{2,18},{10... | collective-permute-start | bytes 1671176 | tf_op jit(solution)/shard_map/ppermute | solution.py:1038
  76.5 15.0 %collective-permute-start.15 = (bf16[528,512]{1,0:T(8,128)(2,1)S(1)}, bf16[528,512]{1,0:T(8,128)(2,1)S(1)}, u32[]{:S(2)}, u32[]{:S(2)}) collective-permute-start(bf16[528,512]{1,0:T(8,128)(2,1)S(1)} %collective-permute-done.3.refs_6_), channel_id=1, source_target_pairs={{0,8},{8,0},{16,24},{24,16},{1,9},{9,1},{17,25},{25,17},{2,10},{10... | collective-permute-start | bytes 1622024 | tf_op jit(solution)/shard_map/ppermute | solution.py:1042
  76.8 14.2 %collective-permute-start.11 = (bf16[512,512]{1,0:T(8,128)(2,1)S(1)}, bf16[512,512]{1,0:T(8,128)(2,1)}, u32[]{:S(2)}, u32[]{:S(2)}) collective-permute-start(bf16[512,512]{1,0:T(8,128)(2,1)S(1)} %pad_maximum_fusion.5), channel_id=1, source_target_pairs={{0,1},{1,0},{2,3},{3,2},{4,5},{5,4},{6,7},{7,6},{8,9},{9,8},{10,11... | collective-permute-start | bytes 1572872 | tf_op jit(solution)/shard_map/ppermute | solution.py:1034
  77.4 14.8 %collective-permute-start.20 = (bf16[784,512]{1,0:T(8,128)(2,1)S(1)}, bf16[784,512]{1,0:T(8,128)(2,1)S(1)}, u32[]{:S(2)}, u32[]{:S(2)}) collective-permute-start(bf16[784,512]{1,0:T(8,128)(2,1)S(1)} %collective-permute-done.8.refs_11_), channel_id=1, source_target_pairs={{0,8},{8,0},{16,24},{24,16},{1,9},{9,1},{17,25},{25,17},{2,10},{10... | collective-permute-start | bytes 2408456 | tf_op jit(solution)/shard_map/ppermute | solution.py:1042
  77.5 14.2 %collective-permute-start.16 = (bf16[528,512]{1,0:T(8,128)(2,1)S(1)}, bf16[528,512]{1,0:T(8,128)(2,1)S(1)}, u32[]{:S(2)}, u32[]{:S(2)}) collective-permute-start(bf16[528,512]{1,0:T(8,128)(2,1)S(1)} %collective-permute-done.6.refs_7_), channel_id=1, source_target_pairs={{0,8},{8,0},{16,24},{24,16},{1,9},{9,1},{17,25},{25,17},{2,10},{10... | collective-permute-start | bytes 1622024 | tf_op jit(solution)/shard_map/ppermute | solution.py:1042
  91.1 6.3 %collective-permute-start.25 = (bf16[800,512]{1,0:T(8,128)(2,1)}, bf16[800,512]{1,0:T(8,128)(2,1)S(1)}, u32[]{:S(2)}, u32[]{:S(2)}) collective-permute-start(bf16[800,512]{1,0:T(8,128)(2,1)} %collective-permute-done.10.refs_16_), channel_id=1, source_target_pairs={{0,8},{8,0},{16,24},{24,16},{1,9},{9,1},{17,25},{25,17},{2,10},{10... | collective-permute-start | bytes 2457608 | tf_op jit(solution)/shard_map/ppermute | solution.py:1042
  91.1 6.3 %collective-permute-start.24 = (bf16[800,512]{1,0:T(8,128)(2,1)S(1)}, bf16[800,512]{1,0:T(8,128)(2,1)}, u32[]{:S(2)}, u32[]{:S(2)}) collective-permute-start(bf16[800,512]{1,0:T(8,128)(2,1)S(1)} %collective-permute-done.9.refs_15_), channel_id=1, source_target_pairs={{0,8},{8,0},{16,24},{24,16},{1,9},{9,1},{17,25},{25,17},{2,10},{10... | collective-permute-start | bytes 2457608 | tf_op jit(solution)/shard_map/ppermute | solution.py:1042
  91.6 5.8 %collective-permute-start.19 = (bf16[784,512]{1,0:T(8,128)(2,1)S(1)}, bf16[784,512]{1,0:T(8,128)(2,1)}, u32[]{:S(2)}, u32[]{:S(2)}) collective-permute-start(bf16[784,512]{1,0:T(8,128)(2,1)S(1)} %collective-permute-done.7.refs_10_), channel_id=1, source_target_pairs={{0,8},{8,0},{16,24},{24,16},{1,9},{9,1},{17,25},{25,17},{2,10},{10... | collective-permute-start | bytes 2408456 | tf_op jit(solution)/shard_map/ppermute | solution.py:1042
  91.7 5.7 %collective-permute-start.26 = (bf16[544,512]{1,0:T(8,128)(2,1)}, bf16[544,512]{1,0:T(8,128)(2,1)}, u32[]{:S(2)}, u32[]{:S(2)}) collective-permute-start(bf16[544,512]{1,0:T(8,128)(2,1)} %collective-permute-done.12.refs_17_), channel_id=1, source_target_pairs={{0,8},{8,0},{16,24},{24,16},{1,9},{9,1},{17,25},{25,17},{2,10},{10... | collective-permute-start | bytes 1671176 | tf_op jit(solution)/shard_map/ppermute | solution.py:1042
  93.4 3.9 %collective-permute-start.21 = (bf16[512,512]{1,0:T(8,128)(2,1)}, bf16[512,512]{1,0:T(8,128)(2,1)S(1)}, u32[]{:S(2)}, u32[]{:S(2)}) collective-permute-start(bf16[512,512]{1,0:T(8,128)(2,1)} %collective-permute-done.11.refs_12_), channel_id=1, source_target_pairs={{0,8},{8,0},{16,24},{24,16},{1,9},{9,1},{17,25},{25,17},{2,10},{10... | collective-permute-start | bytes 1572872 | tf_op jit(solution)/shard_map/ppermute | solution.py:1042
  140.9 15.5 %collective-permute-start.28 = (bf16[4,528,512]{2,1,0:T(8,128)(2,1)}, bf16[4,528,512]{2,1,0:T(8,128)(2,1)S(1)}, u32[]{:S(2)}, u32[]{:S(2)}) collective-permute-start(bf16[4,528,512]{2,1,0:T(8,128)(2,1)} %get-tuple-element.156), channel_id=1, source_target_pairs={{0,8},{8,0},{16,24},{24,16},{1,9},{9,1},{17,25},{25,17},{2,10},{10... | collective-permute-start | bytes 6488072 | tf_op jit(solution)/shard_map/ppermute | solution.py:1042
  155.9 6.0 %collective-permute-start.27 = (bf16[4,528,512]{2,1,0:T(8,128)(2,1)}, bf16[4,528,512]{2,1,0:T(8,128)(2,1)}, u32[]{:S(2)}, u32[]{:S(2)}) collective-permute-start(bf16[4,528,512]{2,1,0:T(8,128)(2,1)} %get-tuple-element.154), channel_id=1, source_target_pairs={{0,8},{8,0},{16,24},{24,16},{1,9},{9,1},{17,25},{25,17},{2,10},{10... | collective-permute-start | bytes 6488072 | tf_op jit(solution)/shard_map/ppermute | solution.py:1042
  156.3 18.8 %collective-permute-start.32 = (bf16[4,528,512]{2,1,0:T(8,128)(2,1)}, bf16[4,528,512]{2,1,0:T(8,128)(2,1)S(1)}, u32[]{:S(2)}, u32[]{:S(2)}) collective-permute-start(bf16[4,528,512]{2,1,0:T(8,128)(2,1)} %get-tuple-element.169), channel_id=1, source_target_pairs={{0,8},{8,0},{16,24},{24,16},{1,9},{9,1},{17,25},{25,17},{2,10},{10... | collective-permute-start | bytes 6488072 | tf_op jit(solution)/shard_map/ppermute | solution.py:1042
  165.9 9.2 %collective-permute-start.31 = (bf16[4,528,512]{2,1,0:T(8,128)(2,1)}, bf16[4,528,512]{2,1,0:T(8,128)(2,1)S(1)}, u32[]{:S(2)}, u32[]{:S(2)}) collective-permute-start(bf16[4,528,512]{2,1,0:T(8,128)(2,1)} %get-tuple-element.168), channel_id=1, source_target_pairs={{0,8},{8,0},{16,24},{24,16},{1,9},{9,1},{17,25},{25,17},{2,10},{10... | collective-permute-start | bytes 6488072 | tf_op jit(solution)/shard_map/ppermute | solution.py:1042
  166.3 29.9 %collective-permute-start.29 = (bf16[2,528,512]{2,1,0:T(8,128)(2,1)}, bf16[2,528,512]{2,1,0:T(8,128)(2,1)S(1)}, u32[]{:S(2)}, u32[]{:S(2)}) collective-permute-start(bf16[2,528,512]{2,1,0:T(8,128)(2,1)} %get-tuple-element.157), channel_id=1, source_target_pairs={{0,1},{1,0},{2,3},{3,2},{4,5},{5,4},{6,7},{7,6},{8,9},{9,8},{10,11... | collective-permute-start | bytes 3244040 | tf_op jit(solution)/shard_map/ppermute | solution.py:1034
  168.0 28.2 %collective-permute-start.30 = (bf16[2,528,512]{2,1,0:T(8,128)(2,1)}, bf16[2,528,512]{2,1,0:T(8,128)(2,1)}, u32[]{:S(2)}, u32[]{:S(2)}) collective-permute-start(bf16[2,528,512]{2,1,0:T(8,128)(2,1)} %get-tuple-element.158), channel_id=1, source_target_pairs={{0,16},{8,24},{16,0},{24,8},{1,17},{9,25},{17,1},{25,9},{2,18},{10... | collective-permute-start | bytes 3244040 | tf_op jit(solution)/shard_map/ppermute | solution.py:1038
  187.5 3.9 %collective-permute-start.34 = (f32[16,512]{1,0:T(8,128)S(1)}, f32[16,512]{1,0:T(8,128)S(1)}, u32[]{:S(2)}, u32[]{:S(2)}) collective-permute-start(f32[16,512]{1,0:T(8,128)S(1)} %add.199), channel_id=1, source_target_pairs={{0,2},{1,3},{2,0},{3,1},{4,6},{5,7},{6,4},{7,5},{8,10},{9,11},{10,... | collective-permute-start | bytes 98312 | tf_op jit(solution)/shard_map/ppermute | solution.py:1050
  191.4 4.8 %collective-permute-start.35 = (f32[16,512]{1,0:T(8,128)S(1)}, f32[16,512]{1,0:T(8,128)S(1)}, u32[]{:S(2)}, u32[]{:S(2)}) collective-permute-start(f32[16,512]{1,0:T(8,128)S(1)} %add.200), channel_id=1, source_target_pairs={{0,4},{1,5},{2,6},{3,7},{4,0},{5,1},{6,2},{7,3},{8,12},{9,13},{10,... | collective-permute-start | bytes 98312 | tf_op jit(solution)/shard_map/ppermute | solution.py:1050
  196.3 20.7 %collective-permute-start.58 = (f32[16,512]{1,0:T(8,128)S(1)}, f32[16,512]{1,0:T(8,128)S(1)}, u32[]{:S(2)}, u32[]{:S(2)}) collective-permute-start(f32[16,512]{1,0:T(8,128)S(1)} %add.201), channel_id=1, source_target_pairs={{0,1},{1,0},{2,3},{3,2},{4,5},{5,4},{6,7},{7,6},{8,9},{9,8},{10,11... | collective-permute-start | bytes 98312 | tf_op jit(solution)/shard_map/ppermute | solution.py:1034
  197.4 9.4 %collective-permute-start.37 = (bf16[256,512]{1,0:T(8,128)(2,1)}, bf16[256,512]{1,0:T(8,128)(2,1)S(1)}, u32[]{:S(2)}, u32[]{:S(2)}) collective-permute-start(bf16[256,512]{1,0:T(8,128)(2,1)} %get-tuple-element.194), channel_id=1, source_target_pairs={{0,16},{8,24},{16,0},{24,8},{1,17},{9,25},{17,1},{25,9},{2,18},{10... | collective-permute-start | bytes 786440 | tf_op jit(solution)/shard_map/ppermute | solution.py:1038
  198.1 14.5 %collective-permute-start.48 = (bf16[272,512]{1,0:T(8,128)(2,1)}, bf16[272,512]{1,0:T(8,128)(2,1)S(1)}, u32[]{:S(2)}, u32[]{:S(2)}) collective-permute-start(bf16[272,512]{1,0:T(8,128)(2,1)} %get-tuple-element.213), channel_id=1, source_target_pairs={{0,16},{8,24},{16,0},{24,8},{1,17},{9,25},{17,1},{25,9},{2,18},{10... | collective-permute-start | bytes 835592 | tf_op jit(solution)/shard_map/ppermute | solution.py:1038
  200.6 9.3 %collective-permute-start.36 = (bf16[256,512]{1,0:T(8,128)(2,1)S(1)}, bf16[256,512]{1,0:T(8,128)(2,1)S(1)}, u32[]{:S(2)}, u32[]{:S(2)}) collective-permute-start(bf16[256,512]{1,0:T(8,128)(2,1)S(1)} %get-tuple-element.238), channel_id=1, source_target_pairs={{0,1},{1,0},{2,3},{3,2},{4,5},{5,4},{6,7},{7,6},{8,9},{9,8},{10,11... | collective-permute-start | bytes 786440 | tf_op jit(solution)/shard_map/ppermute | solution.py:1034
  202.9 13.0 %collective-permute-start.47 = (bf16[272,512]{1,0:T(8,128)(2,1)S(1)}, bf16[272,512]{1,0:T(8,128)(2,1)S(1)}, u32[]{:S(2)}, u32[]{:S(2)}) collective-permute-start(bf16[272,512]{1,0:T(8,128)(2,1)S(1)} %get-tuple-element.242), channel_id=1, source_target_pairs={{0,1},{1,0},{2,3},{3,2},{4,5},{5,4},{6,7},{7,6},{8,9},{9,8},{10,11... | collective-permute-start | bytes 835592 | tf_op jit(solution)/shard_map/ppermute | solution.py:1034
  209.9 11.6 %collective-permute-start.38 = (bf16[256,512]{1,0:T(8,128)(2,1)S(1)}, bf16[256,512]{1,0:T(8,128)(2,1)S(1)}, u32[]{:S(2)}, u32[]{:S(2)}) collective-permute-start(bf16[256,512]{1,0:T(8,128)(2,1)S(1)} %get-tuple-element.195), channel_id=1, source_target_pairs={{0,1},{1,0},{2,3},{3,2},{4,5},{5,4},{6,7},{7,6},{8,9},{9,8},{10,11... | collective-permute-start | bytes 786440 | tf_op jit(solution)/shard_map/ppermute | solution.py:1034
  210.9 12.7 %collective-permute-start.39 = (bf16[256,512]{1,0:T(8,128)(2,1)S(1)}, bf16[256,512]{1,0:T(8,128)(2,1)S(1)}, u32[]{:S(2)}, u32[]{:S(2)}) collective-permute-start(bf16[256,512]{1,0:T(8,128)(2,1)S(1)} %copy-done.48), channel_id=1, source_target_pairs={{0,16},{8,24},{16,0},{24,8},{1,17},{9,25},{17,1},{25,9},{2,18},{10... | collective-permute-start | bytes 786440 | tf_op jit(solution)/shard_map/ppermute | solution.py:1038
  212.6 11.0 %collective-permute-start.44 = (bf16[256,512]{1,0:T(8,128)(2,1)S(1)}, bf16[256,512]{1,0:T(8,128)(2,1)S(1)}, u32[]{:S(2)}, u32[]{:S(2)}) collective-permute-start(bf16[256,512]{1,0:T(8,128)(2,1)S(1)} %add_convert_fusion.5), channel_id=1, source_target_pairs={{0,2},{1,3},{2,4},{3,5},{4,6},{5,7},{6,0},{7,1},{8,10},{9,11},{10,... | collective-permute-start | bytes 786440 | tf_op jit(solution)/shard_map/ppermute | solution.py:1046
  215.9 11.1 %collective-permute-start.49 = (bf16[272,512]{1,0:T(8,128)(2,1)S(1)}, bf16[272,512]{1,0:T(8,128)(2,1)S(1)}, u32[]{:S(2)}, u32[]{:S(2)}) collective-permute-start(bf16[272,512]{1,0:T(8,128)(2,1)S(1)} %get-tuple-element.214), channel_id=1, source_target_pairs={{0,1},{1,0},{2,3},{3,2},{4,5},{5,4},{6,7},{7,6},{8,9},{9,8},{10,11... | collective-permute-start | bytes 835592 | tf_op jit(solution)/shard_map/ppermute | solution.py:1034
  217.0 11.6 %collective-permute-start.50 = (bf16[272,512]{1,0:T(8,128)(2,1)S(1)}, bf16[272,512]{1,0:T(8,128)(2,1)S(1)}, u32[]{:S(2)}, u32[]{:S(2)}) collective-permute-start(bf16[272,512]{1,0:T(8,128)(2,1)S(1)} %copy-done.46), channel_id=1, source_target_pairs={{0,16},{8,24},{16,0},{24,8},{1,17},{9,25},{17,1},{25,9},{2,18},{10... | collective-permute-start | bytes 835592 | tf_op jit(solution)/shard_map/ppermute | solution.py:1038
  221.5 10.9 %collective-permute-start.55 = (bf16[272,512]{1,0:T(8,128)(2,1)S(1)}, bf16[272,512]{1,0:T(8,128)(2,1)S(1)}, u32[]{:S(2)}, u32[]{:S(2)}) collective-permute-start(bf16[272,512]{1,0:T(8,128)(2,1)S(1)} %add_convert_fusion.2), channel_id=1, source_target_pairs={{0,2},{1,3},{2,4},{3,5},{4,6},{5,7},{6,0},{7,1},{8,10},{9,11},{10,... | collective-permute-start | bytes 835592 | tf_op jit(solution)/shard_map/ppermute | solution.py:1046
  223.6 9.7 %collective-permute-start.59 = (f32[16,512]{1,0:T(8,128)S(1)}, f32[16,512]{1,0:T(8,128)S(1)}, u32[]{:S(2)}, u32[]{:S(2)}) collective-permute-start(f32[16,512]{1,0:T(8,128)S(1)} %add.232), channel_id=1, source_target_pairs={{0,16},{8,24},{16,0},{24,8},{1,17},{9,25},{17,1},{25,9},{2,18},{10... | collective-permute-start | bytes 98312 | tf_op jit(solution)/shard_map/ppermute | solution.py:1038
  223.7 9.7 %collective-permute-start.40 = (bf16[256,512]{1,0:T(8,128)(2,1)S(1)}, bf16[256,512]{1,0:T(8,128)(2,1)S(1)}, u32[]{:S(2)}, u32[]{:S(2)}) collective-permute-start(bf16[256,512]{1,0:T(8,128)(2,1)S(1)} %copy-done.47), channel_id=1, source_target_pairs={{0,1},{1,0},{2,3},{3,2},{4,5},{5,4},{6,7},{7,6},{8,9},{9,8},{10,11... | collective-permute-start | bytes 786440 | tf_op jit(solution)/shard_map/ppermute | solution.py:1034
  227.0 11.2 %collective-permute-start.45 = (bf16[256,512]{1,0:T(8,128)(2,1)S(1)}, bf16[256,512]{1,0:T(8,128)(2,1)S(1)}, u32[]{:S(2)}, u32[]{:S(2)}) collective-permute-start(bf16[256,512]{1,0:T(8,128)(2,1)S(1)} %add_convert_fusion.4), channel_id=1, source_target_pairs={{0,2},{1,3},{2,4},{3,5},{4,6},{5,7},{6,0},{7,1},{8,10},{9,11},{10,... | collective-permute-start | bytes 786440 | tf_op jit(solution)/shard_map/ppermute | solution.py:1046
  228.6 8.7 %collective-permute-start.41 = (bf16[256,512]{1,0:T(8,128)(2,1)}, bf16[256,512]{1,0:T(8,128)(2,1)S(1)}, u32[]{:S(2)}, u32[]{:S(2)}) collective-permute-start(bf16[256,512]{1,0:T(8,128)(2,1)} %get-tuple-element.201), channel_id=1, source_target_pairs={{0,16},{8,24},{16,0},{24,8},{1,17},{9,25},{17,1},{25,9},{2,18},{10... | collective-permute-start | bytes 786440 | tf_op jit(solution)/shard_map/ppermute | solution.py:1038
  232.4 9.6 %collective-permute-start.51 = (bf16[272,512]{1,0:T(8,128)(2,1)}, bf16[272,512]{1,0:T(8,128)(2,1)S(1)}, u32[]{:S(2)}, u32[]{:S(2)}) collective-permute-start(bf16[272,512]{1,0:T(8,128)(2,1)} %get-tuple-element.217), channel_id=1, source_target_pairs={{0,1},{1,0},{2,3},{3,2},{4,5},{5,4},{6,7},{7,6},{8,9},{9,8},{10,11... | collective-permute-start | bytes 835592 | tf_op jit(solution)/shard_map/ppermute | solution.py:1034
  233.3 10.7 %collective-permute-start.56 = (bf16[272,512]{1,0:T(8,128)(2,1)S(1)}, bf16[272,512]{1,0:T(8,128)(2,1)S(1)}, u32[]{:S(2)}, u32[]{:S(2)}) collective-permute-start(bf16[272,512]{1,0:T(8,128)(2,1)S(1)} %add_convert_fusion.1), channel_id=1, source_target_pairs={{0,2},{1,3},{2,4},{3,5},{4,6},{5,7},{6,0},{7,1},{8,10},{9,11},{10,... | collective-permute-start | bytes 835592 | tf_op jit(solution)/shard_map/ppermute | solution.py:1046
  233.4 9.7 %collective-permute-start.52 = (bf16[272,512]{1,0:T(8,128)(2,1)S(1)}, bf16[272,512]{1,0:T(8,128)(2,1)S(1)}, u32[]{:S(2)}, u32[]{:S(2)}) collective-permute-start(bf16[272,512]{1,0:T(8,128)(2,1)S(1)} %get-tuple-element.219), channel_id=1, source_target_pairs={{0,16},{8,24},{16,0},{24,8},{1,17},{9,25},{17,1},{25,9},{2,18},{10... | collective-permute-start | bytes 835592 | tf_op jit(solution)/shard_map/ppermute | solution.py:1038
  237.3 9.0 %collective-permute-start.42 = (bf16[256,512]{1,0:T(8,128)(2,1)}, bf16[256,512]{1,0:T(8,128)(2,1)S(1)}, u32[]{:S(2)}, u32[]{:S(2)}) collective-permute-start(bf16[256,512]{1,0:T(8,128)(2,1)} %get-tuple-element.202), channel_id=1, source_target_pairs={{0,1},{1,0},{2,3},{3,2},{4,5},{5,4},{6,7},{7,6},{8,9},{9,8},{10,11... | collective-permute-start | bytes 786440 | tf_op jit(solution)/shard_map/ppermute | solution.py:1034
  238.1 8.6 %collective-permute-start.43 = (bf16[256,512]{1,0:T(8,128)(2,1)}, bf16[256,512]{1,0:T(8,128)(2,1)S(1)}, u32[]{:S(2)}, u32[]{:S(2)}) collective-permute-start(bf16[256,512]{1,0:T(8,128)(2,1)} %get-tuple-element.204), channel_id=1, source_target_pairs={{0,16},{8,24},{16,0},{24,8},{1,17},{9,25},{17,1},{25,9},{2,18},{10... | collective-permute-start | bytes 786440 | tf_op jit(solution)/shard_map/ppermute | solution.py:1038
  242.0 8.2 %collective-permute-start.46 = (bf16[256,512]{1,0:T(8,128)(2,1)S(1)}, bf16[256,512]{1,0:T(8,128)(2,1)S(1)}, u32[]{:S(2)}, u32[]{:S(2)}) collective-permute-start(bf16[256,512]{1,0:T(8,128)(2,1)S(1)} %add_convert_fusion.3), channel_id=1, source_target_pairs={{0,2},{1,3},{2,4},{3,5},{4,6},{5,7},{6,0},{7,1},{8,10},{9,11},{10,... | collective-permute-start | bytes 786440 | tf_op jit(solution)/shard_map/ppermute | solution.py:1046
  243.1 7.2 %collective-permute-start.53 = (bf16[272,512]{1,0:T(8,128)(2,1)}, bf16[272,512]{1,0:T(8,128)(2,1)S(1)}, u32[]{:S(2)}, u32[]{:S(2)}) collective-permute-start(bf16[272,512]{1,0:T(8,128)(2,1)} %get-tuple-element.220), channel_id=1, source_target_pairs={{0,1},{1,0},{2,3},{3,2},{4,5},{5,4},{6,7},{7,6},{8,9},{9,8},{10,11... | collective-permute-start | bytes 835592 | tf_op jit(solution)/shard_map/ppermute | solution.py:1034
  244.0 6.6 %collective-permute-start.54 = (bf16[272,512]{1,0:T(8,128)(2,1)S(1)}, bf16[272,512]{1,0:T(8,128)(2,1)S(1)}, u32[]{:S(2)}, u32[]{:S(2)}) collective-permute-start(bf16[272,512]{1,0:T(8,128)(2,1)S(1)} %get-tuple-element.222), channel_id=1, source_target_pairs={{0,16},{8,24},{16,0},{24,8},{1,17},{9,25},{17,1},{25,9},{2,18},{10... | collective-permute-start | bytes 835592 | tf_op jit(solution)/shard_map/ppermute | solution.py:1038
  246.3 8.4 %collective-permute-start.57 = (bf16[272,512]{1,0:T(8,128)(2,1)S(1)}, bf16[272,512]{1,0:T(8,128)(2,1)S(1)}, u32[]{:S(2)}, u32[]{:S(2)}) collective-permute-start(bf16[272,512]{1,0:T(8,128)(2,1)S(1)} %add_convert_fusion), channel_id=1, source_target_pairs={{0,2},{1,3},{2,4},{3,5},{4,6},{5,7},{6,0},{7,1},{8,10},{9,11},{10,... | collective-permute-start | bytes 835592 | tf_op jit(solution)/shard_map/ppermute | solution.py:1046
  261.8 1.4 collective-permute-start.60
  263.9 3.6 %collective-permute-start.61 = (f32[8,128]{1,0:T(8,128)S(1)}, f32[8,128]{1,0:T(8,128)S(1)}, u32[]{:S(2)}, u32[]{:S(2)}) collective-permute-start(f32[8,128]{1,0:T(8,128)S(1)} %add.237), channel_id=1, source_target_pairs={{0,1},{1,0},{2,3},{3,2},{4,5},{5,4},{6,7},{7,6},{8,9},{9,8},{10,11... | collective-permute-start | bytes 12296 | tf_op jit(solution)/shard_map/ppermute | solution.py:1034
  267.5 3.6 %collective-permute-start.62 = (f32[8,128]{1,0:T(8,128)S(1)}, f32[8,128]{1,0:T(8,128)S(1)}, u32[]{:S(2)}, u32[]{:S(2)}) collective-permute-start(f32[8,128]{1,0:T(8,128)S(1)} %add.238), channel_id=1, source_target_pairs={{0,16},{8,24},{16,0},{24,8},{1,17},{9,25},{17,1},{25,9},{2,18},{10... | collective-permute-start | bytes 12296 | tf_op jit(solution)/shard_map/ppermute | solution.py:1038
  271.1 3.6 %collective-permute-start.63 = (f32[8,128]{1,0:T(8,128)S(1)}, f32[8,128]{1,0:T(8,128)S(1)}, u32[]{:S(2)}, u32[]{:S(2)}) collective-permute-start(f32[8,128]{1,0:T(8,128)S(1)} %add.239), channel_id=1, source_target_pairs={{0,2},{1,3},{2,0},{3,1},{4,6},{5,7},{6,4},{7,5},{8,10},{9,11},{10,... | collective-permute-start | bytes 12296 | tf_op jit(solution)/shard_map/ppermute | solution.py:1050
  274.7 4.5 %collective-permute-start.64 = (f32[8,128]{1,0:T(8,128)S(1)}, f32[8,128]{1,0:T(8,128)S(1)}, u32[]{:S(2)}, u32[]{:S(2)}) collective-permute-start(f32[8,128]{1,0:T(8,128)S(1)} %add.240), channel_id=1, source_target_pairs={{0,4},{1,5},{2,6},{3,7},{4,0},{5,1},{6,2},{7,3},{8,12},{9,13},{10,... | collective-permute-start | bytes 12296 | tf_op jit(solution)/shard_map/ppermute | solution.py:1050
  (52 other events, 811.6 us)

commit v3 on v2

--- a/solution.py
+++ b/solution.py
@@ -1197,13 +1197,13 @@
     for_y, for_x = chip_sum(False, 1, range(4), 2)
     from_x, from_y = over_x(for_x), over_y(for_y)
     low_near = over_core(after(back["low_near"], for_x, for_y))
-    to_x, to_y, mine = [
-        chip_sum(own_half, x, range(4), SIDES) for own_half, x in ((True, 1), (False, 0), (True, 0))
-    ]
-    late = after(back["late"], mine[3][1], to_x[3][1], to_y[3][1])
+    late = after(back["late"], for_x, for_y)
     late = late + over_core(late)
     late = late + over_z(late, 1)
-    late = late + over_z(late, 2)
+    to_x = chip_sum(True, 1, range(4), SIDES)
+    to_y = chip_sum(False, 0, range(4), SIDES)
+    mine = chip_sum(True, 0, range(4), SIDES)
+    late = late + over_z(after(late, mine[3][1], to_y[3][1], to_x[3][1]), 2)
     from_x, from_y, to_x, to_y, mine, late = lax.optimization_barrier((from_x, from_y, to_x, to_y, mine, late))
     late = late + over_x(late)
     late = late + over_y(late)

time: 284 us -> 283 us (level)
  starting transfers between devices: 49.2 us -> 54.7 us
  waiting for transfers between devices: 131 us -> 126 us
    ppermute x4, waiting for transfers between devices: 13.3 us -> 7.69 us  [over_z(): return lax.ppermute(value, 'fsdp', [(i, i ^ 2 * step) for i in range(8)])]
    ppermute x16, starting transfers between devices: 19.6 us -> 25 us  [over_y(): return lax.ppermute(value, 'dp', [(i, i ^ 2) for i in range(4)])]
    ppermute x9, starting transfers between devices: 6.2 us -> 2.99 us  [round_z(): return lax.ppermute(value, 'fsdp', [(i, (i + 2) % 8) for i in range(8)])]
    ppermute x16, waiting for transfers between devices: 31.9 us -> 34.8 us  [over_y(): return lax.ppermute(value, 'dp', [(i, i ^ 2) for i in range(4)])]
    ppermute x4, starting transfers between devices: 2.83 us -> 5.78 us  [over_z(): return lax.ppermute(value, 'fsdp', [(i, i ^ 2 * step) for i in range(8)])]
    unnamed x101 -> x99, local copies, waits for them, and re-layouts: 6.05 us -> 4.7 us
  transfers between devices with their start and end apart: 65 -> 65, of which waited for: 35 -> 38; matrix products, arithmetic and copies ran while one was open for 3% -> 3% of each run, Pallas kernels for 11% -> 11%
where the time goes in v3:
time: 283 us
  waiting for transfers between devices  126 us (45%)
  Pallas kernels  82.3 us (29%)
  starting transfers between devices  54.7 us (19%)
  other arithmetic  9.42 us (3%)
  local copies, waits for them, and re-layouts  7.9 us (3%)
    pallas_call x6, Pallas kernels, call(): pl.pallas_call(kernel, name=name, in_specs=[space for space, _ in ins], o...  73.5 us
    ppermute x16, waiting for transfers between devices, over_x(): return lax.ppermute(value, 'fsdp', [(i, i ^ 1) for i in range(8)])  47 us
    ppermute x16, waiting for transfers between devices, over_y(): return lax.ppermute(value, 'dp', [(i, i ^ 2) for i in range(4)])  34.8 us
    ppermute x9, waiting for transfers between devices, round_z(): return lax.ppermute(value, 'fsdp', [(i, (i + 2) % 8) for i in range(8)])  26 us
    ppermute x16, starting transfers between devices, over_y(): return lax.ppermute(value, 'dp', [(i, i ^ 2) for i in range(4)])  25 us
    ppermute x16, starting transfers between devices, over_x(): return lax.ppermute(value, 'fsdp', [(i, i ^ 1) for i in range(8)])  16.5 us
    ppermute x20, waiting for transfers between devices, over_core(): return lax.ppermute(value, 'dp', [(i, i ^ 1) for i in range(4)])  10.7 us
    ppermute x4, waiting for transfers between devices, over_z(): return lax.ppermute(value, 'fsdp', [(i, i ^ 2 * step) for i in range(8)])  7.69 us
  transfers between devices with their start and end apart: 65, of which 38 were waited for; matrix products, arithmetic and copies ran while one was open for 3% of the time, Pallas kernels for 11%

profile of v3, /device:TPU:0, one launch (start us, length us, event | category | flops | bytes accessed | tf_op | source)
XLA Modules:
  0.0 282.8 jit_solution(12474393324639754615)
XLA Ops:
  0.7 1.3 convert_element_type.246
  2.8 3.0 %collective-permute-start.2 = (bf16[528,512]{1,0:T(8,128)(2,1)S(1)}, bf16[528,512]{1,0:T(8,128)(2,1)S(1)}, u32[]{:S(2)}, u32[]{:S(2)}) collective-permute-start(bf16[528,512]{1,0:T(8,128)(2,1)S(1)} %reshape.49.refs_4_), channel_id=1, source_target_pairs={{0,16},{8,24},{16,0},{24,8},{1,17},{9,25},{17,1},{25,9},{2,18},{10... | collective-permute-start | bytes 1622024 | tf_op jit(solution)/shard_map/ppermute | solution.py:1038
  5.8 1.5 collective-permute-start.1
  7.3 1.6 collective-permute-start
  8.9 9.2 %collective-permute-done.2.refs_13_ = bf16[528,512]{1,0:T(8,128)(2,1)S(1)} collective-permute-done((bf16[528,512]{1,0:T(8,128)(2,1)S(1)}, bf16[528,512]{1,0:T(8,128)(2,1)S(1)}, u32[]{:S(2)}, u32[]{:S(2)}) %collective-permute-start.2) | collective-permute-done | bytes 540704 | tf_op jit(solution)/shard_map/ppermute | solution.py:1038
  18.1 1.5 collective-permute-done.1.refs_8_
  19.5 3.1 %collective-permute-done.refs_5_ = bf16[528,512]{1,0:T(8,128)(2,1)S(1)} collective-permute-done((bf16[528,512]{1,0:T(8,128)(2,1)S(1)}, bf16[528,512]{1,0:T(8,128)(2,1)S(1)}, u32[]{:S(2)}, u32[]{:S(2)}) %collective-permute-start) | collective-permute-done | bytes 540704 | tf_op jit(solution)/shard_map/ppermute | solution.py:1046
  23.6 11.5 %collective-permute-done.5.refs_14_ = bf16[528,512]{1,0:T(8,128)(2,1)S(1)} collective-permute-done((bf16[528,512]{1,0:T(8,128)(2,1)S(1)}, bf16[528,512]{1,0:T(8,128)(2,1)S(1)}, u32[]{:S(2)}, u32[]{:S(2)}) %collective-permute-start.5) | collective-permute-done | bytes 540704 | tf_op jit(solution)/shard_map/ppermute | solution.py:1038
  35.4 2.3 collective-permute-done.3.refs_6_
  37.8 1.3 collective-permute-start.7
  39.2 1.6 collective-permute-start.9
  40.8 10.0 %collective-permute-done.6.refs_7_ = bf16[528,512]{1,0:T(8,128)(2,1)S(1)} collective-permute-done((bf16[528,512]{1,0:T(8,128)(2,1)S(1)}, bf16[528,512]{1,0:T(8,128)(2,1)S(1)}, u32[]{:S(2)}, u32[]{:S(2)}) %collective-permute-start.6) | collective-permute-done | bytes 540704 | tf_op jit(solution)/shard_map/ppermute | solution.py:1046
  52.1 1.6 collective-permute-start.10
  54.1 4.6 %collective-permute-done.7.refs_10_ = bf16[784,512]{1,0:T(8,128)(2,1)S(1)} collective-permute-done((bf16[784,512]{1,0:T(8,128)(2,1)S(1)}, bf16[784,512]{1,0:T(8,128)(2,1)S(1)}, u32[]{:S(2)}, u32[]{:S(2)}) %collective-permute-start.7) | collective-permute-done | bytes 802848 | tf_op jit(solution)/shard_map/ppermute | solution.py:1034
  59.3 12.8 %collective-permute-done.8.refs_11_ = bf16[784,512]{1,0:T(8,128)(2,1)S(1)} collective-permute-done((bf16[784,512]{1,0:T(8,128)(2,1)S(1)}, bf16[784,512]{1,0:T(8,128)(2,1)S(1)}, u32[]{:S(2)}, u32[]{:S(2)}) %collective-permute-start.8) | collective-permute-done | bytes 802848 | tf_op jit(solution)/shard_map/ppermute | solution.py:1034
  72.1 1.7 collective-permute-done.10.refs_16_
  74.9 1.6 collective-permute-start.12
  78.0 13.0 %collective-permute-done.11.refs_12_ = bf16[512,512]{1,0:T(8,128)(2,1)} collective-permute-done((bf16[512,512]{1,0:T(8,128)(2,1)S(1)}, bf16[512,512]{1,0:T(8,128)(2,1)}, u32[]{:S(2)}, u32[]{:S(2)}) %collective-permute-start.11) | collective-permute-done | bytes 524320 | tf_op jit(solution)/shard_map/ppermute | solution.py:1034
  95.1 2.3 collective-permute-done.19.refs_24_
  98.5 42.5 %forward.1 = (bf16[160,512]{1,0:T(8,128)(2,1)}, f32[8,512]{1,0:T(8,128)}, f32[176,512]{1,0:T(8,128)}, bf16[8,528,512]{2,1,0:T(8,128)(2,1)}, bf16[4,528,512]{2,1,...) custom-call(s32[4]{0:T(128)} %pad_add_fusion.refs_0_.coords, ...), custom_call_target="tpu_custom_call" | custom-call | tf_op jit(solution)/shard_map/forward/pallas_call | solution.py:972
  141.2 14.6 %backward.1 = (bf16[160,512]{1,0:T(8,128)(2,1)}, f32[16,512]{1,0:T(8,128)}, bf16[8,528,512]{2,1,0:T(8,128)(2,1)}, bf16[4,528,512]{2,1,0:T(8,128)(2,1)}, bf16[4,528,512]{2,1,0:T(8,128)(2,1)}) custom-call(s32[4]{0:T(128)} %pad_add_fusion.refs_0_.coords, bf16[160,512]{1,0:T(8,128)(2,1)} %bitcast.41, ...), custom_call_target="tpu_custom_call", output_to_operand_aliasing={{2}: (18, {}), {3}: (19, {}), {4}: (20, {})} | custom-call | tf_op jit(solution)/shard_map/backward/pallas_call | solution.py:972
  156.5 5.5 %collective-permute-done.27.low_got = bf16[4,528,512]{2,1,0:T(8,128)(2,1)} collective-permute-done((bf16[4,528,512]{2,1,0:T(8,128)(2,1)}, bf16[4,528,512]{2,1,0:T(8,128)(2,1)}, u32[]{:S(2)}, u32[]{:S(2)}) %collective-permute-start.27) | collective-permute-done | bytes 2162720 | tf_op jit(solution)/shard_map/ppermute | solution.py:1042
  162.0 4.1 %span_sums.4 = (bf16[2,528,512]{2,1,0:T(8,128)(2,1)}, bf16[2,528,512]{2,1,0:T(8,128)(2,1)}) custom-call(s32[4]{0:T(128)} %pad_add_fusion.refs_0_.coords, bf16[8,528,512]{2,1,0:T(8,128)(2,1)} %get-tuple-element.154.low_kept, bf16[4,528,512]{2,1,0:T(8,128)(2,1)} %collective-permute-done.27.low_got, bf16[8,528,512]{2,1,0:T(8,128)(2,1)} %get-tuple-element.156.high_kept, ...), custom_call_target="tpu_custom_call" | custom-call | tf_op jit(solution)/shard_map/span_sums/pallas_call | solution.py:972
  166.5 1.6 collective-permute-start.29
  168.1 3.1 %collective-permute-start.30 = (bf16[2,528,512]{2,1,0:T(8,128)(2,1)}, bf16[2,528,512]{2,1,0:T(8,128)(2,1)}, u32[]{:S(2)}, u32[]{:S(2)}) collective-permute-start(bf16[2,528,512]{2,1,0:T(8,128)(2,1)} %get-tuple-element.159), channel_id=1, source_target_pairs={{0,16},{8,24},{16,0},{24,8},{1,17},{9,25},{17,1},{25,9},{2,18},{10... | collective-permute-start | bytes 3244040 | tf_op jit(solution)/shard_map/ppermute | solution.py:1038
  171.2 1.2 collective-permute-done.33
  172.4 4.0 %span_sums.5 = (bf16[256,512]{1,0:T(8,128)(2,1)}, bf16[272,512]{1,0:T(8,128)(2,1)}, bf16[256,512]{1,0:T(8,128)(2,1)}, bf16[272,512]{1,0:T(8,128)(2,1)}, bf16[256...) custom-call(s32[4]{0:T(128)} %pad_add_fusion.refs_0_.coords, ...), custom_call_target="tpu_custom_call" | custom-call | tf_op jit(solution)/shard_map/span_sums/pallas_call | solution.py:972
  176.5 1.3 copy-done
  177.8 4.0 %span_sums.7 = (bf16[256,512]{1,0:T(8,128)(2,1)}, bf16[272,512]{1,0:T(8,128)(2,1)}, bf16[256,512]{1,0:T(8,128)(2,1)}, bf16[272,512]{1,0:T(8,128)(2,1)}, bf16[256...) custom-call(s32[4]{0:T(128)} %pad_add_fusion.refs_0_.coords, ...), custom_call_target="tpu_custom_call" | custom-call | tf_op jit(solution)/shard_map/span_sums/pallas_call | solution.py:972
  181.8 4.4 %span_sums.6 = (bf16[256,512]{1,0:T(8,128)(2,1)}, bf16[272,512]{1,0:T(8,128)(2,1)}, bf16[256,512]{1,0:T(8,128)(2,1)}, bf16[272,512]{1,0:T(8,128)(2,1)}, bf16[256...) custom-call(s32[4]{0:T(128)} %pad_add_fusion.refs_0_.coords, ...), custom_call_target="tpu_custom_call" | custom-call | tf_op jit(solution)/shard_map/span_sums/pallas_call | solution.py:972
  186.3 4.1 %collective-permute-start.35 = (f32[16,512]{1,0:T(8,128)S(1)}, f32[16,512]{1,0:T(8,128)S(1)}, u32[]{:S(2)}, u32[]{:S(2)}) collective-permute-start(f32[16,512]{1,0:T(8,128)S(1)} %add.200), channel_id=1, source_target_pairs={{0,4},{1,5},{2,6},{3,7},{4,0},{5,1},{6,2},{7,3},{8,12},{9,13},{10,... | collective-permute-start | bytes 98312 | tf_op jit(solution)/shard_map/ppermute | solution.py:1050
  190.5 1.8 collective-permute-done.35
  192.7 2.7 collective-permute-done.30
  195.4 1.1 collective-permute-start.58
  196.5 1.7 collective-permute-start.37
  198.5 1.2 fusion.8
  200.7 1.2 fusion.4
  201.9 1.2 collective-permute-start.47
  203.2 2.7 collective-permute-done.37
  205.9 3.1 %collective-permute-done.36 = bf16[256,512]{1,0:T(8,128)(2,1)S(1)} collective-permute-done((bf16[256,512]{1,0:T(8,128)(2,1)S(1)}, bf16[256,512]{1,0:T(8,128)(2,1)S(1)}, u32[]{:S(2)}, u32[]{:S(2)}) %collective-permute-start.36) | collective-permute-done | bytes 262176 | tf_op jit(solution)/shard_map/ppermute | solution.py:1034
  209.9 1.7 collective-permute-start.39
  211.9 3.1 %collective-permute-done.47 = bf16[272,512]{1,0:T(8,128)(2,1)S(1)} collective-permute-done((bf16[272,512]{1,0:T(8,128)(2,1)S(1)}, bf16[272,512]{1,0:T(8,128)(2,1)S(1)}, u32[]{:S(2)}, u32[]{:S(2)}) %collective-permute-start.47) | collective-permute-done | bytes 278560 | tf_op jit(solution)/shard_map/ppermute | solution.py:1034
  216.0 1.8 collective-permute-start.50
  217.8 2.7 collective-permute-done.38
  221.5 1.8 collective-permute-start.59
  224.4 2.1 collective-permute-done.49
  226.5 1.7 collective-permute-start.41
  228.3 3.6 %collective-permute-done.55 = bf16[272,512]{1,0:T(8,128)(2,1)S(1)} collective-permute-done((bf16[272,512]{1,0:T(8,128)(2,1)S(1)}, bf16[272,512]{1,0:T(8,128)(2,1)S(1)}, u32[]{:S(2)}, u32[]{:S(2)}) %collective-permute-start.55) | collective-permute-done | bytes 278560 | tf_op jit(solution)/shard_map/ppermute | solution.py:1046
  233.1 1.8 collective-permute-start.52
  236.2 1.2 collective-permute-start.42
  240.1 1.8 collective-permute-done.52
  242.9 1.3 collective-permute-done.56
  246.9 2.2 collective-permute-done.46
  249.3 1.5 collective-permute-done.54
  250.8 3.3 %collective-permute-done.57 = bf16[272,512]{1,0:T(8,128)(2,1)S(1)} collective-permute-done((bf16[272,512]{1,0:T(8,128)(2,1)S(1)}, bf16[272,512]{1,0:T(8,128)(2,1)S(1)}, u32[]{:S(2)}, u32[]{:S(2)}) %collective-permute-start.57) | collective-permute-done | bytes 278560 | tf_op jit(solution)/shard_map/ppermute | solution.py:1046
  254.6 1.3 dynamic_slice.11.grad
  255.9 5.3 %update.1 = (f32[256592]{0:T(1024)}, f32[256592]{0:T(1024)}, f32[256592]{0:T(1024)}, f32[8,128]{1,0:T(8,128)}) custom-call(s32[6]{0:T(128)} %pad_add_fusion.1.segments, f32[256592]{0:T(1024)} %params.3, f32[256592]{0:T(1024)} %first.1, f32[256592]{0:T(1024)} %second.1, f32[256592]{0:T(1024)} %dynamic_slice.11.grad), custom_call_target="tpu_custom_call" | custom-call | tf_op jit(solution)/shard_map/update/pallas_call | solution.py:1395
  261.2 1.4 collective-permute-done.60
  264.2 2.7 collective-permute-done.61
  267.6 2.8 %collective-permute-done.62 = f32[8,128]{1,0:T(8,128)S(1)} collective-permute-done((f32[8,128]{1,0:T(8,128)S(1)}, f32[8,128]{1,0:T(8,128)S(1)}, u32[]{:S(2)}, u32[]{:S(2)}) %collective-permute-start.62) | collective-permute-done | bytes 4128 | tf_op jit(solution)/shard_map/ppermute | solution.py:1038
  270.5 3.6 %collective-permute-done.63 = f32[8,128]{1,0:T(8,128)S(1)} collective-permute-done((f32[8,128]{1,0:T(8,128)S(1)}, f32[8,128]{1,0:T(8,128)S(1)}, u32[]{:S(2)}, u32[]{:S(2)}) %collective-permute-start.63) | collective-permute-done | bytes 4128 | tf_op jit(solution)/shard_map/ppermute | solution.py:1050
  274.1 1.6 collective-permute-start.64
  276.3 2.3 collective-permute-done.64
  279.2 3.5 %apply.1 = (f32[256592]{0:T(1024)}, f32[12]{0:T(128)}, f32[12]{0:T(128)}, f32[12]{0:T(128)}) custom-call(s32[6]{0:T(128)} %pad_add_fusion.1.segments, f32[8,128]{1,0:T(8,128)} %add.241.sums, f32[256592]{0:T(1024)} %params.3, f32[256592]{0:T(1024)} %get-tuple-element.230.update), custom_call_target="tpu_custom_call" | custom-call | tf_op jit(solution)/shard_map/apply/pallas_call | solution.py:1405
  (220 shorter events, 31.9 us)
Async XLA Ops:
  2.8 15.3 %collective-permute-start.2 = (bf16[528,512]{1,0:T(8,128)(2,1)S(1)}, bf16[528,512]{1,0:T(8,128)(2,1)S(1)}, u32[]{:S(2)}, u32[]{:S(2)}) collective-permute-start(bf16[528,512]{1,0:T(8,128)(2,1)S(1)} %reshape.49.refs_4_), channel_id=1, source_target_pairs={{0,16},{8,24},{16,0},{24,8},{1,17},{9,25},{17,1},{25,9},{2,18},{10... | collective-permute-start | bytes 1622024 | tf_op jit(solution)/shard_map/ppermute | solution.py:1038
  5.8 13.7 %collective-permute-start.1 = (bf16[528,512]{1,0:T(8,128)(2,1)S(1)}, bf16[528,512]{1,0:T(8,128)(2,1)S(1)}, u32[]{:S(2)}, u32[]{:S(2)}) collective-permute-start(bf16[528,512]{1,0:T(8,128)(2,1)S(1)} %reshape.49.refs_4_), channel_id=1, source_target_pairs={{0,1},{1,0},{2,3},{3,2},{4,5},{5,4},{6,7},{7,6},{8,9},{9,8},{10,11... | collective-permute-start | bytes 1622024 | tf_op jit(solution)/shard_map/ppermute | solution.py:1034
  7.3 15.3 %collective-permute-start = (bf16[528,512]{1,0:T(8,128)(2,1)S(1)}, bf16[528,512]{1,0:T(8,128)(2,1)S(1)}, u32[]{:S(2)}, u32[]{:S(2)}) collective-permute-start(bf16[528,512]{1,0:T(8,128)(2,1)S(1)} %reshape.49.refs_4_), channel_id=1, source_target_pairs={{0,2},{1,3},{2,4},{3,5},{4,6},{5,7},{6,0},{7,1},{8,10},{9,11},{10,... | collective-permute-start | bytes 1622024 | tf_op jit(solution)/shard_map/ppermute | solution.py:1046
  22.6 12.6 %collective-permute-start.5 = (bf16[528,512]{1,0:T(8,128)(2,1)S(1)}, bf16[528,512]{1,0:T(8,128)(2,1)S(1)}, u32[]{:S(2)}, u32[]{:S(2)}) collective-permute-start(bf16[528,512]{1,0:T(8,128)(2,1)S(1)} %collective-permute-done.refs_5_), channel_id=1, source_target_pairs={{0,16},{8,24},{16,0},{24,8},{1,17},{9,25},{17,1},{25,9},{2,18},{10... | collective-permute-start | bytes 1622024 | tf_op jit(solution)/shard_map/ppermute | solution.py:1038
  23.1 12.3 %collective-permute-start.4 = (bf16[528,512]{1,0:T(8,128)(2,1)S(1)}, bf16[528,512]{1,0:T(8,128)(2,1)S(1)}, u32[]{:S(2)}, u32[]{:S(2)}) collective-permute-start(bf16[528,512]{1,0:T(8,128)(2,1)S(1)} %collective-permute-done.refs_5_), channel_id=1, source_target_pairs={{0,1},{1,0},{2,3},{3,2},{4,5},{5,4},{6,7},{7,6},{8,9},{9,8},{10,11... | collective-permute-start | bytes 1622024 | tf_op jit(solution)/shard_map/ppermute | solution.py:1034
  23.6 14.1 %collective-permute-start.3 = (bf16[528,512]{1,0:T(8,128)(2,1)S(1)}, bf16[528,512]{1,0:T(8,128)(2,1)S(1)}, u32[]{:S(2)}, u32[]{:S(2)}) collective-permute-start(bf16[528,512]{1,0:T(8,128)(2,1)S(1)} %collective-permute-done.refs_5_), channel_id=1, source_target_pairs={{0,2},{1,3},{2,4},{3,5},{4,6},{5,7},{6,0},{7,1},{8,10},{9,11},{10,... | collective-permute-start | bytes 1622024 | tf_op jit(solution)/shard_map/ppermute | solution.py:1046
  37.7 13.1 %collective-permute-start.6 = (bf16[528,512]{1,0:T(8,128)(2,1)S(1)}, bf16[528,512]{1,0:T(8,128)(2,1)S(1)}, u32[]{:S(2)}, u32[]{:S(2)}) collective-permute-start(bf16[528,512]{1,0:T(8,128)(2,1)S(1)} %collective-permute-done.3.refs_6_), channel_id=1, source_target_pairs={{0,2},{1,3},{2,4},{3,5},{4,6},{5,7},{6,0},{7,1},{8,10},{9,11},{10,... | collective-permute-start | bytes 1622024 | tf_op jit(solution)/shard_map/ppermute | solution.py:1046
  37.8 20.9 %collective-permute-start.7 = (bf16[784,512]{1,0:T(8,128)(2,1)S(1)}, bf16[784,512]{1,0:T(8,128)(2,1)S(1)}, u32[]{:S(2)}, u32[]{:S(2)}) collective-permute-start(bf16[784,512]{1,0:T(8,128)(2,1)S(1)} %pad_maximum_fusion.2), channel_id=1, source_target_pairs={{0,1},{1,0},{2,3},{3,2},{4,5},{5,4},{6,7},{7,6},{8,9},{9,8},{10,11... | collective-permute-start | bytes 2408456 | tf_op jit(solution)/shard_map/ppermute | solution.py:1034
  39.2 19.5 %collective-permute-start.9 = (bf16[800,512]{1,0:T(8,128)(2,1)S(1)}, bf16[800,512]{1,0:T(8,128)(2,1)S(1)}, u32[]{:S(2)}, u32[]{:S(2)}) collective-permute-start(bf16[800,512]{1,0:T(8,128)(2,1)S(1)} %pad_maximum_fusion), channel_id=1, source_target_pairs={{0,16},{8,24},{16,0},{24,8},{1,17},{9,25},{17,1},{25,9},{2,18},{10... | collective-permute-start | bytes 2457608 | tf_op jit(solution)/shard_map/ppermute | solution.py:1038
  50.9 21.2 %collective-permute-start.8 = (bf16[784,512]{1,0:T(8,128)(2,1)S(1)}, bf16[784,512]{1,0:T(8,128)(2,1)S(1)}, u32[]{:S(2)}, u32[]{:S(2)}) collective-permute-start(bf16[784,512]{1,0:T(8,128)(2,1)S(1)} %pad_maximum_fusion.3), channel_id=1, source_target_pairs={{0,1},{1,0},{2,3},{3,2},{4,5},{5,4},{6,7},{7,6},{8,9},{9,8},{10,11... | collective-permute-start | bytes 2408456 | tf_op jit(solution)/shard_map/ppermute | solution.py:1034
  52.0 1.9 collective-permute-start.13
  52.1 21.7 %collective-permute-start.10 = (bf16[800,512]{1,0:T(8,128)(2,1)S(1)}, bf16[800,512]{1,0:T(8,128)(2,1)}, u32[]{:S(2)}, u32[]{:S(2)}) collective-permute-start(bf16[800,512]{1,0:T(8,128)(2,1)S(1)} %pad_maximum_fusion.1), channel_id=1, source_target_pairs={{0,16},{8,24},{16,0},{24,8},{1,17},{9,25},{17,1},{25,9},{2,18},{10... | collective-permute-start | bytes 2457608 | tf_op jit(solution)/shard_map/ppermute | solution.py:1038
  53.9 20.9 %collective-permute-start.17 = (bf16[528,512]{1,0:T(8,128)(2,1)S(1)}, bf16[528,512]{1,0:T(8,128)(2,1)S(1)}, u32[]{:S(2)}, u32[]{:S(2)}) collective-permute-start(bf16[528,512]{1,0:T(8,128)(2,1)S(1)} %collective-permute-done.1.refs_8_), channel_id=1, source_target_pairs={{0,8},{8,0},{16,24},{24,16},{1,9},{9,1},{17,25},{25,17},{2,10},{10... | collective-permute-start | bytes 1622024 | tf_op jit(solution)/shard_map/ppermute | solution.py:1042
  58.7 17.8 %collective-permute-start.22 = (bf16[528,512]{1,0:T(8,128)(2,1)S(1)}, bf16[528,512]{1,0:T(8,128)(2,1)S(1)}, u32[]{:S(2)}, u32[]{:S(2)}) collective-permute-start(bf16[528,512]{1,0:T(8,128)(2,1)S(1)} %collective-permute-done.2.refs_13_), channel_id=1, source_target_pairs={{0,8},{8,0},{16,24},{24,16},{1,9},{9,1},{17,25},{25,17},{2,10},{10... | collective-permute-start | bytes 1622024 | tf_op jit(solution)/shard_map/ppermute | solution.py:1042
  58.8 18.1 %collective-permute-start.14 = (bf16[528,512]{1,0:T(8,128)(2,1)S(1)}, bf16[528,512]{1,0:T(8,128)(2,1)S(1)}, u32[]{:S(2)}, u32[]{:S(2)}) collective-permute-start(bf16[528,512]{1,0:T(8,128)(2,1)S(1)} %collective-permute-done.refs_5_), channel_id=1, source_target_pairs={{0,8},{8,0},{16,24},{24,16},{1,9},{9,1},{17,25},{25,17},{2,10},{10... | collective-permute-start | bytes 1622024 | tf_op jit(solution)/shard_map/ppermute | solution.py:1042
  72.1 5.3 %collective-permute-start.18 = (bf16[528,512]{1,0:T(8,128)(2,1)S(1)}, bf16[528,512]{1,0:T(8,128)(2,1)S(1)}, u32[]{:S(2)}, u32[]{:S(2)}) collective-permute-start(bf16[528,512]{1,0:T(8,128)(2,1)S(1)} %collective-permute-done.4.refs_9_), channel_id=1, source_target_pairs={{0,8},{8,0},{16,24},{24,16},{1,9},{9,1},{17,25},{25,17},{2,10},{10... | collective-permute-start | bytes 1622024 | tf_op jit(solution)/shard_map/ppermute | solution.py:1042
  73.8 3.7 %collective-permute-start.23 = (bf16[528,512]{1,0:T(8,128)(2,1)S(1)}, bf16[528,512]{1,0:T(8,128)(2,1)S(1)}, u32[]{:S(2)}, u32[]{:S(2)}) collective-permute-start(bf16[528,512]{1,0:T(8,128)(2,1)S(1)} %copy-done.12), channel_id=1, source_target_pairs={{0,8},{8,0},{16,24},{24,16},{1,9},{9,1},{17,25},{25,17},{2,10},{10... | collective-permute-start | bytes 1622024 | tf_op jit(solution)/shard_map/ppermute | solution.py:1042
  74.9 16.2 %collective-permute-start.12 = (bf16[544,512]{1,0:T(8,128)(2,1)S(1)}, bf16[544,512]{1,0:T(8,128)(2,1)}, u32[]{:S(2)}, u32[]{:S(2)}) collective-permute-start(bf16[544,512]{1,0:T(8,128)(2,1)S(1)} %pad_maximum_fusion.4), channel_id=1, source_target_pairs={{0,16},{8,24},{16,0},{24,8},{1,17},{9,25},{17,1},{25,9},{2,18},{10... | collective-permute-start | bytes 1671176 | tf_op jit(solution)/shard_map/ppermute | solution.py:1038
  76.5 15.0 %collective-permute-start.15 = (bf16[528,512]{1,0:T(8,128)(2,1)S(1)}, bf16[528,512]{1,0:T(8,128)(2,1)S(1)}, u32[]{:S(2)}, u32[]{:S(2)}) collective-permute-start(bf16[528,512]{1,0:T(8,128)(2,1)S(1)} %collective-permute-done.3.refs_6_), channel_id=1, source_target_pairs={{0,8},{8,0},{16,24},{24,16},{1,9},{9,1},{17,25},{25,17},{2,10},{10... | collective-permute-start | bytes 1622024 | tf_op jit(solution)/shard_map/ppermute | solution.py:1042
  76.8 14.2 %collective-permute-start.11 = (bf16[512,512]{1,0:T(8,128)(2,1)S(1)}, bf16[512,512]{1,0:T(8,128)(2,1)}, u32[]{:S(2)}, u32[]{:S(2)}) collective-permute-start(bf16[512,512]{1,0:T(8,128)(2,1)S(1)} %pad_maximum_fusion.5), channel_id=1, source_target_pairs={{0,1},{1,0},{2,3},{3,2},{4,5},{5,4},{6,7},{7,6},{8,9},{9,8},{10,11... | collective-permute-start | bytes 1572872 | tf_op jit(solution)/shard_map/ppermute | solution.py:1034
  77.4 14.8 %collective-permute-start.20 = (bf16[784,512]{1,0:T(8,128)(2,1)S(1)}, bf16[784,512]{1,0:T(8,128)(2,1)S(1)}, u32[]{:S(2)}, u32[]{:S(2)}) collective-permute-start(bf16[784,512]{1,0:T(8,128)(2,1)S(1)} %collective-permute-done.8.refs_11_), channel_id=1, source_target_pairs={{0,8},{8,0},{16,24},{24,16},{1,9},{9,1},{17,25},{25,17},{2,10},{10... | collective-permute-start | bytes 2408456 | tf_op jit(solution)/shard_map/ppermute | solution.py:1042
  77.5 14.2 %collective-permute-start.16 = (bf16[528,512]{1,0:T(8,128)(2,1)S(1)}, bf16[528,512]{1,0:T(8,128)(2,1)S(1)}, u32[]{:S(2)}, u32[]{:S(2)}) collective-permute-start(bf16[528,512]{1,0:T(8,128)(2,1)S(1)} %collective-permute-done.6.refs_7_), channel_id=1, source_target_pairs={{0,8},{8,0},{16,24},{24,16},{1,9},{9,1},{17,25},{25,17},{2,10},{10... | collective-permute-start | bytes 1622024 | tf_op jit(solution)/shard_map/ppermute | solution.py:1042
  91.1 6.3 %collective-permute-start.25 = (bf16[800,512]{1,0:T(8,128)(2,1)}, bf16[800,512]{1,0:T(8,128)(2,1)S(1)}, u32[]{:S(2)}, u32[]{:S(2)}) collective-permute-start(bf16[800,512]{1,0:T(8,128)(2,1)} %collective-permute-done.10.refs_16_), channel_id=1, source_target_pairs={{0,8},{8,0},{16,24},{24,16},{1,9},{9,1},{17,25},{25,17},{2,10},{10... | collective-permute-start | bytes 2457608 | tf_op jit(solution)/shard_map/ppermute | solution.py:1042
  91.1 6.3 %collective-permute-start.24 = (bf16[800,512]{1,0:T(8,128)(2,1)S(1)}, bf16[800,512]{1,0:T(8,128)(2,1)}, u32[]{:S(2)}, u32[]{:S(2)}) collective-permute-start(bf16[800,512]{1,0:T(8,128)(2,1)S(1)} %collective-permute-done.9.refs_15_), channel_id=1, source_target_pairs={{0,8},{8,0},{16,24},{24,16},{1,9},{9,1},{17,25},{25,17},{2,10},{10... | collective-permute-start | bytes 2457608 | tf_op jit(solution)/shard_map/ppermute | solution.py:1042
  91.6 5.8 %collective-permute-start.19 = (bf16[784,512]{1,0:T(8,128)(2,1)S(1)}, bf16[784,512]{1,0:T(8,128)(2,1)}, u32[]{:S(2)}, u32[]{:S(2)}) collective-permute-start(bf16[784,512]{1,0:T(8,128)(2,1)S(1)} %collective-permute-done.7.refs_10_), channel_id=1, source_target_pairs={{0,8},{8,0},{16,24},{24,16},{1,9},{9,1},{17,25},{25,17},{2,10},{10... | collective-permute-start | bytes 2408456 | tf_op jit(solution)/shard_map/ppermute | solution.py:1042
  91.7 5.7 %collective-permute-start.26 = (bf16[544,512]{1,0:T(8,128)(2,1)}, bf16[544,512]{1,0:T(8,128)(2,1)}, u32[]{:S(2)}, u32[]{:S(2)}) collective-permute-start(bf16[544,512]{1,0:T(8,128)(2,1)} %collective-permute-done.12.refs_17_), channel_id=1, source_target_pairs={{0,8},{8,0},{16,24},{24,16},{1,9},{9,1},{17,25},{25,17},{2,10},{10... | collective-permute-start | bytes 1671176 | tf_op jit(solution)/shard_map/ppermute | solution.py:1042
  93.5 3.9 %collective-permute-start.21 = (bf16[512,512]{1,0:T(8,128)(2,1)}, bf16[512,512]{1,0:T(8,128)(2,1)S(1)}, u32[]{:S(2)}, u32[]{:S(2)}) collective-permute-start(bf16[512,512]{1,0:T(8,128)(2,1)} %collective-permute-done.11.refs_12_), channel_id=1, source_target_pairs={{0,8},{8,0},{16,24},{24,16},{1,9},{9,1},{17,25},{25,17},{2,10},{10... | collective-permute-start | bytes 1572872 | tf_op jit(solution)/shard_map/ppermute | solution.py:1042
  140.9 15.5 %collective-permute-start.28 = (bf16[4,528,512]{2,1,0:T(8,128)(2,1)}, bf16[4,528,512]{2,1,0:T(8,128)(2,1)S(1)}, u32[]{:S(2)}, u32[]{:S(2)}) collective-permute-start(bf16[4,528,512]{2,1,0:T(8,128)(2,1)} %get-tuple-element.157), channel_id=1, source_target_pairs={{0,8},{8,0},{16,24},{24,16},{1,9},{9,1},{17,25},{25,17},{2,10},{10... | collective-permute-start | bytes 6488072 | tf_op jit(solution)/shard_map/ppermute | solution.py:1042
  155.9 6.1 %collective-permute-start.27 = (bf16[4,528,512]{2,1,0:T(8,128)(2,1)}, bf16[4,528,512]{2,1,0:T(8,128)(2,1)}, u32[]{:S(2)}, u32[]{:S(2)}) collective-permute-start(bf16[4,528,512]{2,1,0:T(8,128)(2,1)} %get-tuple-element.155), channel_id=1, source_target_pairs={{0,8},{8,0},{16,24},{24,16},{1,9},{9,1},{17,25},{25,17},{2,10},{10... | collective-permute-start | bytes 6488072 | tf_op jit(solution)/shard_map/ppermute | solution.py:1042
  156.3 20.2 %collective-permute-start.32 = (bf16[4,528,512]{2,1,0:T(8,128)(2,1)}, bf16[4,528,512]{2,1,0:T(8,128)(2,1)S(1)}, u32[]{:S(2)}, u32[]{:S(2)}) collective-permute-start(bf16[4,528,512]{2,1,0:T(8,128)(2,1)} %get-tuple-element.170), channel_id=1, source_target_pairs={{0,8},{8,0},{16,24},{24,16},{1,9},{9,1},{17,25},{25,17},{2,10},{10... | collective-permute-start | bytes 6488072 | tf_op jit(solution)/shard_map/ppermute | solution.py:1042
  166.1 10.4 %collective-permute-start.31 = (bf16[4,528,512]{2,1,0:T(8,128)(2,1)}, bf16[4,528,512]{2,1,0:T(8,128)(2,1)}, u32[]{:S(2)}, u32[]{:S(2)}) collective-permute-start(bf16[4,528,512]{2,1,0:T(8,128)(2,1)} %get-tuple-element.169), channel_id=1, source_target_pairs={{0,8},{8,0},{16,24},{24,16},{1,9},{9,1},{17,25},{25,17},{2,10},{10... | collective-permute-start | bytes 6488072 | tf_op jit(solution)/shard_map/ppermute | solution.py:1042
  166.5 26.2 %collective-permute-start.29 = (bf16[2,528,512]{2,1,0:T(8,128)(2,1)}, bf16[2,528,512]{2,1,0:T(8,128)(2,1)S(1)}, u32[]{:S(2)}, u32[]{:S(2)}) collective-permute-start(bf16[2,528,512]{2,1,0:T(8,128)(2,1)} %get-tuple-element.158), channel_id=1, source_target_pairs={{0,1},{1,0},{2,3},{3,2},{4,5},{5,4},{6,7},{7,6},{8,9},{9,8},{10,11... | collective-permute-start | bytes 3244040 | tf_op jit(solution)/shard_map/ppermute | solution.py:1034
  168.1 27.3 %collective-permute-start.30 = (bf16[2,528,512]{2,1,0:T(8,128)(2,1)}, bf16[2,528,512]{2,1,0:T(8,128)(2,1)}, u32[]{:S(2)}, u32[]{:S(2)}) collective-permute-start(bf16[2,528,512]{2,1,0:T(8,128)(2,1)} %get-tuple-element.159), channel_id=1, source_target_pairs={{0,16},{8,24},{16,0},{24,8},{1,17},{9,25},{17,1},{25,9},{2,18},{10... | collective-permute-start | bytes 3244040 | tf_op jit(solution)/shard_map/ppermute | solution.py:1038
  172.4 4.1 %collective-permute-start.34 = (f32[16,512]{1,0:T(8,128)S(1)}, f32[16,512]{1,0:T(8,128)S(1)}, u32[]{:S(2)}, u32[]{:S(2)}) collective-permute-start(f32[16,512]{1,0:T(8,128)S(1)} %add.199), channel_id=1, source_target_pairs={{0,2},{1,3},{2,0},{3,1},{4,6},{5,7},{6,4},{7,5},{8,10},{9,11},{10,... | collective-permute-start | bytes 98312 | tf_op jit(solution)/shard_map/ppermute | solution.py:1050
  186.3 6.0 %collective-permute-start.35 = (f32[16,512]{1,0:T(8,128)S(1)}, f32[16,512]{1,0:T(8,128)S(1)}, u32[]{:S(2)}, u32[]{:S(2)}) collective-permute-start(f32[16,512]{1,0:T(8,128)S(1)} %add.200), channel_id=1, source_target_pairs={{0,4},{1,5},{2,6},{3,7},{4,0},{5,1},{6,2},{7,3},{8,12},{9,13},{10,... | collective-permute-start | bytes 98312 | tf_op jit(solution)/shard_map/ppermute | solution.py:1050
  195.4 20.6 %collective-permute-start.58 = (f32[16,512]{1,0:T(8,128)S(1)}, f32[16,512]{1,0:T(8,128)S(1)}, u32[]{:S(2)}, u32[]{:S(2)}) collective-permute-start(f32[16,512]{1,0:T(8,128)S(1)} %add.201), channel_id=1, source_target_pairs={{0,1},{1,0},{2,3},{3,2},{4,5},{5,4},{6,7},{7,6},{8,9},{9,8},{10,11... | collective-permute-start | bytes 98312 | tf_op jit(solution)/shard_map/ppermute | solution.py:1034
  196.5 9.5 %collective-permute-start.37 = (bf16[256,512]{1,0:T(8,128)(2,1)}, bf16[256,512]{1,0:T(8,128)(2,1)S(1)}, u32[]{:S(2)}, u32[]{:S(2)}) collective-permute-start(bf16[256,512]{1,0:T(8,128)(2,1)} %get-tuple-element.196), channel_id=1, source_target_pairs={{0,16},{8,24},{16,0},{24,8},{1,17},{9,25},{17,1},{25,9},{2,18},{10... | collective-permute-start | bytes 786440 | tf_op jit(solution)/shard_map/ppermute | solution.py:1038
  198.2 13.7 %collective-permute-start.48 = (bf16[272,512]{1,0:T(8,128)(2,1)}, bf16[272,512]{1,0:T(8,128)(2,1)S(1)}, u32[]{:S(2)}, u32[]{:S(2)}) collective-permute-start(bf16[272,512]{1,0:T(8,128)(2,1)} %get-tuple-element.215), channel_id=1, source_target_pairs={{0,16},{8,24},{16,0},{24,8},{1,17},{9,25},{17,1},{25,9},{2,18},{10... | collective-permute-start | bytes 835592 | tf_op jit(solution)/shard_map/ppermute | solution.py:1038
  199.7 9.3 %collective-permute-start.36 = (bf16[256,512]{1,0:T(8,128)(2,1)S(1)}, bf16[256,512]{1,0:T(8,128)(2,1)S(1)}, u32[]{:S(2)}, u32[]{:S(2)}) collective-permute-start(bf16[256,512]{1,0:T(8,128)(2,1)S(1)} %get-tuple-element.240), channel_id=1, source_target_pairs={{0,1},{1,0},{2,3},{3,2},{4,5},{5,4},{6,7},{7,6},{8,9},{9,8},{10,11... | collective-permute-start | bytes 786440 | tf_op jit(solution)/shard_map/ppermute | solution.py:1034
  201.9 13.1 %collective-permute-start.47 = (bf16[272,512]{1,0:T(8,128)(2,1)S(1)}, bf16[272,512]{1,0:T(8,128)(2,1)S(1)}, u32[]{:S(2)}, u32[]{:S(2)}) collective-permute-start(bf16[272,512]{1,0:T(8,128)(2,1)S(1)} %get-tuple-element.244), channel_id=1, source_target_pairs={{0,1},{1,0},{2,3},{3,2},{4,5},{5,4},{6,7},{7,6},{8,9},{9,8},{10,11... | collective-permute-start | bytes 835592 | tf_op jit(solution)/shard_map/ppermute | solution.py:1034
  209.0 11.6 %collective-permute-start.38 = (bf16[256,512]{1,0:T(8,128)(2,1)S(1)}, bf16[256,512]{1,0:T(8,128)(2,1)S(1)}, u32[]{:S(2)}, u32[]{:S(2)}) collective-permute-start(bf16[256,512]{1,0:T(8,128)(2,1)S(1)} %get-tuple-element.197), channel_id=1, source_target_pairs={{0,1},{1,0},{2,3},{3,2},{4,5},{5,4},{6,7},{7,6},{8,9},{9,8},{10,11... | collective-permute-start | bytes 786440 | tf_op jit(solution)/shard_map/ppermute | solution.py:1034
  209.9 11.6 %collective-permute-start.39 = (bf16[256,512]{1,0:T(8,128)(2,1)S(1)}, bf16[256,512]{1,0:T(8,128)(2,1)S(1)}, u32[]{:S(2)}, u32[]{:S(2)}) collective-permute-start(bf16[256,512]{1,0:T(8,128)(2,1)S(1)} %copy-done.47), channel_id=1, source_target_pairs={{0,16},{8,24},{16,0},{24,8},{1,17},{9,25},{17,1},{25,9},{2,18},{10... | collective-permute-start | bytes 786440 | tf_op jit(solution)/shard_map/ppermute | solution.py:1038
  211.9 11.5 %collective-permute-start.44 = (bf16[256,512]{1,0:T(8,128)(2,1)S(1)}, bf16[256,512]{1,0:T(8,128)(2,1)S(1)}, u32[]{:S(2)}, u32[]{:S(2)}) collective-permute-start(bf16[256,512]{1,0:T(8,128)(2,1)S(1)} %add_convert_fusion.5), channel_id=1, source_target_pairs={{0,2},{1,3},{2,4},{3,5},{4,6},{5,7},{6,0},{7,1},{8,10},{9,11},{10,... | collective-permute-start | bytes 786440 | tf_op jit(solution)/shard_map/ppermute | solution.py:1046
  215.0 11.6 %collective-permute-start.49 = (bf16[272,512]{1,0:T(8,128)(2,1)S(1)}, bf16[272,512]{1,0:T(8,128)(2,1)S(1)}, u32[]{:S(2)}, u32[]{:S(2)}) collective-permute-start(bf16[272,512]{1,0:T(8,128)(2,1)S(1)} %get-tuple-element.216), channel_id=1, source_target_pairs={{0,1},{1,0},{2,3},{3,2},{4,5},{5,4},{6,7},{7,6},{8,9},{9,8},{10,11... | collective-permute-start | bytes 835592 | tf_op jit(solution)/shard_map/ppermute | solution.py:1034
  216.0 10.5 %collective-permute-start.50 = (bf16[272,512]{1,0:T(8,128)(2,1)S(1)}, bf16[272,512]{1,0:T(8,128)(2,1)S(1)}, u32[]{:S(2)}, u32[]{:S(2)}) collective-permute-start(bf16[272,512]{1,0:T(8,128)(2,1)S(1)} %copy-done.45), channel_id=1, source_target_pairs={{0,16},{8,24},{16,0},{24,8},{1,17},{9,25},{17,1},{25,9},{2,18},{10... | collective-permute-start | bytes 835592 | tf_op jit(solution)/shard_map/ppermute | solution.py:1038
  220.6 11.3 %collective-permute-start.55 = (bf16[272,512]{1,0:T(8,128)(2,1)S(1)}, bf16[272,512]{1,0:T(8,128)(2,1)S(1)}, u32[]{:S(2)}, u32[]{:S(2)}) collective-permute-start(bf16[272,512]{1,0:T(8,128)(2,1)S(1)} %add_convert_fusion.2), channel_id=1, source_target_pairs={{0,2},{1,3},{2,4},{3,5},{4,6},{5,7},{6,0},{7,1},{8,10},{9,11},{10,... | collective-permute-start | bytes 835592 | tf_op jit(solution)/shard_map/ppermute | solution.py:1046
  221.5 11.5 %collective-permute-start.59 = (f32[16,512]{1,0:T(8,128)S(1)}, f32[16,512]{1,0:T(8,128)S(1)}, u32[]{:S(2)}, u32[]{:S(2)}) collective-permute-start(f32[16,512]{1,0:T(8,128)S(1)} %add.232), channel_id=1, source_target_pairs={{0,16},{8,24},{16,0},{24,8},{1,17},{9,25},{17,1},{25,9},{2,18},{10... | collective-permute-start | bytes 98312 | tf_op jit(solution)/shard_map/ppermute | solution.py:1038
  223.3 9.7 %collective-permute-start.40 = (bf16[256,512]{1,0:T(8,128)(2,1)S(1)}, bf16[256,512]{1,0:T(8,128)(2,1)S(1)}, u32[]{:S(2)}, u32[]{:S(2)}) collective-permute-start(bf16[256,512]{1,0:T(8,128)(2,1)S(1)} %copy-done.46), channel_id=1, source_target_pairs={{0,1},{1,0},{2,3},{3,2},{4,5},{5,4},{6,7},{7,6},{8,9},{9,8},{10,11... | collective-permute-start | bytes 786440 | tf_op jit(solution)/shard_map/ppermute | solution.py:1034
  226.5 11.0 %collective-permute-start.45 = (bf16[256,512]{1,0:T(8,128)(2,1)S(1)}, bf16[256,512]{1,0:T(8,128)(2,1)S(1)}, u32[]{:S(2)}, u32[]{:S(2)}) collective-permute-start(bf16[256,512]{1,0:T(8,128)(2,1)S(1)} %add_convert_fusion.4), channel_id=1, source_target_pairs={{0,2},{1,3},{2,4},{3,5},{4,6},{5,7},{6,0},{7,1},{8,10},{9,11},{10,... | collective-permute-start | bytes 786440 | tf_op jit(solution)/shard_map/ppermute | solution.py:1046
  226.5 9.6 %collective-permute-start.41 = (bf16[256,512]{1,0:T(8,128)(2,1)}, bf16[256,512]{1,0:T(8,128)(2,1)S(1)}, u32[]{:S(2)}, u32[]{:S(2)}) collective-permute-start(bf16[256,512]{1,0:T(8,128)(2,1)} %get-tuple-element.203), channel_id=1, source_target_pairs={{0,16},{8,24},{16,0},{24,8},{1,17},{9,25},{17,1},{25,9},{2,18},{10... | collective-permute-start | bytes 786440 | tf_op jit(solution)/shard_map/ppermute | solution.py:1038
  231.9 7.8 %collective-permute-start.51 = (bf16[272,512]{1,0:T(8,128)(2,1)}, bf16[272,512]{1,0:T(8,128)(2,1)S(1)}, u32[]{:S(2)}, u32[]{:S(2)}) collective-permute-start(bf16[272,512]{1,0:T(8,128)(2,1)} %get-tuple-element.219), channel_id=1, source_target_pairs={{0,1},{1,0},{2,3},{3,2},{4,5},{5,4},{6,7},{7,6},{8,9},{9,8},{10,11... | collective-permute-start | bytes 835592 | tf_op jit(solution)/shard_map/ppermute | solution.py:1034
  233.0 11.2 %collective-permute-start.56 = (bf16[272,512]{1,0:T(8,128)(2,1)S(1)}, bf16[272,512]{1,0:T(8,128)(2,1)S(1)}, u32[]{:S(2)}, u32[]{:S(2)}) collective-permute-start(bf16[272,512]{1,0:T(8,128)(2,1)S(1)} %add_convert_fusion.1), channel_id=1, source_target_pairs={{0,2},{1,3},{2,4},{3,5},{4,6},{5,7},{6,0},{7,1},{8,10},{9,11},{10,... | collective-permute-start | bytes 835592 | tf_op jit(solution)/shard_map/ppermute | solution.py:1046
  233.1 8.9 %collective-permute-start.52 = (bf16[272,512]{1,0:T(8,128)(2,1)S(1)}, bf16[272,512]{1,0:T(8,128)(2,1)S(1)}, u32[]{:S(2)}, u32[]{:S(2)}) collective-permute-start(bf16[272,512]{1,0:T(8,128)(2,1)S(1)} %get-tuple-element.221), channel_id=1, source_target_pairs={{0,16},{8,24},{16,0},{24,8},{1,17},{9,25},{17,1},{25,9},{2,18},{10... | collective-permute-start | bytes 835592 | tf_op jit(solution)/shard_map/ppermute | solution.py:1038
  236.2 9.1 %collective-permute-start.42 = (bf16[256,512]{1,0:T(8,128)(2,1)}, bf16[256,512]{1,0:T(8,128)(2,1)S(1)}, u32[]{:S(2)}, u32[]{:S(2)}) collective-permute-start(bf16[256,512]{1,0:T(8,128)(2,1)} %get-tuple-element.204), channel_id=1, source_target_pairs={{0,1},{1,0},{2,3},{3,2},{4,5},{5,4},{6,7},{7,6},{8,9},{9,8},{10,11... | collective-permute-start | bytes 786440 | tf_op jit(solution)/shard_map/ppermute | solution.py:1034
  237.6 9.3 %collective-permute-start.43 = (bf16[256,512]{1,0:T(8,128)(2,1)}, bf16[256,512]{1,0:T(8,128)(2,1)S(1)}, u32[]{:S(2)}, u32[]{:S(2)}) collective-permute-start(bf16[256,512]{1,0:T(8,128)(2,1)} %get-tuple-element.206), channel_id=1, source_target_pairs={{0,16},{8,24},{16,0},{24,8},{1,17},{9,25},{17,1},{25,9},{2,18},{10... | collective-permute-start | bytes 786440 | tf_op jit(solution)/shard_map/ppermute | solution.py:1038
  239.7 9.4 %collective-permute-start.46 = (bf16[256,512]{1,0:T(8,128)(2,1)S(1)}, bf16[256,512]{1,0:T(8,128)(2,1)S(1)}, u32[]{:S(2)}, u32[]{:S(2)}) collective-permute-start(bf16[256,512]{1,0:T(8,128)(2,1)S(1)} %add_convert_fusion.3), channel_id=1, source_target_pairs={{0,2},{1,3},{2,4},{3,5},{4,6},{5,7},{6,0},{7,1},{8,10},{9,11},{10,... | collective-permute-start | bytes 786440 | tf_op jit(solution)/shard_map/ppermute | solution.py:1046
  242.0 7.3 %collective-permute-start.53 = (bf16[272,512]{1,0:T(8,128)(2,1)}, bf16[272,512]{1,0:T(8,128)(2,1)S(1)}, u32[]{:S(2)}, u32[]{:S(2)}) collective-permute-start(bf16[272,512]{1,0:T(8,128)(2,1)} %get-tuple-element.222), channel_id=1, source_target_pairs={{0,1},{1,0},{2,3},{3,2},{4,5},{5,4},{6,7},{7,6},{8,9},{9,8},{10,11... | collective-permute-start | bytes 835592 | tf_op jit(solution)/shard_map/ppermute | solution.py:1034
  244.2 6.5 %collective-permute-start.54 = (bf16[272,512]{1,0:T(8,128)(2,1)S(1)}, bf16[272,512]{1,0:T(8,128)(2,1)S(1)}, u32[]{:S(2)}, u32[]{:S(2)}) collective-permute-start(bf16[272,512]{1,0:T(8,128)(2,1)S(1)} %get-tuple-element.224), channel_id=1, source_target_pairs={{0,16},{8,24},{16,0},{24,8},{1,17},{9,25},{17,1},{25,9},{2,18},{10... | collective-permute-start | bytes 835592 | tf_op jit(solution)/shard_map/ppermute | solution.py:1038
  245.3 8.8 %collective-permute-start.57 = (bf16[272,512]{1,0:T(8,128)(2,1)S(1)}, bf16[272,512]{1,0:T(8,128)(2,1)S(1)}, u32[]{:S(2)}, u32[]{:S(2)}) collective-permute-start(bf16[272,512]{1,0:T(8,128)(2,1)S(1)} %add_convert_fusion), channel_id=1, source_target_pairs={{0,2},{1,3},{2,4},{3,5},{4,6},{5,7},{6,0},{7,1},{8,10},{9,11},{10,... | collective-permute-start | bytes 835592 | tf_op jit(solution)/shard_map/ppermute | solution.py:1046
  261.2 1.4 collective-permute-start.60
  263.3 3.6 %collective-permute-start.61 = (f32[8,128]{1,0:T(8,128)S(1)}, f32[8,128]{1,0:T(8,128)S(1)}, u32[]{:S(2)}, u32[]{:S(2)}) collective-permute-start(f32[8,128]{1,0:T(8,128)S(1)} %add.237), channel_id=1, source_target_pairs={{0,1},{1,0},{2,3},{3,2},{4,5},{5,4},{6,7},{7,6},{8,9},{9,8},{10,11... | collective-permute-start | bytes 12296 | tf_op jit(solution)/shard_map/ppermute | solution.py:1034
  266.9 3.6 %collective-permute-start.62 = (f32[8,128]{1,0:T(8,128)S(1)}, f32[8,128]{1,0:T(8,128)S(1)}, u32[]{:S(2)}, u32[]{:S(2)}) collective-permute-start(f32[8,128]{1,0:T(8,128)S(1)} %add.238), channel_id=1, source_target_pairs={{0,16},{8,24},{16,0},{24,8},{1,17},{9,25},{17,1},{25,9},{2,18},{10... | collective-permute-start | bytes 12296 | tf_op jit(solution)/shard_map/ppermute | solution.py:1038
  270.5 3.6 %collective-permute-start.63 = (f32[8,128]{1,0:T(8,128)S(1)}, f32[8,128]{1,0:T(8,128)S(1)}, u32[]{:S(2)}, u32[]{:S(2)}) collective-permute-start(f32[8,128]{1,0:T(8,128)S(1)} %add.239), channel_id=1, source_target_pairs={{0,2},{1,3},{2,0},{3,1},{4,6},{5,7},{6,4},{7,5},{8,10},{9,11},{10,... | collective-permute-start | bytes 12296 | tf_op jit(solution)/shard_map/ppermute | solution.py:1050
  274.1 4.5 %collective-permute-start.64 = (f32[8,128]{1,0:T(8,128)S(1)}, f32[8,128]{1,0:T(8,128)S(1)}, u32[]{:S(2)}, u32[]{:S(2)}) collective-permute-start(f32[8,128]{1,0:T(8,128)S(1)} %add.240), channel_id=1, source_target_pairs={{0,4},{1,5},{2,6},{3,7},{4,0},{5,1},{6,2},{7,3},{8,12},{9,13},{10,... | collective-permute-start | bytes 12296 | tf_op jit(solution)/shard_map/ppermute | solution.py:1050
  (51 other events, 806.3 us)

commit v4 on v3

--- a/solution.py
+++ b/solution.py
@@ -1204,7 +1204,7 @@
     to_y = chip_sum(False, 0, range(4), SIDES)
     mine = chip_sum(True, 0, range(4), SIDES)
     late = late + over_z(after(late, mine[3][1], to_y[3][1], to_x[3][1]), 2)
-    from_x, from_y, to_x, to_y, mine, late = lax.optimization_barrier((from_x, from_y, to_x, to_y, mine, late))
+    from_y, to_x, to_y, mine, late = lax.optimization_barrier((from_y, to_x, to_y, mine, late))
     late = late + over_x(late)
     late = late + over_y(late)
     running = [None, None]

time: 283 us -> 283 us (level)
    ppermute x16, starting transfers between devices: 25 us -> 27.9 us  [over_y(): return lax.ppermute(value, 'dp', [(i, i ^ 2) for i in range(4)])]
  transfers between devices with their start and end apart: 65 -> 65, of which waited for: 38 -> 34; matrix products, arithmetic and copies ran while one was open for 3% -> 3% of each run, Pallas kernels for 11% -> 11%
where the time goes in v4:
time: 283 us
  waiting for transfers between devices  125 us (44%)
  Pallas kernels  82.4 us (29%)
  starting transfers between devices  56 us (20%)
  other arithmetic  9.42 us (3%)
  local copies, waits for them, and re-layouts  7.9 us (3%)
    pallas_call x6, Pallas kernels, call(): pl.pallas_call(kernel, name=name, in_specs=[space for space, _ in ins], o...  73.6 us
    ppermute x16, waiting for transfers between devices, over_x(): return lax.ppermute(value, 'fsdp', [(i, i ^ 1) for i in range(8)])  45.1 us
    ppermute x16, waiting for transfers between devices, over_y(): return lax.ppermute(value, 'dp', [(i, i ^ 2) for i in range(4)])  35.6 us
    ppermute x16, starting transfers between devices, over_y(): return lax.ppermute(value, 'dp', [(i, i ^ 2) for i in range(4)])  27.9 us
    ppermute x9, waiting for transfers between devices, round_z(): return lax.ppermute(value, 'fsdp', [(i, (i + 2) % 8) for i in range(8)])  24.7 us
    ppermute x16, starting transfers between devices, over_x(): return lax.ppermute(value, 'fsdp', [(i, i ^ 1) for i in range(8)])  16.4 us
    ppermute x20, waiting for transfers between devices, over_core(): return lax.ppermute(value, 'dp', [(i, i ^ 1) for i in range(4)])  10.7 us
    ppermute x4, waiting for transfers between devices, over_z(): return lax.ppermute(value, 'fsdp', [(i, i ^ 2 * step) for i in range(8)])  8.64 us
  transfers between devices with their start and end apart: 65, of which 34 were waited for; matrix products, arithmetic and copies ran while one was open for 3% of the time, Pallas kernels for 11%

profile of v4, /device:TPU:0, one launch (start us, length us, event | category | flops | bytes accessed | tf_op | source)
XLA Modules:
  0.0 282.6 jit_solution(12755949753012139063)
XLA Ops:
  0.7 1.3 convert_element_type.246
  2.8 3.0 %collective-permute-start.2 = (bf16[528,512]{1,0:T(8,128)(2,1)S(1)}, bf16[528,512]{1,0:T(8,128)(2,1)S(1)}, u32[]{:S(2)}, u32[]{:S(2)}) collective-permute-start(bf16[528,512]{1,0:T(8,128)(2,1)S(1)} %reshape.49.refs_4_), channel_id=1, source_target_pairs={{0,16},{8,24},{16,0},{24,8},{1,17},{9,25},{17,1},{25,9},{2,18},{10... | collective-permute-start | bytes 1622024 | tf_op jit(solution)/shard_map/ppermute | solution.py:1038
  5.8 1.5 collective-permute-start.1
  7.3 1.6 collective-permute-start
  8.9 9.2 %collective-permute-done.2.refs_13_ = bf16[528,512]{1,0:T(8,128)(2,1)S(1)} collective-permute-done((bf16[528,512]{1,0:T(8,128)(2,1)S(1)}, bf16[528,512]{1,0:T(8,128)(2,1)S(1)}, u32[]{:S(2)}, u32[]{:S(2)}) %collective-permute-start.2) | collective-permute-done | bytes 540704 | tf_op jit(solution)/shard_map/ppermute | solution.py:1038
  18.1 1.5 collective-permute-done.1.refs_8_
  19.5 3.1 %collective-permute-done.refs_5_ = bf16[528,512]{1,0:T(8,128)(2,1)S(1)} collective-permute-done((bf16[528,512]{1,0:T(8,128)(2,1)S(1)}, bf16[528,512]{1,0:T(8,128)(2,1)S(1)}, u32[]{:S(2)}, u32[]{:S(2)}) %collective-permute-start) | collective-permute-done | bytes 540704 | tf_op jit(solution)/shard_map/ppermute | solution.py:1046
  23.6 11.5 %collective-permute-done.5.refs_14_ = bf16[528,512]{1,0:T(8,128)(2,1)S(1)} collective-permute-done((bf16[528,512]{1,0:T(8,128)(2,1)S(1)}, bf16[528,512]{1,0:T(8,128)(2,1)S(1)}, u32[]{:S(2)}, u32[]{:S(2)}) %collective-permute-start.5) | collective-permute-done | bytes 540704 | tf_op jit(solution)/shard_map/ppermute | solution.py:1038
  35.4 2.3 collective-permute-done.3.refs_6_
  37.8 1.3 collective-permute-start.7
  39.2 1.6 collective-permute-start.9
  40.8 10.0 %collective-permute-done.6.refs_7_ = bf16[528,512]{1,0:T(8,128)(2,1)S(1)} collective-permute-done((bf16[528,512]{1,0:T(8,128)(2,1)S(1)}, bf16[528,512]{1,0:T(8,128)(2,1)S(1)}, u32[]{:S(2)}, u32[]{:S(2)}) %collective-permute-start.6) | collective-permute-done | bytes 540704 | tf_op jit(solution)/shard_map/ppermute | solution.py:1046
  52.1 1.6 collective-permute-start.10
  54.1 4.6 %collective-permute-done.7.refs_10_ = bf16[784,512]{1,0:T(8,128)(2,1)S(1)} collective-permute-done((bf16[784,512]{1,0:T(8,128)(2,1)S(1)}, bf16[784,512]{1,0:T(8,128)(2,1)S(1)}, u32[]{:S(2)}, u32[]{:S(2)}) %collective-permute-start.7) | collective-permute-done | bytes 802848 | tf_op jit(solution)/shard_map/ppermute | solution.py:1034
  59.3 12.8 %collective-permute-done.8.refs_11_ = bf16[784,512]{1,0:T(8,128)(2,1)S(1)} collective-permute-done((bf16[784,512]{1,0:T(8,128)(2,1)S(1)}, bf16[784,512]{1,0:T(8,128)(2,1)S(1)}, u32[]{:S(2)}, u32[]{:S(2)}) %collective-permute-start.8) | collective-permute-done | bytes 802848 | tf_op jit(solution)/shard_map/ppermute | solution.py:1034
  72.1 1.7 collective-permute-done.10.refs_16_
  74.9 1.6 collective-permute-start.12
  78.0 13.0 %collective-permute-done.11.refs_12_ = bf16[512,512]{1,0:T(8,128)(2,1)} collective-permute-done((bf16[512,512]{1,0:T(8,128)(2,1)S(1)}, bf16[512,512]{1,0:T(8,128)(2,1)}, u32[]{:S(2)}, u32[]{:S(2)}) %collective-permute-start.11) | collective-permute-done | bytes 524320 | tf_op jit(solution)/shard_map/ppermute | solution.py:1034
  95.1 2.3 collective-permute-done.19.refs_24_
  98.5 42.5 %forward.1 = (bf16[160,512]{1,0:T(8,128)(2,1)}, f32[8,512]{1,0:T(8,128)}, f32[176,512]{1,0:T(8,128)}, bf16[8,528,512]{2,1,0:T(8,128)(2,1)}, bf16[4,528,512]{2,1,...) custom-call(s32[4]{0:T(128)} %pad_add_fusion.refs_0_.coords, ...), custom_call_target="tpu_custom_call" | custom-call | tf_op jit(solution)/shard_map/forward/pallas_call | solution.py:972
  141.2 14.6 %backward.1 = (bf16[160,512]{1,0:T(8,128)(2,1)}, f32[16,512]{1,0:T(8,128)}, bf16[8,528,512]{2,1,0:T(8,128)(2,1)}, bf16[4,528,512]{2,1,0:T(8,128)(2,1)}, bf16[4,528,512]{2,1,0:T(8,128)(2,1)}) custom-call(s32[4]{0:T(128)} %pad_add_fusion.refs_0_.coords, bf16[160,512]{1,0:T(8,128)(2,1)} %bitcast.49, ...), custom_call_target="tpu_custom_call", output_to_operand_aliasing={{2}: (18, {}), {3}: (19, {}), {4}: (20, {})} | custom-call | tf_op jit(solution)/shard_map/backward/pallas_call | solution.py:972
  156.5 5.5 %collective-permute-done.27.low_got = bf16[4,528,512]{2,1,0:T(8,128)(2,1)} collective-permute-done((bf16[4,528,512]{2,1,0:T(8,128)(2,1)}, bf16[4,528,512]{2,1,0:T(8,128)(2,1)}, u32[]{:S(2)}, u32[]{:S(2)}) %collective-permute-start.27) | collective-permute-done | bytes 2162720 | tf_op jit(solution)/shard_map/ppermute | solution.py:1042
  162.0 4.1 %span_sums.4 = (bf16[2,528,512]{2,1,0:T(8,128)(2,1)}, bf16[2,528,512]{2,1,0:T(8,128)(2,1)}) custom-call(s32[4]{0:T(128)} %pad_add_fusion.refs_0_.coords, bf16[8,528,512]{2,1,0:T(8,128)(2,1)} %get-tuple-element.153.low_kept, bf16[4,528,512]{2,1,0:T(8,128)(2,1)} %collective-permute-done.27.low_got, bf16[8,528,512]{2,1,0:T(8,128)(2,1)} %get-tuple-element.155.high_kept, ...), custom_call_target="tpu_custom_call" | custom-call | tf_op jit(solution)/shard_map/span_sums/pallas_call | solution.py:972
  166.5 3.7 %collective-permute-start.29 = (bf16[2,528,512]{2,1,0:T(8,128)(2,1)}, bf16[2,528,512]{2,1,0:T(8,128)(2,1)}, u32[]{:S(2)}, u32[]{:S(2)}) collective-permute-start(bf16[2,528,512]{2,1,0:T(8,128)(2,1)} %get-tuple-element.157), channel_id=1, source_target_pairs={{0,16},{8,24},{16,0},{24,8},{1,17},{9,25},{17,1},{25,9},{2,18},{10... | collective-permute-start | bytes 3244040 | tf_op jit(solution)/shard_map/ppermute | solution.py:1038
  171.2 1.2 collective-permute-done.32
  172.4 4.0 %span_sums.5 = (bf16[256,512]{1,0:T(8,128)(2,1)}, bf16[272,512]{1,0:T(8,128)(2,1)}, bf16[256,512]{1,0:T(8,128)(2,1)}, bf16[272,512]{1,0:T(8,128)(2,1)}, bf16[256...) custom-call(s32[4]{0:T(128)} %pad_add_fusion.refs_0_.coords, ...), custom_call_target="tpu_custom_call" | custom-call | tf_op jit(solution)/shard_map/span_sums/pallas_call | solution.py:972
  176.5 1.3 copy-done
  177.9 4.0 %span_sums.7 = (bf16[256,512]{1,0:T(8,128)(2,1)}, bf16[272,512]{1,0:T(8,128)(2,1)}, bf16[256,512]{1,0:T(8,128)(2,1)}, bf16[272,512]{1,0:T(8,128)(2,1)}, bf16[256...) custom-call(s32[4]{0:T(128)} %pad_add_fusion.refs_0_.coords, ...), custom_call_target="tpu_custom_call" | custom-call | tf_op jit(solution)/shard_map/span_sums/pallas_call | solution.py:972
  181.9 4.4 %span_sums.6 = (bf16[256,512]{1,0:T(8,128)(2,1)}, bf16[272,512]{1,0:T(8,128)(2,1)}, bf16[256,512]{1,0:T(8,128)(2,1)}, bf16[272,512]{1,0:T(8,128)(2,1)}, bf16[256...) custom-call(s32[4]{0:T(128)} %pad_add_fusion.refs_0_.coords, ...), custom_call_target="tpu_custom_call" | custom-call | tf_op jit(solution)/shard_map/span_sums/pallas_call | solution.py:972
  186.3 4.1 %collective-permute-start.34 = (f32[16,512]{1,0:T(8,128)S(1)}, f32[16,512]{1,0:T(8,128)S(1)}, u32[]{:S(2)}, u32[]{:S(2)}) collective-permute-start(f32[16,512]{1,0:T(8,128)S(1)} %add.200), channel_id=1, source_target_pairs={{0,4},{1,5},{2,6},{3,7},{4,0},{5,1},{6,2},{7,3},{8,12},{9,13},{10,... | collective-permute-start | bytes 98312 | tf_op jit(solution)/shard_map/ppermute | solution.py:1050
  190.5 1.8 collective-permute-done.34
  192.3 2.4 collective-permute-done.29
  195.7 1.7 collective-permute-start.36
  197.7 1.2 fusion.8
  198.9 1.2 collective-permute-start.35
  200.1 1.2 fusion.4
  202.4 2.7 collective-permute-done.36
  205.1 3.1 %collective-permute-done.35 = bf16[256,512]{1,0:T(8,128)(2,1)S(1)} collective-permute-done((bf16[256,512]{1,0:T(8,128)(2,1)S(1)}, bf16[256,512]{1,0:T(8,128)(2,1)S(1)}, u32[]{:S(2)}, u32[]{:S(2)}) %collective-permute-start.35) | collective-permute-done | bytes 262176 | tf_op jit(solution)/shard_map/ppermute | solution.py:1034
  208.2 1.1 collective-permute-start.37
  209.3 1.7 collective-permute-start.38
  211.2 2.9 %collective-permute-done.47 = bf16[272,512]{1,0:T(8,128)(2,1)S(1)} collective-permute-done((bf16[272,512]{1,0:T(8,128)(2,1)S(1)}, bf16[272,512]{1,0:T(8,128)(2,1)S(1)}, u32[]{:S(2)}, u32[]{:S(2)}) %collective-permute-start.47) | collective-permute-done | bytes 278560 | tf_op jit(solution)/shard_map/ppermute | solution.py:1034
  214.2 1.1 collective-permute-start.49
  215.4 1.8 collective-permute-start.50
  217.2 2.6 collective-permute-done.37
  220.7 1.8 collective-permute-start.59
  222.6 1.1 collective-permute-start.39
  223.8 1.9 collective-permute-done.49
  225.8 1.7 collective-permute-start.41
  227.5 3.0 %collective-permute-done.55 = bf16[272,512]{1,0:T(8,128)(2,1)S(1)} collective-permute-done((bf16[272,512]{1,0:T(8,128)(2,1)S(1)}, bf16[272,512]{1,0:T(8,128)(2,1)S(1)}, u32[]{:S(2)}, u32[]{:S(2)}) %collective-permute-start.55) | collective-permute-done | bytes 278560 | tf_op jit(solution)/shard_map/ppermute | solution.py:1046
  230.5 1.1 collective-permute-start.51
  231.9 2.4 collective-permute-start.52
  236.7 1.8 collective-permute-start.43
  239.4 2.4 collective-permute-done.52
  242.8 2.5 collective-permute-start.54
  246.5 2.1 collective-permute-done.46
  249.8 4.0 %collective-permute-done.57 = bf16[272,512]{1,0:T(8,128)(2,1)S(1)} collective-permute-done((bf16[272,512]{1,0:T(8,128)(2,1)S(1)}, bf16[272,512]{1,0:T(8,128)(2,1)S(1)}, u32[]{:S(2)}, u32[]{:S(2)}) %collective-permute-start.57) | collective-permute-done | bytes 278560 | tf_op jit(solution)/shard_map/ppermute | solution.py:1046
  254.4 1.3 dynamic_slice.11.grad
  255.7 5.3 %update.1 = (f32[256592]{0:T(1024)}, f32[256592]{0:T(1024)}, f32[256592]{0:T(1024)}, f32[8,128]{1,0:T(8,128)}) custom-call(s32[6]{0:T(128)} %pad_add_fusion.1.segments, f32[256592]{0:T(1024)} %params.3, f32[256592]{0:T(1024)} %first.1, f32[256592]{0:T(1024)} %second.1, f32[256592]{0:T(1024)} %dynamic_slice.11.grad), custom_call_target="tpu_custom_call" | custom-call | tf_op jit(solution)/shard_map/update/pallas_call | solution.py:1395
  261.1 1.4 collective-permute-done.60
  264.2 2.5 collective-permute-done.61
  266.7 3.6 %collective-permute-done.62 = f32[8,128]{1,0:T(8,128)S(1)} collective-permute-done((f32[8,128]{1,0:T(8,128)S(1)}, f32[8,128]{1,0:T(8,128)S(1)}, u32[]{:S(2)}, u32[]{:S(2)}) %collective-permute-start.62) | collective-permute-done | bytes 4128 | tf_op jit(solution)/shard_map/ppermute | solution.py:1038
  270.3 3.6 %collective-permute-done.63 = f32[8,128]{1,0:T(8,128)S(1)} collective-permute-done((f32[8,128]{1,0:T(8,128)S(1)}, f32[8,128]{1,0:T(8,128)S(1)}, u32[]{:S(2)}, u32[]{:S(2)}) %collective-permute-start.63) | collective-permute-done | bytes 4128 | tf_op jit(solution)/shard_map/ppermute | solution.py:1050
  275.3 3.2 %collective-permute-done.64 = f32[8,128]{1,0:T(8,128)S(1)} collective-permute-done((f32[8,128]{1,0:T(8,128)S(1)}, f32[8,128]{1,0:T(8,128)S(1)}, u32[]{:S(2)}, u32[]{:S(2)}) %collective-permute-start.64) | collective-permute-done | bytes 4128 | tf_op jit(solution)/shard_map/ppermute | solution.py:1050
  279.0 3.5 %apply.1 = (f32[256592]{0:T(1024)}, f32[12]{0:T(128)}, f32[12]{0:T(128)}, f32[12]{0:T(128)}) custom-call(s32[6]{0:T(128)} %pad_add_fusion.1.segments, f32[8,128]{1,0:T(8,128)} %add.241.sums, f32[256592]{0:T(1024)} %params.3, f32[256592]{0:T(1024)} %get-tuple-element.228.update), custom_call_target="tpu_custom_call" | custom-call | tf_op jit(solution)/shard_map/apply/pallas_call | solution.py:1405
  (220 shorter events, 28.6 us)
Async XLA Ops:
  2.8 15.3 %collective-permute-start.2 = (bf16[528,512]{1,0:T(8,128)(2,1)S(1)}, bf16[528,512]{1,0:T(8,128)(2,1)S(1)}, u32[]{:S(2)}, u32[]{:S(2)}) collective-permute-start(bf16[528,512]{1,0:T(8,128)(2,1)S(1)} %reshape.49.refs_4_), channel_id=1, source_target_pairs={{0,16},{8,24},{16,0},{24,8},{1,17},{9,25},{17,1},{25,9},{2,18},{10... | collective-permute-start | bytes 1622024 | tf_op jit(solution)/shard_map/ppermute | solution.py:1038
  5.8 13.7 %collective-permute-start.1 = (bf16[528,512]{1,0:T(8,128)(2,1)S(1)}, bf16[528,512]{1,0:T(8,128)(2,1)S(1)}, u32[]{:S(2)}, u32[]{:S(2)}) collective-permute-start(bf16[528,512]{1,0:T(8,128)(2,1)S(1)} %reshape.49.refs_4_), channel_id=1, source_target_pairs={{0,1},{1,0},{2,3},{3,2},{4,5},{5,4},{6,7},{7,6},{8,9},{9,8},{10,11... | collective-permute-start | bytes 1622024 | tf_op jit(solution)/shard_map/ppermute | solution.py:1034
  7.3 15.3 %collective-permute-start = (bf16[528,512]{1,0:T(8,128)(2,1)S(1)}, bf16[528,512]{1,0:T(8,128)(2,1)S(1)}, u32[]{:S(2)}, u32[]{:S(2)}) collective-permute-start(bf16[528,512]{1,0:T(8,128)(2,1)S(1)} %reshape.49.refs_4_), channel_id=1, source_target_pairs={{0,2},{1,3},{2,4},{3,5},{4,6},{5,7},{6,0},{7,1},{8,10},{9,11},{10,... | collective-permute-start | bytes 1622024 | tf_op jit(solution)/shard_map/ppermute | solution.py:1046
  22.6 12.6 %collective-permute-start.5 = (bf16[528,512]{1,0:T(8,128)(2,1)S(1)}, bf16[528,512]{1,0:T(8,128)(2,1)S(1)}, u32[]{:S(2)}, u32[]{:S(2)}) collective-permute-start(bf16[528,512]{1,0:T(8,128)(2,1)S(1)} %collective-permute-done.refs_5_), channel_id=1, source_target_pairs={{0,16},{8,24},{16,0},{24,8},{1,17},{9,25},{17,1},{25,9},{2,18},{10... | collective-permute-start | bytes 1622024 | tf_op jit(solution)/shard_map/ppermute | solution.py:1038
  23.1 12.3 %collective-permute-start.4 = (bf16[528,512]{1,0:T(8,128)(2,1)S(1)}, bf16[528,512]{1,0:T(8,128)(2,1)S(1)}, u32[]{:S(2)}, u32[]{:S(2)}) collective-permute-start(bf16[528,512]{1,0:T(8,128)(2,1)S(1)} %collective-permute-done.refs_5_), channel_id=1, source_target_pairs={{0,1},{1,0},{2,3},{3,2},{4,5},{5,4},{6,7},{7,6},{8,9},{9,8},{10,11... | collective-permute-start | bytes 1622024 | tf_op jit(solution)/shard_map/ppermute | solution.py:1034
  23.6 14.1 %collective-permute-start.3 = (bf16[528,512]{1,0:T(8,128)(2,1)S(1)}, bf16[528,512]{1,0:T(8,128)(2,1)S(1)}, u32[]{:S(2)}, u32[]{:S(2)}) collective-permute-start(bf16[528,512]{1,0:T(8,128)(2,1)S(1)} %collective-permute-done.refs_5_), channel_id=1, source_target_pairs={{0,2},{1,3},{2,4},{3,5},{4,6},{5,7},{6,0},{7,1},{8,10},{9,11},{10,... | collective-permute-start | bytes 1622024 | tf_op jit(solution)/shard_map/ppermute | solution.py:1046
  37.7 13.1 %collective-permute-start.6 = (bf16[528,512]{1,0:T(8,128)(2,1)S(1)}, bf16[528,512]{1,0:T(8,128)(2,1)S(1)}, u32[]{:S(2)}, u32[]{:S(2)}) collective-permute-start(bf16[528,512]{1,0:T(8,128)(2,1)S(1)} %collective-permute-done.3.refs_6_), channel_id=1, source_target_pairs={{0,2},{1,3},{2,4},{3,5},{4,6},{5,7},{6,0},{7,1},{8,10},{9,11},{10,... | collective-permute-start | bytes 1622024 | tf_op jit(solution)/shard_map/ppermute | solution.py:1046
  37.8 20.9 %collective-permute-start.7 = (bf16[784,512]{1,0:T(8,128)(2,1)S(1)}, bf16[784,512]{1,0:T(8,128)(2,1)S(1)}, u32[]{:S(2)}, u32[]{:S(2)}) collective-permute-start(bf16[784,512]{1,0:T(8,128)(2,1)S(1)} %pad_maximum_fusion.2), channel_id=1, source_target_pairs={{0,1},{1,0},{2,3},{3,2},{4,5},{5,4},{6,7},{7,6},{8,9},{9,8},{10,11... | collective-permute-start | bytes 2408456 | tf_op jit(solution)/shard_map/ppermute | solution.py:1034
  39.2 19.5 %collective-permute-start.9 = (bf16[800,512]{1,0:T(8,128)(2,1)S(1)}, bf16[800,512]{1,0:T(8,128)(2,1)S(1)}, u32[]{:S(2)}, u32[]{:S(2)}) collective-permute-start(bf16[800,512]{1,0:T(8,128)(2,1)S(1)} %pad_maximum_fusion), channel_id=1, source_target_pairs={{0,16},{8,24},{16,0},{24,8},{1,17},{9,25},{17,1},{25,9},{2,18},{10... | collective-permute-start | bytes 2457608 | tf_op jit(solution)/shard_map/ppermute | solution.py:1038
  50.9 21.2 %collective-permute-start.8 = (bf16[784,512]{1,0:T(8,128)(2,1)S(1)}, bf16[784,512]{1,0:T(8,128)(2,1)S(1)}, u32[]{:S(2)}, u32[]{:S(2)}) collective-permute-start(bf16[784,512]{1,0:T(8,128)(2,1)S(1)} %pad_maximum_fusion.3), channel_id=1, source_target_pairs={{0,1},{1,0},{2,3},{3,2},{4,5},{5,4},{6,7},{7,6},{8,9},{9,8},{10,11... | collective-permute-start | bytes 2408456 | tf_op jit(solution)/shard_map/ppermute | solution.py:1034
  52.0 1.9 collective-permute-start.13
  52.1 21.7 %collective-permute-start.10 = (bf16[800,512]{1,0:T(8,128)(2,1)S(1)}, bf16[800,512]{1,0:T(8,128)(2,1)}, u32[]{:S(2)}, u32[]{:S(2)}) collective-permute-start(bf16[800,512]{1,0:T(8,128)(2,1)S(1)} %pad_maximum_fusion.1), channel_id=1, source_target_pairs={{0,16},{8,24},{16,0},{24,8},{1,17},{9,25},{17,1},{25,9},{2,18},{10... | collective-permute-start | bytes 2457608 | tf_op jit(solution)/shard_map/ppermute | solution.py:1038
  53.9 20.9 %collective-permute-start.17 = (bf16[528,512]{1,0:T(8,128)(2,1)S(1)}, bf16[528,512]{1,0:T(8,128)(2,1)S(1)}, u32[]{:S(2)}, u32[]{:S(2)}) collective-permute-start(bf16[528,512]{1,0:T(8,128)(2,1)S(1)} %collective-permute-done.1.refs_8_), channel_id=1, source_target_pairs={{0,8},{8,0},{16,24},{24,16},{1,9},{9,1},{17,25},{25,17},{2,10},{10... | collective-permute-start | bytes 1622024 | tf_op jit(solution)/shard_map/ppermute | solution.py:1042
  58.7 17.8 %collective-permute-start.22 = (bf16[528,512]{1,0:T(8,128)(2,1)S(1)}, bf16[528,512]{1,0:T(8,128)(2,1)S(1)}, u32[]{:S(2)}, u32[]{:S(2)}) collective-permute-start(bf16[528,512]{1,0:T(8,128)(2,1)S(1)} %collective-permute-done.2.refs_13_), channel_id=1, source_target_pairs={{0,8},{8,0},{16,24},{24,16},{1,9},{9,1},{17,25},{25,17},{2,10},{10... | collective-permute-start | bytes 1622024 | tf_op jit(solution)/shard_map/ppermute | solution.py:1042
  58.8 18.1 %collective-permute-start.14 = (bf16[528,512]{1,0:T(8,128)(2,1)S(1)}, bf16[528,512]{1,0:T(8,128)(2,1)S(1)}, u32[]{:S(2)}, u32[]{:S(2)}) collective-permute-start(bf16[528,512]{1,0:T(8,128)(2,1)S(1)} %collective-permute-done.refs_5_), channel_id=1, source_target_pairs={{0,8},{8,0},{16,24},{24,16},{1,9},{9,1},{17,25},{25,17},{2,10},{10... | collective-permute-start | bytes 1622024 | tf_op jit(solution)/shard_map/ppermute | solution.py:1042
  72.1 5.3 %collective-permute-start.18 = (bf16[528,512]{1,0:T(8,128)(2,1)S(1)}, bf16[528,512]{1,0:T(8,128)(2,1)S(1)}, u32[]{:S(2)}, u32[]{:S(2)}) collective-permute-start(bf16[528,512]{1,0:T(8,128)(2,1)S(1)} %collective-permute-done.4.refs_9_), channel_id=1, source_target_pairs={{0,8},{8,0},{16,24},{24,16},{1,9},{9,1},{17,25},{25,17},{2,10},{10... | collective-permute-start | bytes 1622024 | tf_op jit(solution)/shard_map/ppermute | solution.py:1042
  73.8 3.7 %collective-permute-start.23 = (bf16[528,512]{1,0:T(8,128)(2,1)S(1)}, bf16[528,512]{1,0:T(8,128)(2,1)S(1)}, u32[]{:S(2)}, u32[]{:S(2)}) collective-permute-start(bf16[528,512]{1,0:T(8,128)(2,1)S(1)} %copy-done.12), channel_id=1, source_target_pairs={{0,8},{8,0},{16,24},{24,16},{1,9},{9,1},{17,25},{25,17},{2,10},{10... | collective-permute-start | bytes 1622024 | tf_op jit(solution)/shard_map/ppermute | solution.py:1042
  74.9 16.2 %collective-permute-start.12 = (bf16[544,512]{1,0:T(8,128)(2,1)S(1)}, bf16[544,512]{1,0:T(8,128)(2,1)}, u32[]{:S(2)}, u32[]{:S(2)}) collective-permute-start(bf16[544,512]{1,0:T(8,128)(2,1)S(1)} %pad_maximum_fusion.4), channel_id=1, source_target_pairs={{0,16},{8,24},{16,0},{24,8},{1,17},{9,25},{17,1},{25,9},{2,18},{10... | collective-permute-start | bytes 1671176 | tf_op jit(solution)/shard_map/ppermute | solution.py:1038
  76.5 15.0 %collective-permute-start.15 = (bf16[528,512]{1,0:T(8,128)(2,1)S(1)}, bf16[528,512]{1,0:T(8,128)(2,1)S(1)}, u32[]{:S(2)}, u32[]{:S(2)}) collective-permute-start(bf16[528,512]{1,0:T(8,128)(2,1)S(1)} %collective-permute-done.3.refs_6_), channel_id=1, source_target_pairs={{0,8},{8,0},{16,24},{24,16},{1,9},{9,1},{17,25},{25,17},{2,10},{10... | collective-permute-start | bytes 1622024 | tf_op jit(solution)/shard_map/ppermute | solution.py:1042
  76.8 14.2 %collective-permute-start.11 = (bf16[512,512]{1,0:T(8,128)(2,1)S(1)}, bf16[512,512]{1,0:T(8,128)(2,1)}, u32[]{:S(2)}, u32[]{:S(2)}) collective-permute-start(bf16[512,512]{1,0:T(8,128)(2,1)S(1)} %pad_maximum_fusion.5), channel_id=1, source_target_pairs={{0,1},{1,0},{2,3},{3,2},{4,5},{5,4},{6,7},{7,6},{8,9},{9,8},{10,11... | collective-permute-start | bytes 1572872 | tf_op jit(solution)/shard_map/ppermute | solution.py:1034
  77.4 14.8 %collective-permute-start.20 = (bf16[784,512]{1,0:T(8,128)(2,1)S(1)}, bf16[784,512]{1,0:T(8,128)(2,1)S(1)}, u32[]{:S(2)}, u32[]{:S(2)}) collective-permute-start(bf16[784,512]{1,0:T(8,128)(2,1)S(1)} %collective-permute-done.8.refs_11_), channel_id=1, source_target_pairs={{0,8},{8,0},{16,24},{24,16},{1,9},{9,1},{17,25},{25,17},{2,10},{10... | collective-permute-start | bytes 2408456 | tf_op jit(solution)/shard_map/ppermute | solution.py:1042
  77.5 14.2 %collective-permute-start.16 = (bf16[528,512]{1,0:T(8,128)(2,1)S(1)}, bf16[528,512]{1,0:T(8,128)(2,1)S(1)}, u32[]{:S(2)}, u32[]{:S(2)}) collective-permute-start(bf16[528,512]{1,0:T(8,128)(2,1)S(1)} %collective-permute-done.6.refs_7_), channel_id=1, source_target_pairs={{0,8},{8,0},{16,24},{24,16},{1,9},{9,1},{17,25},{25,17},{2,10},{10... | collective-permute-start | bytes 1622024 | tf_op jit(solution)/shard_map/ppermute | solution.py:1042
  91.1 6.3 %collective-permute-start.25 = (bf16[800,512]{1,0:T(8,128)(2,1)}, bf16[800,512]{1,0:T(8,128)(2,1)S(1)}, u32[]{:S(2)}, u32[]{:S(2)}) collective-permute-start(bf16[800,512]{1,0:T(8,128)(2,1)} %collective-permute-done.10.refs_16_), channel_id=1, source_target_pairs={{0,8},{8,0},{16,24},{24,16},{1,9},{9,1},{17,25},{25,17},{2,10},{10... | collective-permute-start | bytes 2457608 | tf_op jit(solution)/shard_map/ppermute | solution.py:1042
  91.1 6.3 %collective-permute-start.24 = (bf16[800,512]{1,0:T(8,128)(2,1)S(1)}, bf16[800,512]{1,0:T(8,128)(2,1)}, u32[]{:S(2)}, u32[]{:S(2)}) collective-permute-start(bf16[800,512]{1,0:T(8,128)(2,1)S(1)} %collective-permute-done.9.refs_15_), channel_id=1, source_target_pairs={{0,8},{8,0},{16,24},{24,16},{1,9},{9,1},{17,25},{25,17},{2,10},{10... | collective-permute-start | bytes 2457608 | tf_op jit(solution)/shard_map/ppermute | solution.py:1042
  91.6 5.8 %collective-permute-start.19 = (bf16[784,512]{1,0:T(8,128)(2,1)S(1)}, bf16[784,512]{1,0:T(8,128)(2,1)}, u32[]{:S(2)}, u32[]{:S(2)}) collective-permute-start(bf16[784,512]{1,0:T(8,128)(2,1)S(1)} %collective-permute-done.7.refs_10_), channel_id=1, source_target_pairs={{0,8},{8,0},{16,24},{24,16},{1,9},{9,1},{17,25},{25,17},{2,10},{10... | collective-permute-start | bytes 2408456 | tf_op jit(solution)/shard_map/ppermute | solution.py:1042
  91.7 5.7 %collective-permute-start.26 = (bf16[544,512]{1,0:T(8,128)(2,1)}, bf16[544,512]{1,0:T(8,128)(2,1)}, u32[]{:S(2)}, u32[]{:S(2)}) collective-permute-start(bf16[544,512]{1,0:T(8,128)(2,1)} %collective-permute-done.12.refs_17_), channel_id=1, source_target_pairs={{0,8},{8,0},{16,24},{24,16},{1,9},{9,1},{17,25},{25,17},{2,10},{10... | collective-permute-start | bytes 1671176 | tf_op jit(solution)/shard_map/ppermute | solution.py:1042
  93.5 3.9 %collective-permute-start.21 = (bf16[512,512]{1,0:T(8,128)(2,1)}, bf16[512,512]{1,0:T(8,128)(2,1)S(1)}, u32[]{:S(2)}, u32[]{:S(2)}) collective-permute-start(bf16[512,512]{1,0:T(8,128)(2,1)} %collective-permute-done.11.refs_12_), channel_id=1, source_target_pairs={{0,8},{8,0},{16,24},{24,16},{1,9},{9,1},{17,25},{25,17},{2,10},{10... | collective-permute-start | bytes 1572872 | tf_op jit(solution)/shard_map/ppermute | solution.py:1042
  140.9 15.5 %collective-permute-start.28 = (bf16[4,528,512]{2,1,0:T(8,128)(2,1)}, bf16[4,528,512]{2,1,0:T(8,128)(2,1)S(1)}, u32[]{:S(2)}, u32[]{:S(2)}) collective-permute-start(bf16[4,528,512]{2,1,0:T(8,128)(2,1)} %get-tuple-element.156), channel_id=1, source_target_pairs={{0,8},{8,0},{16,24},{24,16},{1,9},{9,1},{17,25},{25,17},{2,10},{10... | collective-permute-start | bytes 6488072 | tf_op jit(solution)/shard_map/ppermute | solution.py:1042
  155.9 6.1 %collective-permute-start.27 = (bf16[4,528,512]{2,1,0:T(8,128)(2,1)}, bf16[4,528,512]{2,1,0:T(8,128)(2,1)}, u32[]{:S(2)}, u32[]{:S(2)}) collective-permute-start(bf16[4,528,512]{2,1,0:T(8,128)(2,1)} %get-tuple-element.154), channel_id=1, source_target_pairs={{0,8},{8,0},{16,24},{24,16},{1,9},{9,1},{17,25},{25,17},{2,10},{10... | collective-permute-start | bytes 6488072 | tf_op jit(solution)/shard_map/ppermute | solution.py:1042
  156.3 20.2 %collective-permute-start.31 = (bf16[4,528,512]{2,1,0:T(8,128)(2,1)}, bf16[4,528,512]{2,1,0:T(8,128)(2,1)S(1)}, u32[]{:S(2)}, u32[]{:S(2)}) collective-permute-start(bf16[4,528,512]{2,1,0:T(8,128)(2,1)} %get-tuple-element.169), channel_id=1, source_target_pairs={{0,8},{8,0},{16,24},{24,16},{1,9},{9,1},{17,25},{25,17},{2,10},{10... | collective-permute-start | bytes 6488072 | tf_op jit(solution)/shard_map/ppermute | solution.py:1042
  166.1 10.4 %collective-permute-start.30 = (bf16[4,528,512]{2,1,0:T(8,128)(2,1)}, bf16[4,528,512]{2,1,0:T(8,128)(2,1)}, u32[]{:S(2)}, u32[]{:S(2)}) collective-permute-start(bf16[4,528,512]{2,1,0:T(8,128)(2,1)} %get-tuple-element.168), channel_id=1, source_target_pairs={{0,8},{8,0},{16,24},{24,16},{1,9},{9,1},{17,25},{25,17},{2,10},{10... | collective-permute-start | bytes 6488072 | tf_op jit(solution)/shard_map/ppermute | solution.py:1042
  166.5 28.2 %collective-permute-start.29 = (bf16[2,528,512]{2,1,0:T(8,128)(2,1)}, bf16[2,528,512]{2,1,0:T(8,128)(2,1)}, u32[]{:S(2)}, u32[]{:S(2)}) collective-permute-start(bf16[2,528,512]{2,1,0:T(8,128)(2,1)} %get-tuple-element.157), channel_id=1, source_target_pairs={{0,16},{8,24},{16,0},{24,8},{1,17},{9,25},{17,1},{25,9},{2,18},{10... | collective-permute-start | bytes 3244040 | tf_op jit(solution)/shard_map/ppermute | solution.py:1038
  170.3 31.0 %collective-permute-start.40 = (bf16[2,528,512]{2,1,0:T(8,128)(2,1)}, bf16[2,528,512]{2,1,0:T(8,128)(2,1)S(1)}, u32[]{:S(2)}, u32[]{:S(2)}) collective-permute-start(bf16[2,528,512]{2,1,0:T(8,128)(2,1)} %get-tuple-element.167), channel_id=1, source_target_pairs={{0,1},{1,0},{2,3},{3,2},{4,5},{5,4},{6,7},{7,6},{8,9},{9,8},{10,11... | collective-permute-start | bytes 3244040 | tf_op jit(solution)/shard_map/ppermute | solution.py:1034
  172.4 4.1 %collective-permute-start.33 = (f32[16,512]{1,0:T(8,128)S(1)}, f32[16,512]{1,0:T(8,128)S(1)}, u32[]{:S(2)}, u32[]{:S(2)}) collective-permute-start(f32[16,512]{1,0:T(8,128)S(1)} %add.199), channel_id=1, source_target_pairs={{0,2},{1,3},{2,0},{3,1},{4,6},{5,7},{6,4},{7,5},{8,10},{9,11},{10,... | collective-permute-start | bytes 98312 | tf_op jit(solution)/shard_map/ppermute | solution.py:1050
  186.3 6.0 %collective-permute-start.34 = (f32[16,512]{1,0:T(8,128)S(1)}, f32[16,512]{1,0:T(8,128)S(1)}, u32[]{:S(2)}, u32[]{:S(2)}) collective-permute-start(f32[16,512]{1,0:T(8,128)S(1)} %add.200), channel_id=1, source_target_pairs={{0,4},{1,5},{2,6},{3,7},{4,0},{5,1},{6,2},{7,3},{8,12},{9,13},{10,... | collective-permute-start | bytes 98312 | tf_op jit(solution)/shard_map/ppermute | solution.py:1050
  194.7 20.6 %collective-permute-start.58 = (f32[16,512]{1,0:T(8,128)S(1)}, f32[16,512]{1,0:T(8,128)S(1)}, u32[]{:S(2)}, u32[]{:S(2)}) collective-permute-start(f32[16,512]{1,0:T(8,128)S(1)} %add.201), channel_id=1, source_target_pairs={{0,1},{1,0},{2,3},{3,2},{4,5},{5,4},{6,7},{7,6},{8,9},{9,8},{10,11... | collective-permute-start | bytes 98312 | tf_op jit(solution)/shard_map/ppermute | solution.py:1034
  195.7 9.5 %collective-permute-start.36 = (bf16[256,512]{1,0:T(8,128)(2,1)}, bf16[256,512]{1,0:T(8,128)(2,1)S(1)}, u32[]{:S(2)}, u32[]{:S(2)}) collective-permute-start(bf16[256,512]{1,0:T(8,128)(2,1)} %get-tuple-element.195), channel_id=1, source_target_pairs={{0,16},{8,24},{16,0},{24,8},{1,17},{9,25},{17,1},{25,9},{2,18},{10... | collective-permute-start | bytes 786440 | tf_op jit(solution)/shard_map/ppermute | solution.py:1038
  197.4 13.8 %collective-permute-start.48 = (bf16[272,512]{1,0:T(8,128)(2,1)}, bf16[272,512]{1,0:T(8,128)(2,1)S(1)}, u32[]{:S(2)}, u32[]{:S(2)}) collective-permute-start(bf16[272,512]{1,0:T(8,128)(2,1)} %get-tuple-element.213), channel_id=1, source_target_pairs={{0,16},{8,24},{16,0},{24,8},{1,17},{9,25},{17,1},{25,9},{2,18},{10... | collective-permute-start | bytes 835592 | tf_op jit(solution)/shard_map/ppermute | solution.py:1038
  198.9 9.3 %collective-permute-start.35 = (bf16[256,512]{1,0:T(8,128)(2,1)S(1)}, bf16[256,512]{1,0:T(8,128)(2,1)S(1)}, u32[]{:S(2)}, u32[]{:S(2)}) collective-permute-start(bf16[256,512]{1,0:T(8,128)(2,1)S(1)} %get-tuple-element.238), channel_id=1, source_target_pairs={{0,1},{1,0},{2,3},{3,2},{4,5},{5,4},{6,7},{7,6},{8,9},{9,8},{10,11... | collective-permute-start | bytes 786440 | tf_op jit(solution)/shard_map/ppermute | solution.py:1034
  201.3 12.9 %collective-permute-start.47 = (bf16[272,512]{1,0:T(8,128)(2,1)S(1)}, bf16[272,512]{1,0:T(8,128)(2,1)S(1)}, u32[]{:S(2)}, u32[]{:S(2)}) collective-permute-start(bf16[272,512]{1,0:T(8,128)(2,1)S(1)} %get-tuple-element.242), channel_id=1, source_target_pairs={{0,1},{1,0},{2,3},{3,2},{4,5},{5,4},{6,7},{7,6},{8,9},{9,8},{10,11... | collective-permute-start | bytes 835592 | tf_op jit(solution)/shard_map/ppermute | solution.py:1034
  208.2 11.6 %collective-permute-start.37 = (bf16[256,512]{1,0:T(8,128)(2,1)S(1)}, bf16[256,512]{1,0:T(8,128)(2,1)S(1)}, u32[]{:S(2)}, u32[]{:S(2)}) collective-permute-start(bf16[256,512]{1,0:T(8,128)(2,1)S(1)} %get-tuple-element.196), channel_id=1, source_target_pairs={{0,1},{1,0},{2,3},{3,2},{4,5},{5,4},{6,7},{7,6},{8,9},{9,8},{10,11... | collective-permute-start | bytes 786440 | tf_op jit(solution)/shard_map/ppermute | solution.py:1034
  209.3 11.4 %collective-permute-start.38 = (bf16[256,512]{1,0:T(8,128)(2,1)S(1)}, bf16[256,512]{1,0:T(8,128)(2,1)S(1)}, u32[]{:S(2)}, u32[]{:S(2)}) collective-permute-start(bf16[256,512]{1,0:T(8,128)(2,1)S(1)} %copy-done.47), channel_id=1, source_target_pairs={{0,16},{8,24},{16,0},{24,8},{1,17},{9,25},{17,1},{25,9},{2,18},{10... | collective-permute-start | bytes 786440 | tf_op jit(solution)/shard_map/ppermute | solution.py:1038
  211.2 11.4 %collective-permute-start.44 = (bf16[256,512]{1,0:T(8,128)(2,1)S(1)}, bf16[256,512]{1,0:T(8,128)(2,1)S(1)}, u32[]{:S(2)}, u32[]{:S(2)}) collective-permute-start(bf16[256,512]{1,0:T(8,128)(2,1)S(1)} %add_convert_fusion.5), channel_id=1, source_target_pairs={{0,2},{1,3},{2,4},{3,5},{4,6},{5,7},{6,0},{7,1},{8,10},{9,11},{10,... | collective-permute-start | bytes 786440 | tf_op jit(solution)/shard_map/ppermute | solution.py:1046
  214.2 11.6 %collective-permute-start.49 = (bf16[272,512]{1,0:T(8,128)(2,1)S(1)}, bf16[272,512]{1,0:T(8,128)(2,1)S(1)}, u32[]{:S(2)}, u32[]{:S(2)}) collective-permute-start(bf16[272,512]{1,0:T(8,128)(2,1)S(1)} %get-tuple-element.214), channel_id=1, source_target_pairs={{0,1},{1,0},{2,3},{3,2},{4,5},{5,4},{6,7},{7,6},{8,9},{9,8},{10,11... | collective-permute-start | bytes 835592 | tf_op jit(solution)/shard_map/ppermute | solution.py:1034
  215.4 10.3 %collective-permute-start.50 = (bf16[272,512]{1,0:T(8,128)(2,1)S(1)}, bf16[272,512]{1,0:T(8,128)(2,1)S(1)}, u32[]{:S(2)}, u32[]{:S(2)}) collective-permute-start(bf16[272,512]{1,0:T(8,128)(2,1)S(1)} %copy-done.45), channel_id=1, source_target_pairs={{0,16},{8,24},{16,0},{24,8},{1,17},{9,25},{17,1},{25,9},{2,18},{10... | collective-permute-start | bytes 835592 | tf_op jit(solution)/shard_map/ppermute | solution.py:1038
  219.8 10.7 %collective-permute-start.55 = (bf16[272,512]{1,0:T(8,128)(2,1)S(1)}, bf16[272,512]{1,0:T(8,128)(2,1)S(1)}, u32[]{:S(2)}, u32[]{:S(2)}) collective-permute-start(bf16[272,512]{1,0:T(8,128)(2,1)S(1)} %add_convert_fusion.2), channel_id=1, source_target_pairs={{0,2},{1,3},{2,4},{3,5},{4,6},{5,7},{6,0},{7,1},{8,10},{9,11},{10,... | collective-permute-start | bytes 835592 | tf_op jit(solution)/shard_map/ppermute | solution.py:1046
  220.7 11.1 %collective-permute-start.59 = (f32[16,512]{1,0:T(8,128)S(1)}, f32[16,512]{1,0:T(8,128)S(1)}, u32[]{:S(2)}, u32[]{:S(2)}) collective-permute-start(f32[16,512]{1,0:T(8,128)S(1)} %add.232), channel_id=1, source_target_pairs={{0,16},{8,24},{16,0},{24,8},{1,17},{9,25},{17,1},{25,9},{2,18},{10... | collective-permute-start | bytes 98312 | tf_op jit(solution)/shard_map/ppermute | solution.py:1038
  222.6 9.3 %collective-permute-start.39 = (bf16[256,512]{1,0:T(8,128)(2,1)S(1)}, bf16[256,512]{1,0:T(8,128)(2,1)S(1)}, u32[]{:S(2)}, u32[]{:S(2)}) collective-permute-start(bf16[256,512]{1,0:T(8,128)(2,1)S(1)} %copy-done.46), channel_id=1, source_target_pairs={{0,1},{1,0},{2,3},{3,2},{4,5},{5,4},{6,7},{7,6},{8,9},{9,8},{10,11... | collective-permute-start | bytes 786440 | tf_op jit(solution)/shard_map/ppermute | solution.py:1034
  225.7 11.0 %collective-permute-start.45 = (bf16[256,512]{1,0:T(8,128)(2,1)S(1)}, bf16[256,512]{1,0:T(8,128)(2,1)S(1)}, u32[]{:S(2)}, u32[]{:S(2)}) collective-permute-start(bf16[256,512]{1,0:T(8,128)(2,1)S(1)} %add_convert_fusion.4), channel_id=1, source_target_pairs={{0,2},{1,3},{2,4},{3,5},{4,6},{5,7},{6,0},{7,1},{8,10},{9,11},{10,... | collective-permute-start | bytes 786440 | tf_op jit(solution)/shard_map/ppermute | solution.py:1046
  225.8 9.9 %collective-permute-start.41 = (bf16[256,512]{1,0:T(8,128)(2,1)}, bf16[256,512]{1,0:T(8,128)(2,1)S(1)}, u32[]{:S(2)}, u32[]{:S(2)}) collective-permute-start(bf16[256,512]{1,0:T(8,128)(2,1)} %get-tuple-element.201), channel_id=1, source_target_pairs={{0,16},{8,24},{16,0},{24,8},{1,17},{9,25},{17,1},{25,9},{2,18},{10... | collective-permute-start | bytes 786440 | tf_op jit(solution)/shard_map/ppermute | solution.py:1038
  230.5 8.2 %collective-permute-start.51 = (bf16[272,512]{1,0:T(8,128)(2,1)}, bf16[272,512]{1,0:T(8,128)(2,1)S(1)}, u32[]{:S(2)}, u32[]{:S(2)}) collective-permute-start(bf16[272,512]{1,0:T(8,128)(2,1)} %get-tuple-element.217), channel_id=1, source_target_pairs={{0,1},{1,0},{2,3},{3,2},{4,5},{5,4},{6,7},{7,6},{8,9},{9,8},{10,11... | collective-permute-start | bytes 835592 | tf_op jit(solution)/shard_map/ppermute | solution.py:1034
  231.8 11.0 %collective-permute-start.56 = (bf16[272,512]{1,0:T(8,128)(2,1)S(1)}, bf16[272,512]{1,0:T(8,128)(2,1)S(1)}, u32[]{:S(2)}, u32[]{:S(2)}) collective-permute-start(bf16[272,512]{1,0:T(8,128)(2,1)S(1)} %add_convert_fusion.1), channel_id=1, source_target_pairs={{0,2},{1,3},{2,4},{3,5},{4,6},{5,7},{6,0},{7,1},{8,10},{9,11},{10,... | collective-permute-start | bytes 835592 | tf_op jit(solution)/shard_map/ppermute | solution.py:1046
  231.9 10.0 %collective-permute-start.52 = (bf16[272,512]{1,0:T(8,128)(2,1)S(1)}, bf16[272,512]{1,0:T(8,128)(2,1)S(1)}, u32[]{:S(2)}, u32[]{:S(2)}) collective-permute-start(bf16[272,512]{1,0:T(8,128)(2,1)S(1)} %get-tuple-element.219), channel_id=1, source_target_pairs={{0,16},{8,24},{16,0},{24,8},{1,17},{9,25},{17,1},{25,9},{2,18},{10... | collective-permute-start | bytes 835592 | tf_op jit(solution)/shard_map/ppermute | solution.py:1038
  235.6 9.9 %collective-permute-start.42 = (bf16[256,512]{1,0:T(8,128)(2,1)}, bf16[256,512]{1,0:T(8,128)(2,1)S(1)}, u32[]{:S(2)}, u32[]{:S(2)}) collective-permute-start(bf16[256,512]{1,0:T(8,128)(2,1)} %get-tuple-element.202), channel_id=1, source_target_pairs={{0,1},{1,0},{2,3},{3,2},{4,5},{5,4},{6,7},{7,6},{8,9},{9,8},{10,11... | collective-permute-start | bytes 786440 | tf_op jit(solution)/shard_map/ppermute | solution.py:1034
  236.7 9.8 %collective-permute-start.43 = (bf16[256,512]{1,0:T(8,128)(2,1)}, bf16[256,512]{1,0:T(8,128)(2,1)S(1)}, u32[]{:S(2)}, u32[]{:S(2)}) collective-permute-start(bf16[256,512]{1,0:T(8,128)(2,1)} %get-tuple-element.204), channel_id=1, source_target_pairs={{0,16},{8,24},{16,0},{24,8},{1,17},{9,25},{17,1},{25,9},{2,18},{10... | collective-permute-start | bytes 786440 | tf_op jit(solution)/shard_map/ppermute | solution.py:1038
  238.7 9.9 %collective-permute-start.46 = (bf16[256,512]{1,0:T(8,128)(2,1)S(1)}, bf16[256,512]{1,0:T(8,128)(2,1)S(1)}, u32[]{:S(2)}, u32[]{:S(2)}) collective-permute-start(bf16[256,512]{1,0:T(8,128)(2,1)S(1)} %add_convert_fusion.3), channel_id=1, source_target_pairs={{0,2},{1,3},{2,4},{3,5},{4,6},{5,7},{6,0},{7,1},{8,10},{9,11},{10,... | collective-permute-start | bytes 786440 | tf_op jit(solution)/shard_map/ppermute | solution.py:1046
  241.9 6.9 %collective-permute-start.53 = (bf16[272,512]{1,0:T(8,128)(2,1)}, bf16[272,512]{1,0:T(8,128)(2,1)S(1)}, u32[]{:S(2)}, u32[]{:S(2)}) collective-permute-start(bf16[272,512]{1,0:T(8,128)(2,1)} %get-tuple-element.220), channel_id=1, source_target_pairs={{0,1},{1,0},{2,3},{3,2},{4,5},{5,4},{6,7},{7,6},{8,9},{9,8},{10,11... | collective-permute-start | bytes 835592 | tf_op jit(solution)/shard_map/ppermute | solution.py:1034
  242.8 7.1 %collective-permute-start.54 = (bf16[272,512]{1,0:T(8,128)(2,1)S(1)}, bf16[272,512]{1,0:T(8,128)(2,1)S(1)}, u32[]{:S(2)}, u32[]{:S(2)}) collective-permute-start(bf16[272,512]{1,0:T(8,128)(2,1)S(1)} %get-tuple-element.222), channel_id=1, source_target_pairs={{0,16},{8,24},{16,0},{24,8},{1,17},{9,25},{17,1},{25,9},{2,18},{10... | collective-permute-start | bytes 835592 | tf_op jit(solution)/shard_map/ppermute | solution.py:1038
  245.5 8.4 %collective-permute-start.57 = (bf16[272,512]{1,0:T(8,128)(2,1)S(1)}, bf16[272,512]{1,0:T(8,128)(2,1)S(1)}, u32[]{:S(2)}, u32[]{:S(2)}) collective-permute-start(bf16[272,512]{1,0:T(8,128)(2,1)S(1)} %add_convert_fusion), channel_id=1, source_target_pairs={{0,2},{1,3},{2,4},{3,5},{4,6},{5,7},{6,0},{7,1},{8,10},{9,11},{10,... | collective-permute-start | bytes 835592 | tf_op jit(solution)/shard_map/ppermute | solution.py:1046
  261.0 1.4 collective-permute-start.60
  263.1 3.6 %collective-permute-start.61 = (f32[8,128]{1,0:T(8,128)S(1)}, f32[8,128]{1,0:T(8,128)S(1)}, u32[]{:S(2)}, u32[]{:S(2)}) collective-permute-start(f32[8,128]{1,0:T(8,128)S(1)} %add.237), channel_id=1, source_target_pairs={{0,1},{1,0},{2,3},{3,2},{4,5},{5,4},{6,7},{7,6},{8,9},{9,8},{10,11... | collective-permute-start | bytes 12296 | tf_op jit(solution)/shard_map/ppermute | solution.py:1034
  266.7 3.6 %collective-permute-start.62 = (f32[8,128]{1,0:T(8,128)S(1)}, f32[8,128]{1,0:T(8,128)S(1)}, u32[]{:S(2)}, u32[]{:S(2)}) collective-permute-start(f32[8,128]{1,0:T(8,128)S(1)} %add.238), channel_id=1, source_target_pairs={{0,16},{8,24},{16,0},{24,8},{1,17},{9,25},{17,1},{25,9},{2,18},{10... | collective-permute-start | bytes 12296 | tf_op jit(solution)/shard_map/ppermute | solution.py:1038
  270.3 3.6 %collective-permute-start.63 = (f32[8,128]{1,0:T(8,128)S(1)}, f32[8,128]{1,0:T(8,128)S(1)}, u32[]{:S(2)}, u32[]{:S(2)}) collective-permute-start(f32[8,128]{1,0:T(8,128)S(1)} %add.239), channel_id=1, source_target_pairs={{0,2},{1,3},{2,0},{3,1},{4,6},{5,7},{6,4},{7,5},{8,10},{9,11},{10,... | collective-permute-start | bytes 12296 | tf_op jit(solution)/shard_map/ppermute | solution.py:1050
  273.9 4.5 %collective-permute-start.64 = (f32[8,128]{1,0:T(8,128)S(1)}, f32[8,128]{1,0:T(8,128)S(1)}, u32[]{:S(2)}, u32[]{:S(2)}) collective-permute-start(f32[8,128]{1,0:T(8,128)S(1)} %add.240), channel_id=1, source_target_pairs={{0,4},{1,5},{2,6},{3,7},{4,0},{5,1},{6,2},{7,3},{8,12},{9,13},{10,... | collective-permute-start | bytes 12296 | tf_op jit(solution)/shard_map/ppermute | solution.py:1050
  (51 other events, 805.6 us)
